TPU v7x, 32 devices: a whole 2x2x4 slice. The times are simulated.
32 devices in a mesh: dp: 2 (over core), wa: 16 (over z, y, x).
Axes of the slice: x: 2, y: 2, z: 4, core: 2. Of those that a mesh axis runs over, the one named last changes fastest.
Arguments:
- slow_in: bfloat16 [32, 8, 16, 16, 1024], P('dp', None, None, None, 'wa'), may hold values from -9 to 9
- fast_in: bfloat16 [32, 32, 16, 16, 128], P('dp', 'wa'), may hold values from -13 to 13
- clip_side: int32 [32], P('dp'), may hold values from 10 to 16, as said below
- fast_reduce: bfloat16 [3, 128, 32], replicated, may hold values from -0.3125 to 0.3125
- fast_spatial: bfloat16 [3, 3, 32, 32], replicated, may hold values from -0.375 to 0.375
- fast_expand: bfloat16 [32, 128], replicated, may hold values from -1 to 1
- lateral_weight: bfloat16 [5, 128, 256], replicated, may hold values from -0.25 to 0.25
- slow_reduce: bfloat16 [3, 1280, 256], replicated, may hold values from -0.09375 to 0.09375
- slow_spatial: bfloat16 [3, 3, 256, 256], replicated, may hold values from -0.125 to 0.125
- slow_expand: bfloat16 [256, 1024], replicated, may hold values from -0.375 to 0.375
- slow_project: bfloat16 [1280, 1024], replicated, may hold values from -0.15625 to 0.15625
- fast_reduce_norm: float32 [2, 32], replicated, may hold values from 0.25 to 1.75
- fast_spatial_norm: float32 [2, 32], replicated, may hold values from 0.25 to 1.75
- fast_expand_norm: float32 [2, 128], replicated, may hold values from 0.25 to 1.75
- lateral_norm: float32 [2, 256], replicated, may hold values from 0.25 to 1.75
- slow_reduce_norm: float32 [2, 256], replicated, may hold values from 0.25 to 1.75
- slow_spatial_norm: float32 [2, 256], replicated, may hold values from 0.25 to 1.75
- slow_expand_norm: float32 [2, 1024], replicated, may hold values from 0.25 to 1.75
- slow_project_norm: float32 [2, 1024], replicated, may hold values from 0.25 to 1.75
- slow_cot: bfloat16 [32, 8, 16, 16, 1024], P('dp', None, None, None, 'wa'), may hold values from -6 to 6
- fast_cot: bfloat16 [32, 32, 16, 16, 128], P('dp', 'wa'), may hold values from -6 to 6
Outputs:
- slow_result: bfloat16 [32, 8, 16, 16, 1024], P('dp', None, None, None, 'wa')
- fast_result: bfloat16 [32, 32, 16, 16, 128], P('dp', 'wa')
- slow_grad: bfloat16 [32, 8, 16, 16, 1024], P('dp', None, None, None, 'wa')
- fast_grad: bfloat16 [32, 32, 16, 16, 128], P('dp', 'wa')
- fast_reduce_grad: float32 [3, 128, 32], replicated
- fast_spatial_grad: float32 [3, 3, 32, 32], replicated
- fast_expand_grad: float32 [32, 128], replicated
- lateral_weight_grad: float32 [5, 128, 256], replicated
- slow_reduce_grad: float32 [3, 1280, 256], replicated
- slow_spatial_grad: float32 [3, 3, 256, 256], replicated
- slow_expand_grad: float32 [256, 1024], replicated
- slow_project_grad: float32 [1280, 1024], replicated
- fast_reduce_norm_grad: float32 [2, 32], replicated
- fast_spatial_norm_grad: float32 [2, 32], replicated
- fast_expand_norm_grad: float32 [2, 128], replicated
- lateral_norm_grad: float32 [2, 256], replicated
- slow_reduce_norm_grad: float32 [2, 256], replicated
- slow_spatial_norm_grad: float32 [2, 256], replicated
- slow_expand_norm_grad: float32 [2, 1024], replicated
- slow_project_norm_grad: float32 [2, 1024], replicated
Inputs may be any that keep to these rules, and one draw needn't show every extreme that they name: `clip_side`: each clip's side is one of 10, 14 and 16.
All inputs are finite; a program needn't handle non-finite values.
Results may differ from a plain program's by a relative error of at most 0.018.
Values may be sent and summed in bfloat16 or wider, within the bound.
No kernel may reach another device: no remote copies, remote signals or barrier semaphores. Data moves between devices by JAX's collectives and lax.ppermute only.
A program may use at most 320 MiB of HBM per device.

v0:
```python
import jax
import jax.numpy as jnp
from jax import lax
from jax.sharding import PartitionSpec as P

EPSILON = 1e-05


def with_halo(block, sides, width):
    for axis, dim in sides:
        count = lax.axis_size(axis)
        forward = [(i, i + 1) for i in range(count - 1)]
        backward = [(target, source) for source, target in forward]
        low = lax.ppermute(
            lax.slice_in_dim(block, block.shape[dim] - width, None, axis=dim), axis, forward
        )
        high = lax.ppermute(lax.slice_in_dim(block, 0, width, axis=dim), axis, backward)
        block = jnp.concatenate([low, block, high], axis=dim)
    return block


def silu_slope(values):
    logistic = jax.nn.sigmoid(values)
    return logistic * (1.0 + values * (1.0 - logistic))


def valid_cells(side_list, grid_side):
    row_ids = lax.broadcasted_iota(jnp.int32, (grid_side, grid_side), 0)
    col_ids = lax.broadcasted_iota(jnp.int32, (grid_side, grid_side), 1)
    bounds = side_list[:, None, None]
    inside = (row_ids[None] < bounds) & (col_ids[None] < bounds)
    return inside.astype(jnp.float32)[:, None, :, :, None]


def time_apply(padded, weight, length, stride):
    summed = None
    for offset in range(weight.shape[0]):
        window = lax.slice_in_dim(padded, offset, offset + stride * (length - 1) + 1, stride, 1)
        tap_term = jnp.einsum(
            "nthwi,io->nthwo", window, weight[offset], preferred_element_type=jnp.float32
        )
        summed = tap_term if summed is None else summed + tap_term
    return summed


def time_weight_grad(padded, grad_low, tap_count, length, stride):
    return jnp.stack(
        [
            jnp.einsum(
                "nthwi,nthwo->io",
                lax.slice_in_dim(padded, offset, offset + stride * (length - 1) + 1, stride, 1),
                grad_low,
                preferred_element_type=jnp.float32,
            )
            for offset in range(tap_count)
        ]
    )


def time_back(grad_padded, weight, length):
    tap_count = weight.shape[0]
    summed = None
    for offset in range(tap_count):
        begin = tap_count - 1 - offset
        window = lax.slice_in_dim(grad_padded, begin, begin + length, 1, 1)
        tap_term = jnp.einsum(
            "nthwo,io->nthwi", window, weight[offset], preferred_element_type=jnp.float32
        )
        summed = tap_term if summed is None else summed + tap_term
    return summed


def plane_apply(values, weight):
    grid_rows, grid_cols = (values.shape[2], values.shape[3])
    padded = jnp.pad(values, ((0, 0), (0, 0), (1, 1), (1, 1), (0, 0)))
    summed = None
    for row_tap in range(3):
        for col_tap in range(3):
            window = padded[:, :, row_tap : row_tap + grid_rows, col_tap : col_tap + grid_cols]
            tap_term = jnp.einsum(
                "nthwi,io->nthwo",
                window,
                weight[row_tap, col_tap],
                preferred_element_type=jnp.float32,
            )
            summed = tap_term if summed is None else summed + tap_term
    return summed


def plane_weight_grad(values, grad_low):
    grid_rows, grid_cols = (values.shape[2], values.shape[3])
    padded = jnp.pad(values, ((0, 0), (0, 0), (1, 1), (1, 1), (0, 0)))
    row_list = []
    for row_tap in range(3):
        col_list = []
        for col_tap in range(3):
            window = padded[:, :, row_tap : row_tap + grid_rows, col_tap : col_tap + grid_cols]
            col_list.append(
                jnp.einsum("nthwi,nthwo->io", window, grad_low, preferred_element_type=jnp.float32)
            )
        row_list.append(jnp.stack(col_list))
    return jnp.stack(row_list)


def plane_back(grad_low, weight):
    grid_rows, grid_cols = (grad_low.shape[2], grad_low.shape[3])
    padded = jnp.pad(grad_low, ((0, 0), (0, 0), (1, 1), (1, 1), (0, 0)))
    summed = None
    for row_tap in range(3):
        for col_tap in range(3):
            window = padded[
                :, :, 2 - row_tap : 2 - row_tap + grid_rows, 2 - col_tap : 2 - col_tap + grid_cols
            ]
            tap_term = jnp.einsum(
                "nthwo,io->nthwi",
                window,
                weight[row_tap, col_tap],
                preferred_element_type=jnp.float32,
            )
            summed = tap_term if summed is None else summed + tap_term
    return summed


def norm_forward(pre_list, valid, param_list, count_term):
    moments = jnp.stack(
        [
            jnp.stack(
                [
                    jnp.sum(pre_value * valid, axis=(0, 1, 2, 3)),
                    jnp.sum(pre_value * pre_value * valid, axis=(0, 1, 2, 3)),
                ]
            )
            for pre_value in pre_list
        ]
    )
    totals, count_all = lax.psum((moments, count_term), ("dp", "wa"))
    outputs = []
    for position in range(len(pre_list)):
        mean_value = totals[position, 0] / count_all
        variance = totals[position, 1] / count_all - mean_value * mean_value
        inv_std = lax.rsqrt(variance + EPSILON)
        centered = (pre_list[position] - mean_value) * inv_std
        outputs.append(
            (param_list[position][0] * centered + param_list[position][1], centered, inv_std)
        )
    return (outputs, count_all)


def norm_backward(grad_list, centered_list, inv_list, param_list, valid, count_all):
    stacked = jnp.stack(
        [
            jnp.stack(
                [
                    jnp.sum(grad_value * centered, axis=(0, 1, 2, 3)),
                    jnp.sum(grad_value, axis=(0, 1, 2, 3)),
                ]
            )
            for grad_value, centered in zip(grad_list, centered_list)
        ]
    )
    totals = lax.psum(stacked, ("dp", "wa"))
    inputs = []
    for position in range(len(grad_list)):
        inner = (
            grad_list[position]
            - (totals[position, 1] + centered_list[position] * totals[position, 0]) / count_all
        )
        inputs.append(valid * param_list[position][0] * inv_list[position] * inner)
    return (inputs, [totals[position] for position in range(len(grad_list))])


def per_device(
    slow_in,
    fast_in,
    clip_side,
    fast_reduce,
    fast_spatial,
    fast_expand,
    lateral_weight,
    slow_reduce,
    slow_spatial,
    slow_expand,
    slow_project,
    fast_reduce_norm,
    fast_spatial_norm,
    fast_expand_norm,
    lateral_norm,
    slow_reduce_norm,
    slow_spatial_norm,
    slow_expand_norm,
    slow_project_norm,
    slow_cot,
    fast_cot,
):
    wa_count = lax.axis_size("wa")
    wa_place = lax.axis_index("wa")
    clips_dev = fast_in.shape[0]
    frames_dev = fast_in.shape[1]
    grid_side = fast_in.shape[2]
    slow_frames = slow_in.shape[1]
    own_clips = clips_dev // wa_count
    tap_count = lateral_weight.shape[0]
    stride = frames_dev * wa_count // slow_frames
    fast_valid = valid_cells(clip_side, grid_side)
    own_sides = lax.dynamic_slice_in_dim(clip_side, wa_place * own_clips, own_clips)
    own_valid = valid_cells(own_sides, grid_side)
    fast_area = jnp.sum(clip_side * clip_side).astype(jnp.float32) * frames_dev
    own_area = jnp.sum(own_sides * own_sides).astype(jnp.float32) * slow_frames
    fast_padded = with_halo(fast_in, (("wa", 1),), 1)
    reduce_pre = time_apply(fast_padded, fast_reduce, frames_dev, 1)
    normed, fast_count = norm_forward([reduce_pre], fast_valid, [fast_reduce_norm], fast_area)
    reduce_out, reduce_centered, reduce_inv = normed[0]
    reduce_act = (fast_valid * jax.nn.silu(reduce_out)).astype(jnp.bfloat16)
    spatial_pre = plane_apply(reduce_act, fast_spatial)
    normed, fast_count = norm_forward([spatial_pre], fast_valid, [fast_spatial_norm], fast_area)
    spatial_out, spatial_centered, spatial_inv = normed[0]
    spatial_act = (fast_valid * jax.nn.silu(spatial_out)).astype(jnp.bfloat16)
    expand_pre = jnp.einsum(
        "nthwi,io->nthwo", spatial_act, fast_expand, preferred_element_type=jnp.float32
    )
    normed, fast_count = norm_forward([expand_pre], fast_valid, [fast_expand_norm], fast_area)
    expand_out, expand_centered, expand_inv = normed[0]
    fast_sum = fast_in.astype(jnp.float32) + expand_out
    fast_result = (fast_valid * jax.nn.silu(fast_sum)).astype(jnp.bfloat16)
    reach = min((frames_dev + tap_count - 2) // stride + 1, slow_frames)
    first_frame = wa_place * frames_dev
    window_start = jnp.clip(
        (first_frame - tap_count // 2 + stride - 1) // stride, 0, slow_frames - reach
    )
    grid_shape = (frames_dev, reach, tap_count)
    frame_ids = first_frame + lax.broadcasted_iota(jnp.int32, grid_shape, 0)
    slow_ids = window_start + lax.broadcasted_iota(jnp.int32, grid_shape, 1)
    tap_ids = lax.broadcasted_iota(jnp.int32, grid_shape, 2)
    selector = (frame_ids == stride * slow_ids - tap_count // 2 + tap_ids).astype(jnp.bfloat16)
    picked = jnp.einsum(
        "fsk,cfhwi->cskhwi", selector, fast_result, preferred_element_type=jnp.float32
    ).astype(jnp.bfloat16)
    windowed = jnp.einsum(
        "cskhwi,kio->cshwo", picked, lateral_weight, preferred_element_type=jnp.float32
    )
    placed = jnp.zeros(
        (lax.axis_size("wa") * own_clips, slow_frames) + windowed.shape[2:], jnp.float32
    )
    lateral_pre = lax.psum_scatter(
        lax.dynamic_update_slice_in_dim(placed, windowed, window_start, 1).astype(jnp.bfloat16),
        "wa",
        scatter_dimension=0,
        tiled=True,
    ).astype(jnp.float32)
    normed, slow_count = norm_forward([lateral_pre], own_valid, [lateral_norm], own_area)
    lateral_out, lateral_centered, lateral_inv = normed[0]
    lateral_act = (own_valid * jax.nn.silu(lateral_out)).astype(jnp.bfloat16)
    slow_own, cot_own = (
        lax.all_to_all(slow_in, "wa", split_axis=0, concat_axis=4, tiled=True),
        lax.all_to_all(slow_cot, "wa", split_axis=0, concat_axis=4, tiled=True),
    )
    slow_width = slow_own.shape[4]
    joined = jnp.concatenate([slow_own, lateral_act], axis=4)
    joined_padded = jnp.pad(joined, ((0, 0), (1, 1), (0, 0), (0, 0), (0, 0)))
    narrow_pre = time_apply(joined_padded, slow_reduce, slow_frames, 1)
    normed, slow_count = norm_forward([narrow_pre], own_valid, [slow_reduce_norm], own_area)
    narrow_out, narrow_centered, narrow_inv = normed[0]
    narrow_act = (own_valid * jax.nn.silu(narrow_out)).astype(jnp.bfloat16)
    middle_pre = plane_apply(narrow_act, slow_spatial)
    normed, slow_count = norm_forward([middle_pre], own_valid, [slow_spatial_norm], own_area)
    middle_out, middle_centered, middle_inv = normed[0]
    middle_act = (own_valid * jax.nn.silu(middle_out)).astype(jnp.bfloat16)
    widen_pre = jnp.einsum(
        "nthwi,io->nthwo", middle_act, slow_expand, preferred_element_type=jnp.float32
    )
    project_pre = jnp.einsum(
        "nthwi,io->nthwo", joined, slow_project, preferred_element_type=jnp.float32
    )
    normed, slow_count = norm_forward(
        [widen_pre, project_pre], own_valid, [slow_expand_norm, slow_project_norm], own_area
    )
    widen_out, widen_centered, widen_inv = normed[0]
    project_out, project_centered, project_inv = normed[1]
    slow_sum = widen_out + project_out
    slow_done = (own_valid * jax.nn.silu(slow_sum)).astype(jnp.bfloat16)
    slow_result = lax.all_to_all(slow_done, "wa", split_axis=4, concat_axis=0, tiled=True)
    sum_grad = cot_own.astype(jnp.float32) * own_valid * silu_slope(slow_sum)
    grad_list, pair_norm_grads = norm_backward(
        [sum_grad, sum_grad],
        [widen_centered, project_centered],
        [widen_inv, project_inv],
        [slow_expand_norm, slow_project_norm],
        own_valid,
        slow_count,
    )
    widen_low = grad_list[0].astype(jnp.bfloat16)
    project_low = grad_list[1].astype(jnp.bfloat16)
    slow_expand_grad = jnp.einsum(
        "nthwi,nthwo->io", middle_act, widen_low, preferred_element_type=jnp.float32
    )
    slow_project_grad = jnp.einsum(
        "nthwi,nthwo->io", joined, project_low, preferred_element_type=jnp.float32
    )
    middle_grad = (
        jnp.einsum("nthwo,io->nthwi", widen_low, slow_expand, preferred_element_type=jnp.float32)
        * own_valid
        * silu_slope(middle_out)
    )
    joined_grad = jnp.einsum(
        "nthwo,io->nthwi", project_low, slow_project, preferred_element_type=jnp.float32
    )
    grad_list, middle_norm_grads = norm_backward(
        [middle_grad], [middle_centered], [middle_inv], [slow_spatial_norm], own_valid, slow_count
    )
    middle_low = grad_list[0].astype(jnp.bfloat16)
    slow_spatial_grad = plane_weight_grad(narrow_act, middle_low)
    narrow_grad = plane_back(middle_low, slow_spatial) * own_valid * silu_slope(narrow_out)
    grad_list, narrow_norm_grads = norm_backward(
        [narrow_grad], [narrow_centered], [narrow_inv], [slow_reduce_norm], own_valid, slow_count
    )
    narrow_low = grad_list[0].astype(jnp.bfloat16)
    slow_reduce_grad = time_weight_grad(
        joined_padded, narrow_low, slow_reduce.shape[0], slow_frames, 1
    )
    narrow_padded = jnp.pad(narrow_low, ((0, 0), (1, 1), (0, 0), (0, 0), (0, 0)))
    joined_grad = joined_grad + time_back(narrow_padded, slow_reduce, slow_frames)
    slow_grad = lax.all_to_all(
        joined_grad[:, :, :, :, :slow_width].astype(jnp.bfloat16),
        "wa",
        split_axis=4,
        concat_axis=0,
        tiled=True,
    )
    lateral_out_grad = joined_grad[:, :, :, :, slow_width:] * own_valid * silu_slope(lateral_out)
    grad_list, lateral_norm_grads = norm_backward(
        [lateral_out_grad], [lateral_centered], [lateral_inv], [lateral_norm], own_valid, slow_count
    )
    lateral_low = grad_list[0].astype(jnp.bfloat16)
    reached = lax.dynamic_slice_in_dim(
        lax.all_gather(lateral_low, "wa", axis=0, tiled=True), window_start, reach, 1
    )
    spread = jnp.einsum(
        "fsk,cshwo->cfkhwo", selector, reached, preferred_element_type=jnp.float32
    ).astype(jnp.bfloat16)
    frame_part = jnp.einsum(
        "cfkhwo,kio->cfhwi", spread, lateral_weight, preferred_element_type=jnp.float32
    )
    weight_part = jnp.einsum(
        "cfhwi,cfkhwo->kio", fast_result, spread, preferred_element_type=jnp.float32
    )
    frames_grad = frame_part
    frames_grad, lateral_weight_grad = (frames_grad, weight_part)
    lateral_back = frames_grad.astype(jnp.bfloat16)
    fast_total = fast_cot.astype(jnp.float32) + lateral_back.astype(jnp.float32)
    fast_sum_grad = fast_total * fast_valid * silu_slope(fast_sum)
    grad_list, expand_norm_grads = norm_backward(
        [fast_sum_grad], [expand_centered], [expand_inv], [fast_expand_norm], fast_valid, fast_count
    )
    expand_low = grad_list[0].astype(jnp.bfloat16)
    fast_expand_grad = jnp.einsum(
        "nthwi,nthwo->io", spatial_act, expand_low, preferred_element_type=jnp.float32
    )
    spatial_grad = (
        jnp.einsum("nthwo,io->nthwi", expand_low, fast_expand, preferred_element_type=jnp.float32)
        * fast_valid
        * silu_slope(spatial_out)
    )
    grad_list, spatial_norm_grads = norm_backward(
        [spatial_grad],
        [spatial_centered],
        [spatial_inv],
        [fast_spatial_norm],
        fast_valid,
        fast_count,
    )
    spatial_low = grad_list[0].astype(jnp.bfloat16)
    fast_spatial_grad = plane_weight_grad(reduce_act, spatial_low)
    reduce_grad = plane_back(spatial_low, fast_spatial) * fast_valid * silu_slope(reduce_out)
    grad_list, reduce_norm_grads = norm_backward(
        [reduce_grad], [reduce_centered], [reduce_inv], [fast_reduce_norm], fast_valid, fast_count
    )
    reduce_low = grad_list[0].astype(jnp.bfloat16)
    reduce_rims = with_halo(reduce_low, (("wa", 1),), 1)
    fast_reduce_grad = time_weight_grad(
        fast_padded, reduce_low, fast_reduce.shape[0], frames_dev, 1
    )
    fast_grad = (fast_sum_grad + time_back(reduce_rims, fast_reduce, frames_dev)).astype(
        jnp.bfloat16
    )
    (
        fast_reduce_grad,
        fast_spatial_grad,
        fast_expand_grad,
        lateral_weight_grad,
        slow_reduce_grad,
        slow_spatial_grad,
        slow_expand_grad,
        slow_project_grad,
    ) = lax.psum(
        (
            fast_reduce_grad,
            fast_spatial_grad,
            fast_expand_grad,
            lateral_weight_grad,
            slow_reduce_grad,
            slow_spatial_grad,
            slow_expand_grad,
            slow_project_grad,
        ),
        ("dp", "wa"),
    )
    return (
        slow_result,
        fast_result,
        slow_grad,
        fast_grad,
        fast_reduce_grad,
        fast_spatial_grad,
        fast_expand_grad,
        lateral_weight_grad,
        slow_reduce_grad,
        slow_spatial_grad,
        slow_expand_grad,
        slow_project_grad,
        reduce_norm_grads[0],
        spatial_norm_grads[0],
        expand_norm_grads[0],
        lateral_norm_grads[0],
        narrow_norm_grads[0],
        middle_norm_grads[0],
        pair_norm_grads[0],
        pair_norm_grads[1],
    )


def solution(mesh):
    return jax.shard_map(
        per_device,
        mesh=mesh,
        in_specs=(
            P("dp", None, None, None, "wa"),
            P("dp", "wa", None, None, None),
            P("dp"),
            P(),
            P(),
            P(),
            P(),
            P(),
            P(),
            P(),
            P(),
            P(),
            P(),
            P(),
            P(),
            P(),
            P(),
            P(),
            P(),
            P("dp", None, None, None, "wa"),
            P("dp", "wa", None, None, None),
        ),
        out_specs=(
            P("dp", None, None, None, "wa"),
            P("dp", "wa", None, None, None),
            P("dp", None, None, None, "wa"),
            P("dp", "wa", None, None, None),
            P(),
            P(),
            P(),
            P(),
            P(),
            P(),
            P(),
            P(),
            P(),
            P(),
            P(),
            P(),
            P(),
            P(),
            P(),
            P(),
        ),
        check_vma=False,
    )
```

profile of v0, /device:TPU:0, one launch (start us, length us, event | category | flops | bytes accessed | tf_op | source)
XLA Modules:
  0.0 2298.5 jit_solution(2117330193145232)
XLA Ops:
  24.4 36.5 %collective-permute-done = bf16[16,1,16,16,128]{4,3,2,1,0:T(8,128)(2,1)} collective-permute-done((bf16[16,1,16,16,128]{4,3,2,1,0:T(8,128)(2,1)}, bf16[16,1,16,16,128]{4,3,2,1,0:T(8,128)(2,1)}, u32[]{:S(2)}, u32[]{:S(2)}) %collective-permute-start) | collective-permute-done | bytes 1048608 | tf_op jit(solution)/shard_map/ppermute | solution.py:14
  70.4 40.3 %all-reduce.8 = (f32[1,2,32]{2,1,0:T(2,128)S(1)}, f32[]{:T(128)}) all-reduce(f32[1,2,32]{2,1,0:T(2,128)S(1)} %maximum_bitcast_fusion.14, f32[]{:T(128)S(6)} %mul.994), channel_id=1, replica_groups=mesh['dp'=2,'wa'=16] {'dp','wa'}, use_global_device_ids=true, to_apply=%region_2.0 | all-reduce | flops 65 | bytes 520 | tf_op jit(solution)/shard_map/psum | solution.py:136
  134.6 12.9 multiply_reduce_fusion.12
  147.6 40.4 %psum.185 = f32[1,2,32]{2,1,0:T(2,128)S(1)} all-reduce(f32[1,2,32]{2,1,0:T(2,128)S(1)} %maximum_bitcast_fusion.15), channel_id=1, replica_groups=mesh['dp'=2,'wa'=16] {'dp','wa'}, use_global_device_ids=true, to_apply=%region_7.8 | all-reduce | flops 64 | bytes 512 | tf_op jit(solution)/shard_map/psum | solution.py:136
  194.6 40.5 %psum.186 = f32[1,2,128]{2,1,0:T(2,128)S(1)} all-reduce(f32[1,2,128]{2,1,0:T(2,128)S(1)} %maximum_bitcast_fusion.16), channel_id=1, replica_groups=mesh['dp'=2,'wa'=16] {'dp','wa'}, use_global_device_ids=true, to_apply=%region_10.11 | all-reduce | flops 256 | bytes 2048 | tf_op jit(solution)/shard_map/psum | solution.py:136
  240.9 8.2 fusion.80
  249.0 8.3 broadcast_in_dim.2
  265.5 14.1 reshape.709
  279.6 6.6 all-to-all-start
  286.3 14.0 reshape.713
  300.3 102.7 %all-to-all-done = bf16[16,2,65536]{2,1,0:T(2,128)(2,1)} async-done(((bf16[16,2,65536]{2,1,0:T(2,128)(2,1)}), bf16[16,2,65536]{2,1,0:T(2,128)(2,1)}, u32[]{:S(2)}, u32[]{:S(2)}) %all-to-all-start) | async-done | bytes 4194336 | tf_op jit(solution)/shard_map/all_to_all | solution.py:254
  403.0 39.0 %all-to-all-start.2 = ((bf16[16,2,65536]{2,1,0:T(2,128)(2,1)}), bf16[16,2,65536]{2,1,0:T(2,128)(2,1)}, u32[]{:S(2)}, u32[]{:S(2)}) async-start(bf16[16,2,65536]{2,1,0:T(2,128)(2,1)} %reshape.713), calls=%async_computation.3 | async-start | bytes 8388608 | tf_op jit(solution)/shard_map/all_to_all | solution.py:255
  444.9 13.6 reshape.710
  458.5 16.7 copy.103
  475.1 11.9 all_to_all.49
  487.0 54.3 %all-to-all-done.2 = bf16[16,2,65536]{2,1,0:T(2,128)(2,1)} async-done(((bf16[16,2,65536]{2,1,0:T(2,128)(2,1)}), bf16[16,2,65536]{2,1,0:T(2,128)(2,1)}, u32[]{:S(2)}, u32[]{:S(2)}) %all-to-all-start.2) | async-done | bytes 4194336 | tf_op jit(solution)/shard_map/all_to_all | solution.py:255
  541.3 13.8 reshape.714
  555.1 11.6 convert_bitcast_fusion.1
  566.7 17.7 copy.106
  584.4 14.5 reshape.646
  598.9 117.8 %reduce-scatter.2.cloned.1.call-done = bf16[1,8,16,16,256]{4,3,2,1,0:T(8,128)(2,1)} async-done(((bf16[16,8,16,16,256]{4,3,2,1,0:T(8,128)(2,1)}), bf16[1,8,16,16,256]{4,3,2,1,0:T(8,128)(2,1)}) %reduce-scatter.2.cloned.1.call-update) | async-done | bytes 1048592 | tf_op jit(solution)/shard_map/reduce_scatter | solution.py:244
  718.5 44.2 %all-reduce.7 = (f32[1,2,256]{2,1,0:T(2,128)S(1)}, f32[]{:T(128)}) all-reduce(f32[1,2,256]{2,1,0:T(2,128)S(1)} %maximum_bitcast_fusion.8, f32[]{:T(128)} %bitcast.76), channel_id=1, replica_groups=mesh['dp'=2,'wa'=16] {'dp','wa'}, use_global_device_ids=true, to_apply=%region_14.15 | all-reduce | flops 513 | bytes 4104 | tf_op jit(solution)/shard_map/psum | solution.py:136
  765.3 7.8 fusion.418
  781.2 40.5 %psum.189 = f32[1,2,256]{2,1,0:T(2,128)S(1)} all-reduce(f32[1,2,256]{2,1,0:T(2,128)S(1)} %maximum_bitcast_fusion.9), channel_id=1, replica_groups=mesh['dp'=2,'wa'=16] {'dp','wa'}, use_global_device_ids=true, to_apply=%region_18.19 | all-reduce | flops 512 | bytes 4096 | tf_op jit(solution)/shard_map/psum | solution.py:136
  832.7 40.2 %psum.190 = f32[1,2,256]{2,1,0:T(2,128)S(1)} all-reduce(f32[1,2,256]{2,1,0:T(2,128)S(1)} %maximum_bitcast_fusion.10), channel_id=1, replica_groups=mesh['dp'=2,'wa'=16] {'dp','wa'}, use_global_device_ids=true, to_apply=%region_21.22 | all-reduce | flops 512 | bytes 4096 | tf_op jit(solution)/shard_map/psum | solution.py:136
  873.6 7.7 fusion.45
  881.5 5.8 multiply_reduce_fusion.5
  887.4 40.0 %psum.191 = f32[2,2,1024]{2,1,0:T(2,128)S(1)} all-reduce(f32[2,2,1024]{2,1,0:T(2,128)S(1)} %pad_maximum_fusion.5), channel_id=1, replica_groups=mesh['dp'=2,'wa'=16] {'dp','wa'}, use_global_device_ids=true, to_apply=%region_26.27 | all-reduce | flops 4096 | bytes 32768 | tf_op jit(solution)/shard_map/psum | solution.py:136
  929.7 15.4 multiply_reduce_fusion.1
  945.1 40.4 %psum.192 = f32[2,2,1024]{2,1,0:T(2,128)S(1)} all-reduce(f32[2,2,1024]{2,1,0:T(2,128)S(1)} %pad_maximum_fusion.6), channel_id=1, replica_groups=mesh['dp'=2,'wa'=16] {'dp','wa'}, use_global_device_ids=true, to_apply=%region_30.31 | all-reduce | flops 4096 | bytes 32768 | tf_op jit(solution)/shard_map/psum | solution.py:161
  985.6 13.9 multiply_convert_fusion
  1003.1 39.7 %psum.193 = f32[1,2,256]{2,1,0:T(2,128)S(1)} all-reduce(f32[1,2,256]{2,1,0:T(2,128)S(1)} %maximum_bitcast_fusion.11), channel_id=1, replica_groups=mesh['dp'=2,'wa'=16] {'dp','wa'}, use_global_device_ids=true, to_apply=%region_33.34 | all-reduce | flops 512 | bytes 4096 | tf_op jit(solution)/shard_map/psum | solution.py:161
  1054.7 40.6 %psum.194 = f32[1,2,256]{2,1,0:T(2,128)S(1)} all-reduce(f32[1,2,256]{2,1,0:T(2,128)S(1)} %maximum_bitcast_fusion.12), channel_id=1, replica_groups=mesh['dp'=2,'wa'=16] {'dp','wa'}, use_global_device_ids=true, to_apply=%region_36.37 | all-reduce | flops 512 | bytes 4096 | tf_op jit(solution)/shard_map/psum | solution.py:161
  1109.9 8.2 fusion.43
  1118.1 15.4 add_bitcast_fusion
  1137.7 40.1 %psum.195 = f32[1,2,256]{2,1,0:T(2,128)S(1)} all-reduce(f32[1,2,256]{2,1,0:T(2,128)S(1)} %maximum_bitcast_fusion.13), channel_id=1, replica_groups=mesh['dp'=2,'wa'=16] {'dp','wa'}, use_global_device_ids=true, to_apply=%region_39.40 | all-reduce | flops 512 | bytes 4096 | tf_op jit(solution)/shard_map/psum | solution.py:161
  1186.0 8.0 pad_slice_fusion.17
  1194.0 6.1 slice.912
  1200.1 44.9 %copy.107 = bf16[1,8,16,16,1024]{3,2,1,0,4:T(8,128)(2,1)} copy(bf16[1,8,16,16,1024]{4,3,2,1,0:T(8,128)(2,1)} %slice.912) | data formatting | bytes 8388608 | tf_op jit(solution)/shard_map/slice | solution.py:323
  1245.0 37.0 %reshape.715 = bf16[16,2,65536]{2,1,0:T(2,128)(2,1)} reshape(bf16[1024,1,8,16,16]{4,3,2,1,0:T(8,128)(2,1)} %bitcast.749) | data formatting | bytes 8388608
  1287.4 44.9 %copy.104 = bf16[1,8,16,16,1024]{3,2,1,0,4:T(8,128)(2,1)} copy(bf16[1,8,16,16,1024]{4,3,2,1,0:T(8,128)(2,1)} %get-tuple-element.113) | data formatting | bytes 8388608 | tf_op jit(solution)/shard_map/convert_element_type | solution.py:280
  1332.4 37.0 %reshape.711 = bf16[16,2,65536]{2,1,0:T(2,128)(2,1)} reshape(bf16[1024,1,8,16,16]{4,3,2,1,0:T(8,128)(2,1)} %bitcast.750) | data formatting | bytes 8388608
  1377.6 9.1 fusion.7
  1404.3 23.6 %all-to-all-done.3 = bf16[16,2,65536]{2,1,0:T(2,128)(2,1)} async-done(((bf16[16,2,65536]{2,1,0:T(2,128)(2,1)}), bf16[16,2,65536]{2,1,0:T(2,128)(2,1)}, u32[]{:S(2)}, u32[]{:S(2)}) %all-to-all-start.3) | async-done | bytes 4194336 | tf_op jit(solution)/shard_map/all_to_all | solution.py:322
  1427.9 36.5 %all-to-all-start.1 = ((bf16[16,2,65536]{2,1,0:T(2,128)(2,1)}), bf16[16,2,65536]{2,1,0:T(2,128)(2,1)}, u32[]{:S(2)}, u32[]{:S(2)}) async-start(bf16[16,2,65536]{2,1,0:T(2,128)(2,1)} %reshape.711), calls=%async_computation.2 | async-start | bytes 8388608 | tf_op jit(solution)/shard_map/all_to_all | solution.py:281
  1464.5 10.5 fusion.17
  1475.0 25.6 %reshape.716 = bf16[1024,1,8,16,16]{4,3,2,1,0:T(8,128)(2,1)} reshape(bf16[16,2,65536]{2,1,0:T(2,128)(2,1)} %all-to-all-done.3) | data formatting | bytes 8388608
  1500.6 39.5 %copy.108 = bf16[1,8,16,16,16,64]{5,3,2,1,4,0:T(8,128)(2,1)} copy(bf16[1,8,16,16,16,64]{3,2,1,5,4,0:T(8,128)(2,1)} %bitcast.747) | data formatting | bytes 8388608 | tf_op jit(solution)/shard_map/all_to_all | solution.py:322
  1544.1 25.6 %reshape.712 = bf16[1024,1,8,16,16]{4,3,2,1,0:T(8,128)(2,1)} reshape(bf16[16,2,65536]{2,1,0:T(2,128)(2,1)} %all-to-all-done.1) | data formatting | bytes 8388608
  1569.7 39.5 %copy.105 = bf16[1,8,16,16,16,64]{5,3,2,1,4,0:T(8,128)(2,1)} copy(bf16[1,8,16,16,16,64]{3,2,1,5,4,0:T(8,128)(2,1)} %bitcast.748) | data formatting | bytes 8388608 | tf_op jit(solution)/shard_map/all_to_all | solution.py:281
  1611.8 14.3 convert_bitcast_fusion
  1626.2 30.3 %fusion.118 = f32[5,128,256]{1,2,0:T(8,128)} fusion(bf16[16,2,5,16,16,256]{5,2,1,4,3,0:T(8,128)(2,1)} %convert_bitcast_fusion, bf16[16,2,16,16,128]{4,3,2,1,0:T(8,128)(2,1)S(1)} %copy-done.27), kind=kOutput, calls=%fused_computation.219 | convolution fusion | flops 2684354560 | bytes 23724032 | tf_op jit(solution)/shard_map/cfhwi,cfkhwo->kio/dot_general | solution.py:343
  1656.5 27.7 %multiply_reduce_fusion.8 = (f32[128]{0:T(128)S(1)}, f32[128]{0:T(128)S(1)}, f32[16,2,16,16,128]{4,3,2,1,0:T(8,128)}) fusion(f32[16,2,16,16,128]{4,3,2,1,0:T(8,128)} %get-tuple-element.197, f32[128]{0:T(128)S(1)} %copy-done.86, f32[128]{0:T(128)S(1)} %copy-done.98, f32[128]{0:T(128)S(1)} %copy-done.119, f32[128]{0:T(128)S(1)} %copy-done.101, ...), kind=kOutput, calls=%fused_computation.69 | convolution fusion | flops 2707423232 | bytes 33901568 | tf_op jit(solution)/shard_map/cfkhwo,kio->cfhwi/dot_general | solution.py:340
  1684.3 55.2 %psum.196 = f32[1,2,128]{2,1,0:T(2,128)S(1)} all-reduce(f32[1,2,128]{2,1,0:T(2,128)S(1)} %maximum_bitcast_fusion.17), channel_id=1, replica_groups=mesh['dp'=2,'wa'=16] {'dp','wa'}, use_global_device_ids=true, to_apply=%region_42.43 | all-reduce | flops 256 | bytes 2048 | tf_op jit(solution)/shard_map/psum | solution.py:161
  1739.6 6.5 multiply_convert_fusion.5
  1750.3 39.6 %psum.197 = f32[1,2,32]{2,1,0:T(2,128)S(1)} all-reduce(f32[1,2,32]{2,1,0:T(2,128)S(1)} %maximum_bitcast_fusion.18), channel_id=1, replica_groups=mesh['dp'=2,'wa'=16] {'dp','wa'}, use_global_device_ids=true, to_apply=%region_45.46 | all-reduce | flops 64 | bytes 512 | tf_op jit(solution)/shard_map/psum | solution.py:161
  1789.9 6.0 multiply_convert_fusion.4
  1818.5 15.0 multiply_reduce_fusion.6
  1833.5 40.8 %psum.198 = f32[1,2,32]{2,1,0:T(2,128)S(1)} all-reduce(f32[1,2,32]{2,1,0:T(2,128)S(1)} %maximum_bitcast_fusion.19), channel_id=1, replica_groups=mesh['dp'=2,'wa'=16] {'dp','wa'}, use_global_device_ids=true, to_apply=%region_48.49 | all-reduce | flops 64 | bytes 512 | tf_op jit(solution)/shard_map/psum | solution.py:161
  1874.9 6.1 multiply_convert_fusion.3
  1884.3 6.2 collective-permute-start.3
  1920.3 24.3 %collective-permute-done.3 = bf16[16,1,16,16,32]{4,3,2,1,0:T(8,128)(2,1)} collective-permute-done((bf16[16,1,16,16,32]{4,3,2,1,0:T(8,128)(2,1)}, bf16[16,1,16,16,32]{4,3,2,1,0:T(8,128)(2,1)}, u32[]{:S(2)}, u32[]{:S(2)}) %collective-permute-start.3) | collective-permute-done | bytes 262176 | tf_op jit(solution)/shard_map/ppermute | solution.py:14
  1948.3 196.9 %all-reduce.15.cloned.1.call-done = (f32[5,128,256]{1,2,0:T(8,128)}, f32[3,1280,256]{2,1,0:T(8,128)}, f32[3,3,256,256]{3,2,1,0:T(8,128)}, f32[256,1024]{1,0:T(8,128)}, f32[1280,1024]{1,0:T(8,128)}) async-done(((f32[5,128,256]{1,2,0:T(8,128)}, f32[3,1280,256]{2,1,0:T(8,128)}, f32[3,3,256,256]{3,2,1,0:T(8,128)}, f32[256,1024]{1,0:T(8,128)}, f32[1280,1024]{1,0:T(8,128)}), (f32[5,128,256]{1,2,0:T(8,128)}, ...) | async-done | bytes 13238288 | tf_op jit(solution)/shard_map/psum | solution.py:394
  2147.4 128.9 %all-reduce.13.cloned.1.call-done = (f32[3,128,32]{1,2,0:T(8,128)}, f32[3,3,32,32]{3,2,1,0:T(8,128)}, f32[32,128]{1,0:T(8,128)}) async-done(((f32[3,128,32]{1,2,0:T(8,128)}, f32[3,3,32,32]{3,2,1,0:T(8,128)}, f32[32,128]{1,0:T(8,128)}), (f32[3,128,32]{1,2,0:T(8,128)}, f32[3,3,32,32]{3,2,1,0:T(8,128)}, f32[32,128]{1,0:T(8,128)})) %all-reduce.13.cloned.1.call-update) | async-done | bytes 102416 | tf_op jit(solution)/shard_map/psum | solution.py:394
  (462 shorter events, 259.8 us)
Async XLA Ops:
  7.2 866.4 %copy-start = (bf16[1280,1024]{1,0:T(8,128)(2,1)S(1)}, bf16[1280,1024]{1,0:T(8,128)(2,1)}, u32[]{:S(2)}) copy-start(bf16[1280,1024]{1,0:T(8,128)(2,1)} %param.31) | copy-start | bytes 7864324
  7.2 10.8 copy-start.123
  7.2 10.8 copy-start.124
  7.2 10.8 copy-start.125
  7.2 11.5 copy-start.70
  7.3 709.4 %reduce-scatter.2.cloned.1.call-start = ((), (), s32[]{:S(2)}) async-start(), calls=%async_computation.5 | async-start | bytes 17825792 | tf_op jit(solution)/shard_map/reduce_scatter | solution.py:244
  10.9 50.0 %collective-permute-start = (bf16[16,1,16,16,128]{4,3,2,1,0:T(8,128)(2,1)}, bf16[16,1,16,16,128]{4,3,2,1,0:T(8,128)(2,1)}, u32[]{:S(2)}, u32[]{:S(2)}) collective-permute-start(bf16[16,1,16,16,128]{4,3,2,1,0:T(8,128)(2,1)} %get-tuple-element.131), channel_id=1, source_target_pairs={{0,1},{1,2},{2,3},{3,4},{4,5},{5,6},{6,7},{7,8},{8,9},{9,10},{10,1... | collective-permute-start | bytes 3145736 | tf_op jit(solution)/shard_map/ppermute | solution.py:14
  16.7 48.6 %collective-permute-start.1 = (bf16[16,1,16,16,128]{4,3,2,1,0:T(8,128)(2,1)}, bf16[16,1,16,16,128]{4,3,2,1,0:T(8,128)(2,1)}, u32[]{:S(2)}, u32[]{:S(2)}) collective-permute-start(bf16[16,1,16,16,128]{4,3,2,1,0:T(8,128)(2,1)} %get-tuple-element.130), channel_id=1, source_target_pairs={{1,0},{2,1},{3,2},{4,3},{5,4},{6,5},{7,6},{8,7},{9,8},{10,9},{11,1... | collective-permute-start | bytes 3145736 | tf_op jit(solution)/shard_map/ppermute | solution.py:17
  18.0 93.4 %copy-start.92 = (f32[32]{0:T(128)}, f32[32]{0:T(128)S(1)}, u32[]{:S(2)}) copy-start(f32[32]{0:T(128)S(1)} %get-tuple-element.193) | copy-start | bytes 388
  18.0 93.4 %copy-start.105 = (f32[32]{0:T(128)}, f32[32]{0:T(128)S(1)}, u32[]{:S(2)}) copy-start(f32[32]{0:T(128)S(1)} %get-tuple-element.194) | copy-start | bytes 388
  18.1 170.6 %copy-start.102 = (f32[32]{0:T(128)}, f32[32]{0:T(128)S(1)}, u32[]{:S(2)}) copy-start(f32[32]{0:T(128)S(1)} %get-tuple-element.191) | copy-start | bytes 388
  18.1 170.6 %copy-start.116 = (f32[32]{0:T(128)}, f32[32]{0:T(128)S(1)}, u32[]{:S(2)}) copy-start(f32[32]{0:T(128)S(1)} %get-tuple-element.192) | copy-start | bytes 388
  18.1 217.7 %copy-start.99 = (f32[128]{0:T(128)}, f32[128]{0:T(128)S(1)}, u32[]{:S(2)}) copy-start(f32[128]{0:T(128)S(1)} %get-tuple-element.189) | copy-start | bytes 1540
  18.1 217.7 %copy-start.118 = (f32[128]{0:T(128)}, f32[128]{0:T(128)S(1)}, u32[]{:S(2)}) copy-start(f32[128]{0:T(128)S(1)} %get-tuple-element.190) | copy-start | bytes 1540
  24.3 38.0 %copy-start.13 = (bf16[16,2,16,16,128]{4,3,2,1,0:T(8,128)(2,1)S(1)}, bf16[16,2,16,16,128]{4,3,2,1,0:T(8,128)(2,1)}, u32[]{:S(2)}) copy-start(bf16[16,2,16,16,128]{4,3,2,1,0:T(8,128)(2,1)} %param.22) | copy-start | bytes 6291460
  24.4 211.4 %copy-start.28 = (f32[16,16,16]{2,1,0:T(8,128)}, f32[16,16,16]{2,1,0:T(8,128)S(1)}, u32[]{:S(2)}) copy-start(f32[16,16,16]{2,1,0:T(8,128)S(1)} %fusion.267) | copy-start | bytes 49156
  114.7 20.0 copy-start.2
  240.9 16.5 copy-start.131
  249.0 11.5 copy-start.19
  279.6 123.3 %all-to-all-start = ((bf16[16,2,65536]{2,1,0:T(2,128)(2,1)}), bf16[16,2,65536]{2,1,0:T(2,128)(2,1)}, u32[]{:S(2)}, u32[]{:S(2)}) async-start(bf16[16,2,65536]{2,1,0:T(2,128)(2,1)} %reshape.709), calls=%async_computation | async-start | bytes 8388608 | tf_op jit(solution)/shard_map/all_to_all | solution.py:254
  300.3 144.4 %copy-start.120 = (f32[2,256]{1,0:T(2,128)S(1)}, f32[2,256]{1,0:T(2,128)}, u32[]{:S(2)}) copy-start(f32[2,256]{1,0:T(2,128)} %param.35) | copy-start | bytes 6148
  300.3 144.5 %copy-start.121 = (f32[2,256]{1,0:T(2,128)S(1)}, f32[2,256]{1,0:T(2,128)}, u32[]{:S(2)}) copy-start(f32[2,256]{1,0:T(2,128)} %param.36) | copy-start | bytes 6148
  300.3 144.5 %copy-start.122 = (f32[2,256]{1,0:T(2,128)S(1)}, f32[2,256]{1,0:T(2,128)}, u32[]{:S(2)}) copy-start(f32[2,256]{1,0:T(2,128)} %param.37) | copy-start | bytes 6148
  300.3 144.5 %copy-start.79 = (f32[2,1024]{1,0:T(2,128)S(1)}, f32[2,1024]{1,0:T(2,128)}, u32[]{:S(2)}) copy-start(f32[2,1024]{1,0:T(2,128)} %param.38) | copy-start | bytes 24580
  300.3 144.6 %copy-start.80 = (f32[2,1024]{1,0:T(2,128)S(1)}, f32[2,1024]{1,0:T(2,128)}, u32[]{:S(2)}) copy-start(f32[2,1024]{1,0:T(2,128)} %param.39) | copy-start | bytes 24580
  403.0 138.3 %all-to-all-start.2 = ((bf16[16,2,65536]{2,1,0:T(2,128)(2,1)}), bf16[16,2,65536]{2,1,0:T(2,128)(2,1)}, u32[]{:S(2)}, u32[]{:S(2)}) async-start(bf16[16,2,65536]{2,1,0:T(2,128)(2,1)} %reshape.713), calls=%async_computation.3 | async-start | bytes 8388608 | tf_op jit(solution)/shard_map/all_to_all | solution.py:255
  442.0 1167.2 %all-gather.2.cloned.1.call-start = ((), (), s32[]{:S(2)}) async-start(), calls=%async_computation.6 | async-start | bytes 17825792 | tf_op jit(solution)/shard_map/all_gather | solution.py:335
  444.7 688.8 %copy-start.64 = (f32[16,16]{1,0:T(8,128)}, f32[16,16]{1,0:T(8,128)S(1)}, u32[]{:S(2)}) copy-start(f32[16,16]{1,0:T(8,128)S(1)} %fusion.349) | copy-start | bytes 3076
  444.8 554.7 %copy-start.111 = (f32[1,256]{1,0:T(1,128)}, f32[1,256]{1,0:T(1,128)S(1)}, u32[]{:S(2)}) copy-start(f32[1,256]{1,0:T(1,128)S(1)} %get-tuple-element.171) | copy-start | bytes 3076
  444.8 554.7 %copy-start.126 = (f32[1,256]{1,0:T(1,128)}, f32[1,256]{1,0:T(1,128)S(1)}, u32[]{:S(2)}) copy-start(f32[1,256]{1,0:T(1,128)S(1)} %get-tuple-element.172) | copy-start | bytes 3076
  765.3 7.8 copy-start.46
  765.3 7.8 copy-start.60
  873.6 169.2 %copy-start.77 = (f32[1,1,256]{2,1,0:T(1,128)}, f32[1,1,256]{2,1,0:T(1,128)S(1)}, u32[]{:S(2)}) copy-start(f32[1,1,256]{2,1,0:T(1,128)S(1)} %get-tuple-element.173) | copy-start | bytes 3076
  873.6 7.9 copy-start.33
  873.6 7.9 copy-start.129
  881.3 161.5 %copy-start.75 = (f32[256]{0:T(256)}, f32[256]{0:T(256)S(1)}, u32[]{:S(2)}) copy-start(f32[256]{0:T(256)S(1)} %add_rsqrt_fusion.2) | copy-start | bytes 3076
  985.6 13.9 copy-start.68
  985.6 14.0 copy-start.34
  985.6 14.0 copy-start.130
  1098.9 19.2 copy-start.21
  1118.1 15.4 copy-start.24
  1282.0 145.9 %all-to-all-start.3 = ((bf16[16,2,65536]{2,1,0:T(2,128)(2,1)}), bf16[16,2,65536]{2,1,0:T(2,128)(2,1)}, u32[]{:S(2)}, u32[]{:S(2)}) async-start(bf16[16,2,65536]{2,1,0:T(2,128)(2,1)} %reshape.715), calls=%async_computation.4 | async-start | bytes 8388608 | tf_op jit(solution)/shard_map/all_to_all | solution.py:322
  1332.4 37.0 %copy-start.6 = (bf16[1,8,16,16,256]{4,3,2,1,0:T(8,128)(2,1)S(1)}, bf16[1,8,16,16,256]{4,3,2,1,0:T(8,128)(2,1)}, u32[]{:S(2)}) copy-start(bf16[1,8,16,16,256]{4,3,2,1,0:T(8,128)(2,1)} %copy-done.5) | copy-start | bytes 3145732
  1377.6 9.1 copy-start.22
  1427.9 116.2 %all-to-all-start.1 = ((bf16[16,2,65536]{2,1,0:T(2,128)(2,1)}), bf16[16,2,65536]{2,1,0:T(2,128)(2,1)}, u32[]{:S(2)}, u32[]{:S(2)}) async-start(bf16[16,2,65536]{2,1,0:T(2,128)(2,1)} %reshape.711), calls=%async_computation.2 | async-start | bytes 8388608 | tf_op jit(solution)/shard_map/all_to_all | solution.py:281
  1464.4 680.8 %all-reduce.15.cloned.1.call-start = ((), (), s32[]{:S(2)}) async-start(), calls=%async_computation.8 | async-start | bytes 26476544 | tf_op jit(solution)/shard_map/psum | solution.py:394
  1611.8 14.4 copy-start.27
  1626.2 30.3 %copy-start.14 = (bf16[16,2,16,16,128]{4,3,2,1,0:T(8,128)(2,1)S(1)}, bf16[16,2,16,16,128]{4,3,2,1,0:T(8,128)(2,1)}, u32[]{:S(2)}) copy-start(bf16[16,2,16,16,128]{4,3,2,1,0:T(8,128)(2,1)} %param.22) | copy-start | bytes 6291460
  1626.2 30.3 %copy-start.30 = (f32[16,16,16]{2,1,0:T(8,128)S(1)}, f32[16,16,16]{2,1,0:T(8,128)}, u32[]{:S(2)}) copy-start(f32[16,16,16]{2,1,0:T(8,128)} %copy-done.28) | copy-start | bytes 49156
  1626.2 30.3 %copy-start.86 = (f32[128]{0:T(128)S(1)}, f32[128]{0:T(128)}, u32[]{:S(2)}) copy-start(f32[128]{0:T(128)} %copy-done.84) | copy-start | bytes 1540
  1626.2 30.3 %copy-start.98 = (f32[128]{0:T(128)S(1)}, f32[128]{0:T(128)}, u32[]{:S(2)}) copy-start(f32[128]{0:T(128)} %copy-done.97) | copy-start | bytes 1540
  1626.2 30.3 %copy-start.101 = (f32[128]{0:T(128)S(1)}, f32[128]{0:T(128)}, u32[]{:S(2)}) copy-start(f32[128]{0:T(128)} %copy-done.99) | copy-start | bytes 1540
  1626.2 30.3 %copy-start.119 = (f32[128]{0:T(128)S(1)}, f32[128]{0:T(128)}, u32[]{:S(2)}) copy-start(f32[128]{0:T(128)} %copy-done.118) | copy-start | bytes 1540
  1626.2 30.3 %copy-start.132 = (bf16[5,128,256]{2,1,0:T(8,128)(2,1)S(1)}, bf16[5,128,256]{2,1,0:T(8,128)(2,1)}, u32[]{:S(2)}) copy-start(bf16[5,128,256]{2,1,0:T(8,128)(2,1)} %param.27) | copy-start | bytes 983044
  1739.6 6.6 copy-start.89
  1739.6 6.6 copy-start.96
  1874.9 401.4 %all-reduce.13.cloned.1.call-start = ((), (), s32[]{:S(2)}) async-start(), calls=%async_computation.7 | async-start | bytes 425984 | tf_op jit(solution)/shard_map/psum | solution.py:394
  1881.0 27.0 %copy-start.10 = (bf16[16,2,16,16,32]{4,3,2,1,0:T(8,128)(2,1)}, bf16[16,2,16,16,32]{4,3,2,1,0:T(8,128)(2,1)S(1)}, u32[]{:S(2)}) copy-start(bf16[16,2,16,16,32]{4,3,2,1,0:T(8,128)(2,1)S(1)} %multiply_convert_fusion.3) | copy-start | bytes 1572868
  1881.0 9.5 copy-start.55
  1882.7 35.7 %collective-permute-start.2 = (bf16[16,1,16,16,32]{4,3,2,1,0:T(8,128)(2,1)}, bf16[16,1,16,16,32]{4,3,2,1,0:T(8,128)(2,1)}, u32[]{:S(2)}, u32[]{:S(2)}) collective-permute-start(bf16[16,1,16,16,32]{4,3,2,1,0:T(8,128)(2,1)} %get-tuple-element.129), channel_id=1, source_target_pairs={{1,0},{2,1},{3,2},{4,3},{5,4},{6,5},{7,6},{8,7},{9,8},{10,9},{11,1... | collective-permute-start | bytes 786440 | tf_op jit(solution)/shard_map/ppermute | solution.py:17
  1884.3 60.3 %collective-permute-start.3 = (bf16[16,1,16,16,32]{4,3,2,1,0:T(8,128)(2,1)}, bf16[16,1,16,16,32]{4,3,2,1,0:T(8,128)(2,1)}, u32[]{:S(2)}, u32[]{:S(2)}) collective-permute-start(bf16[16,1,16,16,32]{4,3,2,1,0:T(8,128)(2,1)} %get-tuple-element.128), channel_id=1, source_target_pairs={{0,1},{1,2},{2,3},{3,4},{4,5},{5,6},{6,7},{7,8},{8,9},{9,10},{10,1... | collective-permute-start | bytes 786440 | tf_op jit(solution)/shard_map/ppermute | solution.py:14
  1913.4 31.2 %copy-start.25 = (f32[16,2,16,16,128]{4,3,2,1,0:T(8,128)S(1)}, f32[16,2,16,16,128]{4,3,2,1,0:T(8,128)}, u32[]{:S(2)}) copy-start(f32[16,2,16,16,128]{4,3,2,1,0:T(8,128)} %get-tuple-element.203) | copy-start | bytes 12582916
  2277.7 10.4 slice-start
  2280.8 7.4 slice-start.1
  (87 other events, 279.1 us)
Sparse Core Ops, SparseCore 0:
  265.6 450.9 reduce-scatter.1
  1181.8 274.0 all-gather.1
  1874.5 270.7 all-reduce.14
  2152.6 123.6 all-reduce.12
where the time goes:
time: 2310 us; the launch traced here: 2300 us
  waiting for transfers between devices  694 us (30%)
  blocking collectives  583 us (25%)
  local copies, waits for them, and re-layouts  501 us (22%)
  matrix products  283 us (12%)
  other arithmetic  117 us (5%)
  starting transfers between devices  103 us (4%)
    psum x2, waiting for transfers between devices, per_device(): lax.psum((fast_reduce_grad, fast_spatial_grad, fast_expand_grad, lateral_...  326 us
    psum x7, blocking collectives, norm_backward(): totals = lax.psum(stacked, ('dp', 'wa'))  296 us
    psum x7, blocking collectives, norm_forward(): totals, count_all = lax.psum((moments, count_term), ('dp', 'wa'))  286 us
    unnamed x296, local copies, waits for them, and re-layouts  225 us
    reduce_scatter x1, waiting for transfers between devices, per_device(): lax.psum_scatter(lax.dynamic_update_slice_in_dim(placed, windowed, window...  118 us
    all_to_all x1, waiting for transfers between devices, per_device(): lax.all_to_all(slow_in, 'wa', split_axis=0, concat_axis=4, tiled=True)  103 us
    ppermute x2, waiting for transfers between devices, with_halo(): lax.ppermute(lax.slice_in_dim(block, block.shape[dim] - width, None, axis...  60.8 us
    all_to_all x1, waiting for transfers between devices, per_device(): lax.all_to_all(slow_cot, 'wa', split_axis=0, concat_axis=4, tiled=True)  54.3 us
  transfers between devices with their start and end apart: 12, of which 10 were waited for; matrix products, arithmetic and copies ran while one was open for 22% of the time, Pallas kernels for 0%

commit v1 on v0

v1 whole, which is shorter than its diff:
```python
import functools

import jax
import jax.numpy as jnp
from jax import lax
from jax.experimental import pallas as pl
from jax.experimental.pallas import tpu as pltpu
from jax.sharding import PartitionSpec as P

EPSILON = 1e-05
BF = jnp.bfloat16
F32 = jnp.float32
LANES = 128
GROUPS = 4
VMEM_BYTES = 52 * 1024 * 1024


def whole(array):
    rank = len(array.shape)
    return pl.BlockSpec(array.shape, lambda *_: (0,) * rank)


def scalars():
    return pl.BlockSpec(memory_space=pltpu.SMEM)


def launch(body, name, grid, inputs, outputs, scratch=(), flops=0, after=(), carry=()):
    used, given = len(inputs), len(outputs)
    held = pl.BlockSpec(memory_space=pl.ANY)
    inputs = inputs + [(array, held) for array in (*after, *carry)]
    outputs = outputs + [(array.shape, array.dtype, held) for array in carry]
    first = used + len(after)
    aliases = {first + k: given + k for k in range(len(carry))}

    def kernel(*refs):
        outs = refs[len(inputs) :]
        body(*refs[:used], *outs[:given], *outs[len(outputs) :])

    traffic = sum(a.size * a.dtype.itemsize for a, _ in inputs)
    for shape, dtype, _ in outputs:
        count = 1
        for entry in shape:
            count *= entry
        traffic += count * jnp.dtype(dtype).itemsize
    return pl.pallas_call(
        kernel,
        name=name,
        grid=grid,
        in_specs=[spec for _, spec in inputs],
        out_specs=[spec for _, _, spec in outputs],
        out_shape=[jax.ShapeDtypeStruct(shape, dtype) for shape, dtype, _ in outputs],
        scratch_shapes=list(scratch),
        input_output_aliases=aliases,
        compiler_params=pltpu.CompilerParams(vmem_limit_bytes=VMEM_BYTES),
        cost_estimate=pl.CostEstimate(flops=flops, bytes_accessed=traffic, transcendentals=0),
    )(*[array for array, _ in inputs])


def dot(a, b):
    return lax.dot_general(a, b, (((1,), (0,)), ((), ())), preferred_element_type=F32)


def dot_nt(a, b):
    return lax.dot_general(a, b, (((1,), (1,)), ((), ())), preferred_element_type=F32)


def dot_tn(a, b):
    return lax.dot_general(a, b, (((0,), (0,)), ((), ())), preferred_element_type=F32)


def logistic(u):
    return 0.5 * jnp.tanh(0.5 * u) + 0.5


def silu(u):
    return u * logistic(u)


def silu_slope(u):
    g = logistic(u)
    return g + u * g * (1.0 - g)


def cell_ids(rows):
    ids = lax.broadcasted_iota(jnp.int32, (rows, 1), 0)
    return (ids >> 4) & 15, ids & 15


def clip_mask(side, rows):
    h, w = cell_ids(rows)
    return jnp.where((h < side) & (w < side), 1.0, 0.0).astype(F32)


def packed_mask(side_row, rows):
    ids = lax.broadcasted_iota(jnp.int32, (rows, LANES), 0)
    h, w = (ids >> 4) & 15, ids & 15
    return jnp.where((h < side_row) & (w < side_row), 1.0, 0.0).astype(F32)


def fold(row):
    width = LANES // GROUPS
    out = row
    for step in range(1, GROUPS):
        out = out + pltpu.roll(row, step * width, 1)
    return out


def norm_terms(gathered, params, count, folded=False):
    total = jnp.sum(gathered, axis=0)
    if folded:
        total = fold(total)
    mean = total[0:1] / count
    variance = total[1:2] / count - mean * mean
    inv = lax.rsqrt(variance + EPSILON)
    scale = params[0:1] * inv
    return mean, inv, scale, params[1:2] - mean * scale


def back_terms(gathered, params, count, mean, inv, folded=False):
    total = jnp.sum(gathered, axis=0)
    if folded:
        total = fold(total)
    a = params[0:1] * inv
    b = -a * inv * inv * total[1:2] / count
    return a, b, -a * total[0:1] / count - b * mean


def col_sum(v):
    return jnp.sum(v, axis=0, keepdims=True)


def add_stats(acc, first, rows, values):
    @pl.when(first)
    def _():
        acc[...] = jnp.zeros_like(acc)

    for row, value in zip(rows, values):
        acc[row : row + 1, :] += value


def send_stats(last, acc, out):
    @pl.when(last)
    def _():
        out[...] = jnp.broadcast_to(acc[...][None], out.shape)


def put_columns(wide, out):
    rows, width = wide.shape[0], out.shape[1]
    for block in range(wide.shape[1] // width):
        out[block * rows : (block + 1) * rows, :] = wide[:, block * width : (block + 1) * width].astype(BF)


def plane_windows(values, cells):
    rows = values.shape[0]
    w = lax.broadcasted_iota(jnp.int32, (rows, 1), 0) & (cells - 1)
    left = jnp.where(w == 0, 0.0, pltpu.roll(values, 1, 0))
    right = jnp.where(w == cells - 1, 0.0, pltpu.roll(values, rows - 1, 0))
    return jnp.concatenate([left.astype(BF), values.astype(BF), right.astype(BF)], axis=1)


def fill_windows(scratch, windows, cells):
    rows = windows.shape[0]
    zeros = jnp.zeros((cells, windows.shape[1]), BF)
    scratch[0:cells, :] = zeros
    scratch[cells : cells + rows, :] = windows
    scratch[cells + rows : 2 * cells + rows, :] = zeros


def plane_dot(scratch, weight, rows, cells):
    out = dot(scratch[0:rows, :], weight[0])
    for tap in (1, 2):
        out = out + dot(scratch[tap * cells : tap * cells + rows, :], weight[tap])
    return out


def fast_first(x, w, y, to_next, to_prev):
    def over(frame, tap):
        out = dot(x[0, frame], w[tap, 0])
        for g in range(1, GROUPS):
            out = out + dot(x[g, frame], w[tap, g])
        return out

    y[0, 0] = over(0, 1) + over(1, 2)
    y[0, 1] = over(0, 0) + over(1, 1)
    to_next[0] = over(1, 0).astype(BF)
    to_prev[0] = over(0, 2).astype(BF)


def fast_join(y, from_prev, from_next, sides, pre, stats, acc):
    i = pl.program_id(0)
    mask = packed_mask(sides[0], 256)
    first = y[0, 0] + from_prev[0].astype(F32)
    second = y[0, 1] + from_next[0].astype(F32)
    pre[0, 0] = first
    pre[0, 1] = second
    m1, m2 = first * mask, second * mask
    add_stats(acc, i == 0, (0, 1), (col_sum(m1 + m2), col_sum(m1 * first + m2 * second)))
    send_stats(i == pl.num_programs(0) - 1, acc, stats)


def fast_plane(count, pre, g1, params, sides, w, act, out, stats, acc, win):
    i = pl.program_id(0)
    _, _, scale, shift = norm_terms(g1[...], params[...], count[0, 0], True)
    mask = packed_mask(sides[0], 256)
    sums, squares = [], []
    for frame in range(2):
        a = mask * silu(pre[0, frame] * scale + shift)
        act[0, frame] = a.astype(BF)
        fill_windows(win, plane_windows(a, 16), 16)
        v = plane_dot(win, w, 256, 16)
        out[0, frame] = v
        mv = mask * v
        sums.append(mv)
        squares.append(mv * v)
    add_stats(acc, i == 0, (0, 1), (col_sum(sums[0] + sums[1]), col_sum(squares[0] + squares[1])))
    send_stats(i == pl.num_programs(0) - 1, acc, stats)


def fast_widen(count, pre, g2, params, sides, w, act, stats, acc):
    i = pl.program_id(0)
    _, _, scale, shift = norm_terms(g2[...], params[...], count[0, 0], True)
    mask = packed_mask(sides[0], 256)
    total, square = None, None
    for frame in range(2):
        a = (mask * silu(pre[0, frame] * scale + shift)).astype(BF)
        act[0, frame] = a
        for g in range(GROUPS):
            v = dot(a, w[g])
            total = v if total is None else total + v
            square = v * v if square is None else square + v * v
    add_stats(acc, i == 0, (0, 1), (col_sum(total), col_sum(square)))
    send_stats(i == pl.num_programs(0) - 1, acc, stats)


def fast_out(count, sides, x, act, g3, params, w, result):
    i = pl.program_id(0)
    _, _, scale, shift = norm_terms(g3[...], params[...], count[0, 0])
    for g in range(GROUPS):
        mask = clip_mask(sides[i * GROUPS + g], 256)
        for frame in range(2):
            u = x[g, frame].astype(F32) + dot(act[0, frame], w[g]) * scale + shift
            result[g, frame] = (mask * silu(u)).astype(BF)


def fast_back_sum(count, sides, cot, back, x, act, g3, params, w, grad, stats, acc):
    i = pl.program_id(0)
    mean, _, scale, shift = norm_terms(g3[...], params[...], count[0, 0])
    total, cross = None, None
    for g in range(GROUPS):
        mask = clip_mask(sides[i * GROUPS + g], 256)
        for frame in range(2):
            v = dot(act[0, frame], w[g])
            u = x[g, frame].astype(F32) + v * scale + shift
            e = (cot[g, frame].astype(F32) + back[g, frame].astype(F32)) * mask * silu_slope(u)
            grad[g, frame] = e
            total = e if total is None else total + e
            c = e * (v - mean)
            cross = c if cross is None else cross + c
    add_stats(acc, i == 0, (0, 1), (col_sum(total), col_sum(cross)))
    send_stats(i == pl.num_programs(0) - 1, acc, stats)


def fast_back_widen(
    count, sides, grad, act, g3, h3, params3, w, pre, g2, params2, lane_sides, out, w_grad, stats, acc
):
    i = pl.program_id(0)
    c = count[0, 0]
    mean3, inv3, _, _ = norm_terms(g3[...], params3[...], c)
    a, b, d = back_terms(h3[...], params3[...], c, mean3, inv3)
    mean2, _, scale2, shift2 = norm_terms(g2[...], params2[...], c, True)
    lane_mask = packed_mask(lane_sides[0], 256)

    @pl.when(i == 0)
    def _():
        w_grad[...] = jnp.zeros_like(w_grad)

    total, cross = None, None
    for frame in range(2):
        s = act[0, frame]
        back = None
        for g in range(GROUPS):
            mask = clip_mask(sides[i * GROUPS + g], 256)
            v = dot(s, w[g])
            low = (mask * (grad[g, frame] * a + v * b + d)).astype(BF)
            part = dot_nt(low, w[g])
            back = part if back is None else back + part
            w_grad[g] += dot_tn(s, low)
        p = pre[0, frame]
        e = back * lane_mask * silu_slope(p * scale2 + shift2)
        out[0, frame] = e
        total = e if total is None else total + e
        x = e * (p - mean2)
        cross = x if cross is None else cross + x
    add_stats(acc, i == 0, (0, 1), (col_sum(total), col_sum(cross)))
    send_stats(i == pl.num_programs(0) - 1, acc, stats)


def fast_back_plane(
    count, e2, pre2, g2, h2, params2, act1, pre1, g1, params1, lane_sides, w, out, w_grad, stats, acc, win
):
    i = pl.program_id(0)
    c = count[0, 0]
    mean2, inv2, _, _ = norm_terms(g2[...], params2[...], c, True)
    a, b, d = back_terms(h2[...], params2[...], c, mean2, inv2, True)
    mean1, _, scale1, shift1 = norm_terms(g1[...], params1[...], c, True)
    mask = packed_mask(lane_sides[0], 256)

    @pl.when(i == 0)
    def _():
        w_grad[...] = jnp.zeros_like(w_grad)

    total, cross = None, None
    for frame in range(2):
        low = mask * (e2[0, frame] * a + pre2[0, frame] * b + d)
        fill_windows(win, plane_windows(low, 16), 16)
        p = pre1[0, frame]
        e = plane_dot(win, w, 256, 16) * mask * silu_slope(p * scale1 + shift1)
        out[0, frame] = e
        total = e if total is None else total + e
        x = e * (p - mean1)
        cross = x if cross is None else cross + x
        low = low.astype(BF)
        fill_windows(win, plane_windows(act1[0, frame].astype(F32), 16), 16)
        for tap in range(3):
            w_grad[tap] += dot_tn(win[16 * tap : 16 * tap + 256, :], low)
    add_stats(acc, i == 0, (0, 1), (col_sum(total), col_sum(cross)))
    send_stats(i == pl.num_programs(0) - 1, acc, stats)


def fast_back_first(count, e1, pre1, g1, h1, params1, lane_sides, low):
    c = count[0, 0]
    mean1, inv1, _, _ = norm_terms(g1[...], params1[...], c, True)
    a, b, d = back_terms(h1[...], params1[...], c, mean1, inv1, True)
    mask = packed_mask(lane_sides[0], 256)
    for frame in range(2):
        low[frame, 0] = (mask * (e1[0, frame] * a + pre1[0, frame] * b + d)).astype(BF)


def fast_back_out(grad, low, from_prev, from_next, x, w, out, w_grad):
    i = pl.program_id(0)

    @pl.when(i == 0)
    def _():
        w_grad[...] = jnp.zeros_like(w_grad)

    around = (from_prev[0], low[0, 0], low[1, 0], from_next[0])
    for frame in range(2):
        before, here, after = around[frame], around[frame + 1], around[frame + 2]
        joined = jnp.concatenate([after, here, before], axis=1)
        for g in range(GROUPS):
            out[g, frame] = (grad[g, frame] + dot_nt(joined, w[g])).astype(BF)
            w_grad[g] += dot_tn(x[g, frame], joined)


def pack_kernel(x, out):
    half = x.shape[1] // 2
    for clip in range(x.shape[0]):
        out[clip] = jnp.concatenate([x[clip, :half], x[clip, half:]], axis=1)


def unpack_kernel(x, out):
    half = x.shape[1]
    width = x.shape[2] // 2
    for clip in range(x.shape[0]):
        out[clip, :half] = x[clip, :, :width]
        out[clip, half:] = x[clip, :, width:]


def gather_halves(x):
    devices, _, lanes = x.shape
    width = lanes // 2
    low, high = [], []
    for j in range(devices):
        part = x[j]
        low.append(part[:, :width])
        high.append(part[:, width:])
    return jnp.concatenate(low, axis=1), jnp.concatenate(high, axis=1)


def scatter_halves(low, high, out):
    devices, _, lanes = out.shape
    width = lanes // 2
    for j in range(devices):
        out[j] = jnp.concatenate(
            [low[:, j * width : (j + 1) * width], high[:, j * width : (j + 1) * width]], axis=1
        )


def slow_enter(x, w_time, w_project, own, narrow, project):
    i = pl.program_id(0)
    frames = narrow.shape[0] - 2

    @pl.when(i == 0)
    def _():
        narrow[...] = jnp.zeros_like(narrow)

    for half, frame in enumerate(gather_halves(x)):
        own[half, 0] = frame
        depth = frame.shape[1]
        project[half, 0] = dot(frame, w_project[:depth]).astype(BF)
        t = i + half * (frames // 2)
        for tap in range(3):
            narrow[t + 2 - tap] += dot(frame, w_time[tap, :depth])


def lateral_enter(side, fast, w, pre, stats, acc):
    frames = pre.shape[0]
    width = w.shape[1]
    mask = clip_mask(side[0], 256)
    for t in range(frames):
        taps = [k for k in range(5) if 0 <= 4 * t - 2 + k < 4 * frames]
        joined = jnp.concatenate([fast[4 * t - 2 + k] for k in taps], axis=1)
        v = dot(joined, w[taps[0] : taps[-1] + 1].reshape(len(taps) * width, w.shape[2]))
        pre[t] = v
        mv = mask * v
        add_stats(acc, t == 0, (0, 1), (col_sum(mv), col_sum(mv * v)))
    send_stats(True, acc, stats)


def narrow_enter(count, side, lateral, gl, params, base, w, act, pre, stats, acc):
    frames = pre.shape[0]
    _, _, scale, shift = norm_terms(gl[...], params[...], count[0, 0])
    mask = clip_mask(side[0], 256)
    for t in range(frames):
        act[t] = (mask * silu(lateral[t] * scale + shift)).astype(BF)
    width = act.shape[2]
    for t in range(frames):
        taps = [k for k in range(3) if 0 <= t - 1 + k < frames]
        joined = jnp.concatenate([act[t - 1 + k] for k in taps], axis=1)
        v = base[t + 1] + dot(joined, w[taps[0] * width : (taps[-1] + 1) * width, :])
        pre[t] = v
        mv = mask * v
        add_stats(acc, t == 0, (0, 1), (col_sum(mv), col_sum(mv * v)))
    send_stats(True, acc, stats)


def middle_enter(count, side, pre, gn, params, w, act, out, stats, acc, win):
    i = pl.program_id(0)
    _, _, scale, shift = norm_terms(gn[...], params[...], count[0, 0])
    mask = clip_mask(side[0], 256)
    a = mask * silu(pre[0] * scale + shift)
    act[0] = a.astype(BF)
    fill_windows(win, plane_windows(a, 16), 16)
    v = plane_dot(win, w, 256, 16)
    out[0] = v
    mv = mask * v
    add_stats(acc, i == 0, (0, 1), (col_sum(mv), col_sum(mv * v)))
    send_stats(i == pl.num_programs(0) - 1, acc, stats)


def wide_enter(count, side, pre, gm, params, base, lateral, w, w_project, act, project, acc):
    i = pl.program_id(0)
    _, _, scale, shift = norm_terms(gm[...], params[...], count[0, 0])
    mask = clip_mask(side[0], 256)
    a = (mask * silu(pre[0] * scale + shift)).astype(BF)
    act[0] = a
    v = dot(a, w[...])
    p = base[0].astype(F32) + dot(lateral[0], w_project[...])
    project[0] = p.astype(BF)
    mp = mask * p
    add_stats(
        acc, i == 0, (0, 1, 2, 3), (col_sum(v), col_sum(v * v), col_sum(mp), col_sum(mp * p))
    )


def wide_out(count, side, act, project, cot, g, params_w, params_p, w, result, grad, acc):
    i = pl.program_id(0)
    c = count[0, 0]
    gathered = g[...]
    mean_w, _, scale_w, shift_w = norm_terms(gathered[:, 0:2], params_w[...], c)
    mean_p, _, scale_p, shift_p = norm_terms(gathered[:, 2:4], params_p[...], c)
    mask = clip_mask(side[0], 256)
    shift = shift_w + shift_p
    halves = []
    sums = [None, None, None]
    for half, cot_half in enumerate(gather_halves(cot)):
        v = dot(act[half, 0], w[...])
        p = project[half, 0].astype(F32)
        u = v * scale_w + p * scale_p + shift
        gate = logistic(u)
        s = u * gate
        halves.append((mask * s).astype(BF))
        e = mask * cot_half.astype(F32) * (gate + s * (1.0 - gate))
        grad[half, 0] = e
        for k, value in enumerate((e, e * (v - mean_w), e * (p - mean_p))):
            value = col_sum(value)
            sums[k] = value if sums[k] is None else sums[k] + value
    scatter_halves(halves[0], halves[1], result)
    add_stats(acc, i == 0, (0, 1, 2), sums)


def middle_back(
    count, side, grad, act, g, h, params_w, w, pre, gm, params_m, out, w_grad, stats, acc, w_acc
):
    i = pl.program_id(0)
    c = count[0, 0]
    mean_w, inv_w, _, _ = norm_terms(g[...][:, 0:2], params_w[...], c)
    a, b, d = back_terms(h[...][:, 0:2], params_w[...], c, mean_w, inv_w)
    mean_m, _, scale_m, shift_m = norm_terms(gm[...], params_m[...], c)
    mask = clip_mask(side[0], 256)
    s = act[0]
    v = dot(s, w[...])
    low = (mask * (grad[0] * a + v * b + d)).astype(BF)
    p = pre[0]
    e = dot_nt(low, w[...]) * mask * silu_slope(p * scale_m + shift_m)
    out[0] = e
    add_stats(acc, i == 0, (0, 1), (col_sum(e), col_sum(e * (p - mean_m))))
    send_stats(i == pl.num_programs(0) - 1, acc, stats)

    @pl.when(i == 0)
    def _():
        w_acc[...] = jnp.zeros_like(w_acc)

    w_acc[...] += dot_tn(s, low)

    @pl.when(i == pl.num_programs(0) - 1)
    def _():
        put_columns(w_acc, w_grad)


def project_back(
    count, side, grad, project, g, h, params_p, own, lateral, w, joined, w_grad, w_acc
):
    i = pl.program_id(0)
    c = count[0, 0]
    mean_p, inv_p, _, _ = norm_terms(g[...][:, 2:4], params_p[...], c)
    rows = h[...]
    total = jnp.concatenate([rows[:, 0:1], rows[:, 2:3]], axis=1)
    a, b, d = back_terms(total, params_p[...], c, mean_p, inv_p)
    mask = clip_mask(side[0], 256)
    low = (mask * (grad[0] * a + project[0].astype(F32) * b + d)).astype(BF)
    joined[0] = dot_nt(low, w[...]).astype(BF)

    @pl.when(i == 0)
    def _():
        w_acc[...] = jnp.zeros_like(w_acc)

    width = own.shape[2]
    w_acc[0:width, :] += dot_tn(own[0], low)
    w_acc[width:, :] += dot_tn(lateral[0], low)

    @pl.when(i == pl.num_programs(0) - 1)
    def _():
        put_columns(w_acc, w_grad)


def narrow_back(
    count, side, grad, pre_m, gm, hm, params_m, w, pre_n, gn, params_n, low_out, out, stats, acc, win
):
    i = pl.program_id(0)
    c = count[0, 0]
    mean_m, inv_m, _, _ = norm_terms(gm[...], params_m[...], c)
    a, b, d = back_terms(hm[...], params_m[...], c, mean_m, inv_m)
    mean_n, _, scale_n, shift_n = norm_terms(gn[...], params_n[...], c)
    mask = clip_mask(side[0], 256)
    low = mask * (grad[0] * a + pre_m[0] * b + d)
    low_out[0] = low.astype(BF)
    fill_windows(win, plane_windows(low, 16), 16)
    p = pre_n[0]
    e = plane_dot(win, w, 256, 16) * mask * silu_slope(p * scale_n + shift_n)
    out[0] = e
    add_stats(acc, i == 0, (0, 1), (col_sum(e), col_sum(e * (p - mean_n))))
    send_stats(i == pl.num_programs(0) - 1, acc, stats)


def plane_weight(act, low, w_grad, w_acc, win):
    i = pl.program_id(0)

    @pl.when(i == 0)
    def _():
        w_acc[...] = jnp.zeros_like(w_acc)

    fill_windows(win, plane_windows(act[0].astype(F32), 16), 16)
    for tap in range(3):
        w_acc[tap] += dot_tn(win[16 * tap : 16 * tap + 256, :], low[0])

    @pl.when(i == pl.num_programs(0) - 1)
    def _():
        w_grad[...] = w_acc[...].astype(BF)


def join_back(
    count, side, grad, pre_n, gn, hn, params_n, w, joined, pre_l, gl, params_l, low, slow, out, stats, acc
):
    i = pl.program_id(0)
    steps = pl.num_programs(0)
    c = count[0, 0]
    frames = low.shape[0] - 2
    width = low.shape[2]
    mask = clip_mask(side[0], 256)

    @pl.when(i == 0)
    def _():
        mean_n, inv_n, _, _ = norm_terms(gn[...], params_n[...], c)
        a, b, d = back_terms(hn[...], params_n[...], c, mean_n, inv_n)
        low[0] = jnp.zeros((256, width), BF)
        low[frames + 1] = jnp.zeros((256, width), BF)
        for t in range(frames):
            low[t + 1] = (mask * (grad[t] * a + pre_n[t] * b + d)).astype(BF)

    mean_l, _, scale_l, shift_l = norm_terms(gl[...], params_l[...], c)
    halves = []
    sums = [None, None]
    for half in range(2):
        t = i + half * (frames // 2)
        j = joined[half, 0].astype(F32)
        for tap in range(3):
            j = j + dot_nt(low[t + 2 - tap], w[tap])
        slow_width = j.shape[1] - out.shape[3]
        halves.append(j[:, :slow_width].astype(BF))
        p = pre_l[half, 0]
        e = j[:, slow_width:] * mask * silu_slope(p * scale_l + shift_l)
        out[half, 0] = e
        for k, value in enumerate((e, e * (p - mean_l))):
            value = col_sum(value)
            sums[k] = value if sums[k] is None else sums[k] + value
    scatter_halves(halves[0], halves[1], slow)
    add_stats(acc, i == 0, (0, 1), sums)
    send_stats(i == steps - 1, acc, stats)


def lateral_back(count, side, grad, pre_l, gl, hl, params_l, w, low, out):
    c = count[0, 0]
    frames = grad.shape[0]
    mean_l, inv_l, _, _ = norm_terms(gl[...], params_l[...], c)
    a, b, d = back_terms(hl[...], params_l[...], c, mean_l, inv_l)
    mask = clip_mask(side[0], 256)
    for t in range(frames):
        low[t] = (mask * (grad[t] * a + pre_l[t] * b + d)).astype(BF)
    for t in range(frames):
        here = low[t]
        out[4 * t] = dot_nt(here, w[2]).astype(BF)
        out[4 * t + 1] = dot_nt(here, w[3]).astype(BF)
        third = dot_nt(here, w[4])
        if t + 1 < frames:
            after = low[t + 1]
            third = third + dot_nt(after, w[0])
            out[4 * t + 3] = dot_nt(after, w[1]).astype(BF)
        else:
            out[4 * t + 3] = jnp.zeros(out.shape[1:], BF)
        out[4 * t + 2] = third.astype(BF)


def lateral_weight_back(fast, low, w_grad, w_acc):
    frames = low.shape[0]
    width = fast.shape[2]
    w_acc[...] = jnp.zeros_like(w_acc)
    for t in range(frames):
        taps = [k for k in range(5) if 0 <= 4 * t - 2 + k < 4 * frames]
        joined = jnp.concatenate([fast[4 * t - 2 + k] for k in taps], axis=1)
        w_acc[taps[0] * width : (taps[-1] + 1) * width, :] += dot_tn(joined, low[t])
    w_grad[...] = w_acc[...].astype(BF)


def weight_merge(core, *refs):
    out = refs[-1]
    count = (len(refs) - 1) // 2
    rows = out.shape[0]
    for half in range(2):

        @pl.when(core[0] == half)
        def _(half=half):
            begin = 0
            for mine, other in zip(refs[:count], refs[count : 2 * count]):
                end = begin + mine.shape[0]
                low, high = max(begin, half * rows), min(end, (half + 1) * rows)
                if low < high:
                    part = slice(low - begin, high - begin)
                    total = mine[part, :].astype(F32) + other[part, :].astype(F32)
                    out[low - half * rows : high - half * rows, :] = total.astype(BF)
                begin = end


def weight_split(place, *refs):
    project, expand, spatial, time, lateral, full = refs[-6:]
    pieces = refs[:-6]
    near = 4
    rows = pieces[0].shape[0]
    for k, piece in enumerate(pieces):
        half = place[0] if k < near else 1 - place[0]
        if len(pieces) == near:
            half = 0
        spot = place[1] ^ (k % near)
        begin = pl.multiple_of((half * near + spot) * rows, 16)
        full[pl.ds(begin, rows), :] = piece[...]
    begin = 0
    for out in (project, expand):
        height, width = out.shape[0], full.shape[1]
        for block in range(out.shape[1] // width):
            out[:, block * width : (block + 1) * width] = full[begin : begin + height, :].astype(F32)
            begin += height
    spatial[...] = full[begin : begin + spatial.shape[0], :].astype(F32)
    begin += spatial.shape[0]
    height = project.shape[1]
    for tap in range(3):
        time[tap, :height] = full[begin : begin + height, :].astype(F32)
        begin += height
    rest = time.shape[1] - height
    for tap in range(3):
        time[tap, height:] = full[begin : begin + rest, :].astype(F32)
        begin += rest
    lateral[...] = full[begin : begin + lateral.shape[0], :].astype(F32)


def per_device(
    slow_in,
    fast_in,
    clip_side,
    fast_reduce,
    fast_spatial,
    fast_expand,
    lateral_weight,
    slow_reduce,
    slow_spatial,
    slow_expand,
    slow_project,
    fast_reduce_norm,
    fast_spatial_norm,
    fast_expand_norm,
    lateral_norm,
    slow_reduce_norm,
    slow_spatial_norm,
    slow_expand_norm,
    slow_project_norm,
    slow_cot,
    fast_cot,
):
    axes = ("dp", "wa")
    wa_count = lax.axis_size("wa")
    place = lax.axis_index("wa")
    devices = lax.axis_size("dp") * wa_count
    clips = fast_in.shape[0]
    cells = fast_in.shape[2] * fast_in.shape[3]
    frames = slow_in.shape[1]
    packs = clips // GROUPS
    c_f, b_f = fast_reduce.shape[1], fast_reduce.shape[2]
    c_l = lateral_weight.shape[2]
    b_s = slow_reduce.shape[2]
    c_s = slow_expand.shape[1]
    c_cat = slow_project.shape[0]
    half = frames // 2

    def exchange(array):
        return lax.all_to_all(array, "wa", 0, 0, tiled=True)

    def gather_stats(copies):
        return lax.all_to_all(copies, axes, 0, 0, tiled=True)

    def gather_wide(sums):
        dp_count = lax.axis_size("dp")
        if dp_count == 2:
            sums = sums + lax.ppermute(sums, "dp", [(0, 1), (1, 0)])
            copies = jnp.broadcast_to(sums[None], (wa_count,) + sums.shape)
            return lax.all_to_all(copies, "wa", 0, 0, tiled=True)
        return gather_stats(jnp.broadcast_to(sums[None], (devices,) + sums.shape))

    smem = scalars()

    area = jnp.sum(clip_side * clip_side)
    area_all = lax.psum(area, "dp").astype(F32)
    fast_count = (area_all * (fast_in.shape[1] * wa_count)).reshape(1, 1)
    slow_count = (area_all * frames).reshape(1, 1)
    own_side = lax.dynamic_slice_in_dim(clip_side, place, 1)
    lane_sides = jnp.repeat(clip_side.reshape(packs, GROUPS), LANES // GROUPS, axis=1)
    lane_sides = lane_sides.reshape(packs, 1, LANES)

    eye = jnp.eye(GROUPS, dtype=BF)
    w_first = jnp.einsum("kio,gh->kgiho", fast_reduce, eye).reshape(3, GROUPS, c_f, LANES)
    w_first_back = w_first.transpose(1, 2, 0, 3).reshape(GROUPS, c_f, 3 * LANES)
    w_plane = jnp.einsum("ijab,gh->ijgahb", fast_spatial, eye).reshape(3, 3 * LANES, LANES)
    flipped = fast_spatial[::-1, ::-1].transpose(0, 1, 3, 2)
    w_plane_back = jnp.einsum("ijab,gh->ijgahb", flipped, eye).reshape(3, 3 * LANES, LANES)
    w_widen = jnp.einsum("io,gh->ghio", fast_expand, eye).reshape(GROUPS, LANES, c_f)
    params1 = jnp.tile(fast_reduce_norm, (1, GROUPS))
    params2 = jnp.tile(fast_spatial_norm, (1, GROUPS))
    w_time_lateral = slow_reduce[:, c_s:].reshape(3 * c_l, b_s)
    w_middle = slow_spatial.reshape(3, 3 * b_s, b_s)
    w_middle_back = slow_spatial[::-1, ::-1].transpose(0, 1, 3, 2).reshape(3, 3 * b_s, b_s)

    def pack(array):
        rows = frames * cells
        width = array.shape[4]
        flat = array.reshape(clips, rows, width)
        return launch(
            pack_kernel,
            "pack",
            (packs,),
            [(flat, pl.BlockSpec((GROUPS, rows, width), lambda i: (i, 0, 0)))],
            [((clips, rows // 2, 2 * width), BF, pl.BlockSpec((GROUPS, rows // 2, 2 * width), lambda i: (i, 0, 0)))],
        )[0]

    def unpack(array, shape):
        rows = frames * cells
        width = shape[4]
        return launch(
            unpack_kernel,
            "unpack",
            (packs,),
            [(array, pl.BlockSpec((GROUPS, rows // 2, 2 * width), lambda i: (i, 0, 0)))],
            [((clips, rows, width), BF, pl.BlockSpec((GROUPS, rows, width), lambda i: (i, 0, 0)))],
        )[0].reshape(shape)

    slow_got = exchange(pack(slow_in))
    cot_got = exchange(pack(slow_cot))

    x = fast_in.reshape(clips, 2, cells, c_f)
    x_spec = pl.BlockSpec((GROUPS, 2, cells, c_f), lambda i: (i, 0, 0, 0))
    packed_shape = (packs, 2, cells, LANES)
    packed_spec = pl.BlockSpec((1, 2, cells, LANES), lambda i: (i, 0, 0, 0))
    rim_shape = (packs, cells, LANES)
    rim_spec = pl.BlockSpec((1, cells, LANES), lambda i: (i, 0, 0))
    sides_spec = pl.BlockSpec((1, 1, LANES), lambda i: (i, 0, 0))
    stat8 = ((devices, 8, LANES), F32, pl.BlockSpec((devices, 8, LANES), lambda *_: (0, 0, 0)))
    acc8 = pltpu.VMEM((8, LANES), F32)
    fast_win = pltpu.VMEM((cells + 32, 3 * LANES), BF)

    y, to_next, to_prev = launch(
        fast_first,
        "fast_first",
        (packs,),
        [(x, x_spec), (w_first, whole(w_first))],
        [(packed_shape, F32, packed_spec), (rim_shape, BF, rim_spec), (rim_shape, BF, rim_spec)],
    )
    forward = [(i, i + 1) for i in range(wa_count - 1)]
    backward = [(i + 1, i) for i in range(wa_count - 1)]
    from_prev = lax.ppermute(to_next, "wa", forward)
    from_next = lax.ppermute(to_prev, "wa", backward)
    pre1, s1 = launch(
        fast_join,
        "fast_join",
        (packs,),
        [(y, packed_spec), (from_prev, rim_spec), (from_next, rim_spec), (lane_sides, sides_spec)],
        [(packed_shape, F32, packed_spec), stat8],
        [acc8],
        after=(slow_got,),
    )
    g1 = gather_stats(s1)
    act1, pre2, s2 = launch(
        fast_plane,
        "fast_plane",
        (packs,),
        [
            (fast_count, smem),
            (pre1, packed_spec),
            (g1, whole(g1)),
            (params1, whole(params1)),
            (lane_sides, sides_spec),
            (w_plane, whole(w_plane)),
        ],
        [(packed_shape, BF, packed_spec), (packed_shape, F32, packed_spec), stat8],
        [acc8, fast_win],
    )
    g2 = gather_stats(s2)
    act2, s3 = launch(
        fast_widen,
        "fast_widen",
        (packs,),
        [
            (fast_count, smem),
            (pre2, packed_spec),
            (g2, whole(g2)),
            (params2, whole(params2)),
            (lane_sides, sides_spec),
            (w_widen, whole(w_widen)),
        ],
        [(packed_shape, BF, packed_spec), stat8],
        [acc8],
    )
    g3 = gather_stats(s3)
    (fast_result,) = launch(
        fast_out,
        "fast_out",
        (packs,),
        [
            (fast_count, smem),
            (clip_side, smem),
            (x, x_spec),
            (act2, packed_spec),
            (g3, whole(g3)),
            (fast_expand_norm, whole(fast_expand_norm)),
            (w_widen, whole(w_widen)),
        ],
        [(x.shape, BF, x_spec)],
    )

    fast_got = exchange(fast_result.reshape(clips, 2 * cells, c_f)).reshape(4 * frames, cells, c_f)

    def stat(rows, width):
        return ((devices, rows, width), F32, pl.BlockSpec((devices, rows, width), lambda *_: (0, 0, 0)))

    pre_l, s_l = launch(
        lateral_enter,
        "lateral_enter",
        (),
        [(own_side, smem), (fast_got, whole(fast_got)), (lateral_weight, whole(lateral_weight))],
        [
            ((frames, cells, c_l), F32, pl.BlockSpec((frames, cells, c_l), lambda *_: (0, 0, 0))),
            stat(2, c_l),
        ],
        [pltpu.VMEM((2, c_l), F32)],
    )
    g_l = gather_stats(s_l)

    got_spec = pl.BlockSpec((wa_count, cells, LANES), lambda i: (0, i, 0))

    def pair_spec(width):
        return pl.BlockSpec((2, 1, cells, width), lambda i: (0, i, 0, 0))

    def frame_spec(width):
        return pl.BlockSpec((1, cells, width), lambda i: (i, 0, 0))

    def pairs(array):
        return array.reshape((2, half) + array.shape[1:])

    own, base_n, base_p = launch(
        slow_enter,
        "slow_enter",
        (half,),
        [(slow_got, got_spec), (slow_reduce, whole(slow_reduce)), (slow_project, whole(slow_project))],
        [
            ((2, half, cells, c_s), BF, pair_spec(c_s)),
            (
                (frames + 2, cells, b_s),
                F32,
                pl.BlockSpec((frames + 2, cells, b_s), lambda *_: (0, 0, 0)),
            ),
            ((2, half, cells, c_s), BF, pair_spec(c_s)),
        ],
        flops=2 * frames * cells * c_s * (3 * b_s + c_s),
    )
    own = own.reshape(frames, cells, c_s)
    base_p = base_p.reshape(frames, cells, c_s)
    lateral_act, pre_n, s_n = launch(
        narrow_enter,
        "narrow_enter",
        (),
        [
            (slow_count, smem),
            (own_side, smem),
            (pre_l, whole(pre_l)),
            (g_l, whole(g_l)),
            (lateral_norm, whole(lateral_norm)),
            (base_n, whole(base_n)),
            (w_time_lateral, whole(w_time_lateral)),
        ],
        [
            ((frames, cells, c_l), BF, pl.BlockSpec((frames, cells, c_l), lambda *_: (0, 0, 0))),
            ((frames, cells, b_s), F32, pl.BlockSpec((frames, cells, b_s), lambda *_: (0, 0, 0))),
            stat(2, b_s),
        ],
        [pltpu.VMEM((2, b_s), F32)],
    )
    g_n = gather_stats(s_n)
    slow_win = pltpu.VMEM((cells + 32, 3 * b_s), BF)
    act_n, pre_m, s_m = launch(
        middle_enter,
        "middle_enter",
        (frames,),
        [
            (slow_count, smem),
            (own_side, smem),
            (pre_n, frame_spec(b_s)),
            (g_n, whole(g_n)),
            (slow_reduce_norm, whole(slow_reduce_norm)),
            (w_middle, whole(w_middle)),
        ],
        [
            ((frames, cells, b_s), BF, frame_spec(b_s)),
            ((frames, cells, b_s), F32, frame_spec(b_s)),
            stat(2, b_s),
        ],
        [pltpu.VMEM((2, b_s), F32), slow_win],
    )
    g_m = gather_stats(s_m)
    act_m, project, s_w = launch(
        wide_enter,
        "wide_enter",
        (frames,),
        [
            (slow_count, smem),
            (own_side, smem),
            (pre_m, frame_spec(b_s)),
            (g_m, whole(g_m)),
            (slow_spatial_norm, whole(slow_spatial_norm)),
            (base_p, frame_spec(c_s)),
            (lateral_act, frame_spec(c_l)),
            (slow_expand, whole(slow_expand)),
            (slow_project, pl.BlockSpec((c_l, c_s), lambda i: (c_s // c_l, 0))),
        ],
        [
            ((frames, cells, b_s), BF, frame_spec(b_s)),
            ((frames, cells, c_s), BF, frame_spec(c_s)),
            ((4, c_s), F32, pl.BlockSpec((4, c_s), lambda *_: (0, 0))),
        ],
    )
    g_w = gather_wide(s_w)
    out_packed, wide_grad, t_w = launch(
        wide_out,
        "wide_out",
        (half,),
        [
            (slow_count, smem),
            (own_side, smem),
            (pairs(act_m), pair_spec(b_s)),
            (pairs(project), pair_spec(c_s)),
            (cot_got, got_spec),
            (g_w, whole(g_w)),
            (slow_expand_norm, whole(slow_expand_norm)),
            (slow_project_norm, whole(slow_project_norm)),
            (slow_expand, whole(slow_expand)),
        ],
        [
            ((wa_count, half * cells, LANES), BF, got_spec),
            ((2, half, cells, c_s), F32, pair_spec(c_s)),
            ((4, c_s), F32, pl.BlockSpec((4, c_s), lambda *_: (0, 0))),
        ],
    )
    wide_grad = wide_grad.reshape(frames, cells, c_s)
    h_w = gather_wide(t_w)
    result_got = exchange(out_packed)
    slow_result = unpack(result_got, slow_in.shape)

    middle_grad, expand_w_grad, t_m = launch(
        middle_back,
        "middle_back",
        (frames,),
        [
            (slow_count, smem),
            (own_side, smem),
            (wide_grad, frame_spec(c_s)),
            (act_m, frame_spec(b_s)),
            (g_w, whole(g_w)),
            (h_w, whole(h_w)),
            (slow_expand_norm, whole(slow_expand_norm)),
            (slow_expand, whole(slow_expand)),
            (pre_m, frame_spec(b_s)),
            (g_m, whole(g_m)),
            (slow_spatial_norm, whole(slow_spatial_norm)),
        ],
        [
            ((frames, cells, b_s), F32, frame_spec(b_s)),
            ((c_s, b_s), BF, pl.BlockSpec((c_s, b_s), lambda *_: (0, 0))),
            stat(2, b_s),
        ],
        [pltpu.VMEM((2, b_s), F32), pltpu.VMEM((b_s, c_s), F32)],
    )
    h_m = gather_stats(t_m)
    joined_part, project_w_grad = launch(
        project_back,
        "project_back",
        (frames,),
        [
            (slow_count, smem),
            (own_side, smem),
            (wide_grad, frame_spec(c_s)),
            (project, frame_spec(c_s)),
            (g_w, whole(g_w)),
            (h_w, whole(h_w)),
            (slow_project_norm, whole(slow_project_norm)),
            (own, frame_spec(c_s)),
            (lateral_act, frame_spec(c_l)),
            (slow_project, whole(slow_project)),
        ],
        [
            ((frames, cells, c_cat), BF, frame_spec(c_cat)),
            ((c_cat * c_s // b_s, b_s), BF, pl.BlockSpec((c_cat * c_s // b_s, b_s), lambda *_: (0, 0))),
        ],
        [pltpu.VMEM((c_cat, c_s), F32)],
        flops=4 * frames * cells * c_cat * c_s,
    )
    middle_low, narrow_grad, t_n = launch(
        narrow_back,
        "narrow_back",
        (frames,),
        [
            (slow_count, smem),
            (own_side, smem),
            (middle_grad, frame_spec(b_s)),
            (pre_m, frame_spec(b_s)),
            (g_m, whole(g_m)),
            (h_m, whole(h_m)),
            (slow_spatial_norm, whole(slow_spatial_norm)),
            (w_middle_back, whole(w_middle_back)),
            (pre_n, frame_spec(b_s)),
            (g_n, whole(g_n)),
            (slow_reduce_norm, whole(slow_reduce_norm)),
        ],
        [
            ((frames, cells, b_s), BF, frame_spec(b_s)),
            ((frames, cells, b_s), F32, frame_spec(b_s)),
            stat(2, b_s),
        ],
        [pltpu.VMEM((2, b_s), F32), slow_win],
    )
    h_n = gather_stats(t_n)
    (spatial_w_grad,) = launch(
        plane_weight,
        "plane_weight",
        (frames,),
        [(act_n, frame_spec(b_s)), (middle_low, frame_spec(b_s))],
        [((3, 3 * b_s, b_s), BF, pl.BlockSpec((3, 3 * b_s, b_s), lambda *_: (0, 0, 0)))],
        [pltpu.VMEM((3, 3 * b_s, b_s), F32), slow_win],
        flops=18 * frames * cells * b_s * b_s,
    )
    narrow_low, grad_packed, lateral_grad, t_l = launch(
        join_back,
        "join_back",
        (half,),
        [
            (slow_count, smem),
            (own_side, smem),
            (narrow_grad, whole(narrow_grad)),
            (pre_n, whole(pre_n)),
            (g_n, whole(g_n)),
            (h_n, whole(h_n)),
            (slow_reduce_norm, whole(slow_reduce_norm)),
            (slow_reduce, whole(slow_reduce)),
            (pairs(joined_part), pair_spec(c_cat)),
            (pairs(pre_l), pair_spec(c_l)),
            (g_l, whole(g_l)),
            (lateral_norm, whole(lateral_norm)),
        ],
        [
            (
                (frames + 2, cells, b_s),
                BF,
                pl.BlockSpec((frames + 2, cells, b_s), lambda *_: (0, 0, 0)),
            ),
            ((wa_count, half * cells, LANES), BF, got_spec),
            ((2, half, cells, c_l), F32, pair_spec(c_l)),
            stat(2, c_l),
        ],
        [pltpu.VMEM((2, c_l), F32)],
        after=(result_got,),
    )
    lateral_grad = lateral_grad.reshape(frames, cells, c_l)
    h_l = gather_stats(t_l)
    grad_got = exchange(grad_packed)
    slow_grad = unpack(grad_got, slow_in.shape)

    def time_weight(values):
        flat = values.reshape(frames * cells, values.shape[2])
        low = narrow_low.reshape((frames + 2) * cells, b_s)
        parts = []
        for tap in range(3):
            begin = (2 - tap) * cells
            parts.append(
                lax.dot_general(
                    flat,
                    lax.slice_in_dim(low, begin, begin + frames * cells, 1, 0),
                    (((0,), (0,)), ((), ())),
                    preferred_element_type=F32,
                )
            )
        return jnp.stack(parts).astype(BF)

    lateral_low, frames_back = launch(
        lateral_back,
        "lateral_back",
        (),
        [
            (slow_count, smem),
            (own_side, smem),
            (lateral_grad, whole(lateral_grad)),
            (pre_l, whole(pre_l)),
            (g_l, whole(g_l)),
            (h_l, whole(h_l)),
            (lateral_norm, whole(lateral_norm)),
            (lateral_weight, whole(lateral_weight)),
        ],
        [
            ((frames, cells, c_l), BF, pl.BlockSpec((frames, cells, c_l), lambda *_: (0, 0, 0))),
            ((4 * frames, cells, c_f), BF, pl.BlockSpec((4 * frames, cells, c_f), lambda *_: (0, 0, 0))),
        ],
    )
    back_got = exchange(frames_back.reshape(wa_count, 2 * cells, c_f)).reshape(x.shape)
    (lateral_w_grad,) = launch(
        lateral_weight_back,
        "lateral_weight_back",
        (),
        [(fast_got, whole(fast_got)), (lateral_low, whole(lateral_low))],
        [((5 * c_f, c_l), BF, pl.BlockSpec((5 * c_f, c_l), lambda *_: (0, 0)))],
        [pltpu.VMEM((5 * c_f, c_l), F32)],
    )

    weight_parts = [
        part.reshape(-1, b_s)
        for part in (
            project_w_grad,
            expand_w_grad,
            spatial_w_grad,
            time_weight(own),
            time_weight(lateral_act),
            lateral_w_grad,
        )
    ]
    sizes = [part.shape[0] for part in weight_parts]
    near = 4
    inner = [[near * k + j for j in range(near)] for k in range(wa_count // near)]
    outer = [[near * k + j for k in range(wa_count // near)] for j in range(near)]
    dp_count = lax.axis_size("dp")
    core = lax.axis_index("dp")
    swap = [(0, 1), (1, 0)]
    paired = dp_count == 2
    if paired:
        others = [lax.ppermute(part, "dp", swap) for part in weight_parts]
        rows = sum(sizes) // 2
        place_core = core.reshape(1)
        (weights,) = launch(
            weight_merge,
            "weight_merge",
            (),
            [(place_core, smem)] + [(part, whole(part)) for part in weight_parts + others],
            [((rows, b_s), BF, pl.BlockSpec((rows, b_s), lambda *_: (0, 0)))],
        )
    else:
        weights = jnp.concatenate(weight_parts, axis=0)
    first_stage = lax.psum_scatter(weights, "wa", axis_index_groups=inner, tiled=True)
    second_stage = lax.psum(first_stage, "wa", axis_index_groups=outer)

    cot = fast_cot.reshape(x.shape)
    fast_grad3, t3 = launch(
        fast_back_sum,
        "fast_back_sum",
        (packs,),
        [
            (fast_count, smem),
            (clip_side, smem),
            (cot, x_spec),
            (back_got, x_spec),
            (x, x_spec),
            (act2, packed_spec),
            (g3, whole(g3)),
            (fast_expand_norm, whole(fast_expand_norm)),
            (w_widen, whole(w_widen)),
        ],
        [(x.shape, F32, x_spec), stat8],
        [acc8],
        after=(first_stage,),
    )
    h3 = gather_stats(t3)
    fast_grad2, widen_blocks, t2 = launch(
        fast_back_widen,
        "fast_back_widen",
        (packs,),
        [
            (fast_count, smem),
            (clip_side, smem),
            (fast_grad3, x_spec),
            (act2, packed_spec),
            (g3, whole(g3)),
            (h3, whole(h3)),
            (fast_expand_norm, whole(fast_expand_norm)),
            (w_widen, whole(w_widen)),
            (pre2, packed_spec),
            (g2, whole(g2)),
            (params2, whole(params2)),
            (lane_sides, sides_spec),
        ],
        [
            (packed_shape, F32, packed_spec),
            ((GROUPS, LANES, c_f), F32, pl.BlockSpec((GROUPS, LANES, c_f), lambda *_: (0, 0, 0))),
            stat8,
        ],
        [acc8],
    )
    h2 = gather_stats(t2)
    fast_grad1, plane_blocks, t1 = launch(
        fast_back_plane,
        "fast_back_plane",
        (packs,),
        [
            (fast_count, smem),
            (fast_grad2, packed_spec),
            (pre2, packed_spec),
            (g2, whole(g2)),
            (h2, whole(h2)),
            (params2, whole(params2)),
            (act1, packed_spec),
            (pre1, packed_spec),
            (g1, whole(g1)),
            (params1, whole(params1)),
            (lane_sides, sides_spec),
            (w_plane_back, whole(w_plane_back)),
        ],
        [
            (packed_shape, F32, packed_spec),
            (
                (3, 3 * LANES, LANES),
                F32,
                pl.BlockSpec((3, 3 * LANES, LANES), lambda *_: (0, 0, 0)),
            ),
            stat8,
        ],
        [acc8, fast_win],
    )
    h1 = gather_stats(t1)
    (low1,) = launch(
        fast_back_first,
        "fast_back_first",
        (packs,),
        [
            (fast_count, smem),
            (fast_grad1, packed_spec),
            (pre1, packed_spec),
            (g1, whole(g1)),
            (h1, whole(h1)),
            (params1, whole(params1)),
            (lane_sides, sides_spec),
        ],
        [((2, packs, cells, LANES), BF, pl.BlockSpec((2, 1, cells, LANES), lambda i: (0, i, 0, 0)))],
    )
    low_prev = lax.ppermute(low1[1], "wa", forward)
    low_next = lax.ppermute(low1[0], "wa", backward)
    fast_grad, first_blocks, second_stage = launch(
        fast_back_out,
        "fast_back_out",
        (packs,),
        [
            (fast_grad3, x_spec),
            (low1, pl.BlockSpec((2, 1, cells, LANES), lambda i: (0, i, 0, 0))),
            (low_prev, rim_spec),
            (low_next, rim_spec),
            (x, x_spec),
            (w_first_back, whole(w_first_back)),
        ],
        [
            (x.shape, BF, x_spec),
            (
                (GROUPS, c_f, 3 * LANES),
                F32,
                pl.BlockSpec((GROUPS, c_f, 3 * LANES), lambda *_: (0, 0, 0)),
            ),
        ],
        after=(grad_got,),
        carry=(second_stage,),
    )
    pieces = [second_stage] + [
        lax.ppermute(second_stage, "wa", [(i, i ^ step) for i in range(wa_count)])
        for step in range(1, near)
    ]
    if paired:
        pieces = pieces + [lax.ppermute(piece, "dp", swap) for piece in pieces]
    else:
        pieces = [lax.psum(piece, "dp") for piece in pieces]

    final = [
        ((c_cat, c_s), F32),
        ((b_s, c_s), F32),
        ((9 * b_s, b_s), F32),
        ((3, c_cat, b_s), F32),
        ((5 * c_f, c_l), F32),
    ]
    project_all, expand_all, spatial_all, time_all, lateral_all = launch(
        weight_split,
        "weight_split",
        (),
        [(jnp.stack([core, place % near]), smem)] + [(piece, whole(piece)) for piece in pieces],
        [
            (shape, dtype, pl.BlockSpec(shape, lambda *_, rank=len(shape): (0,) * rank))
            for shape, dtype in final
        ],
        [pltpu.VMEM((sum(sizes), b_s), BF)],
    )
    expand_part = sum(widen_blocks[g, g * b_f : (g + 1) * b_f] for g in range(GROUPS))
    plane_view = plane_blocks.reshape(3, 3, GROUPS, b_f, GROUPS, b_f)
    spatial_part = sum(plane_view[:, :, g, :, g] for g in range(GROUPS))
    first_view = first_blocks.reshape(GROUPS, c_f, 3, GROUPS, b_f)
    reduce_part = sum(first_view[g, :, :, g] for g in range(GROUPS)).transpose(1, 0, 2)

    small = jnp.concatenate(
        [reduce_part.reshape(-1), spatial_part.reshape(-1), expand_part.reshape(-1)]
    )
    share = -(-small.shape[0] // (devices * LANES)) * LANES
    padded = jnp.pad(small, (0, share * devices - small.shape[0])).reshape(devices, share // LANES, LANES)
    mine = jnp.sum(gather_stats(padded), axis=0)
    small_all = gather_stats(jnp.broadcast_to(mine[None], padded.shape)).reshape(-1)
    first_size, plane_size = reduce_part.size, spatial_part.size
    fast_reduce_grad = small_all[:first_size].reshape(fast_reduce.shape)
    fast_spatial_grad = small_all[first_size : first_size + plane_size].reshape(fast_spatial.shape)
    fast_expand_grad = small_all[first_size + plane_size : small.shape[0]].reshape(fast_expand.shape)

    def norm_grad(sums, moments, count, folded=False):
        total, moment = jnp.sum(sums, axis=0), jnp.sum(moments, axis=0)
        if folded:
            total = total.reshape(total.shape[0], GROUPS, -1).sum(axis=1)
            moment = moment.reshape(moment.shape[0], GROUPS, -1).sum(axis=1)
        mean = moment[0] / count[0, 0]
        inv = lax.rsqrt(moment[1] / count[0, 0] - mean * mean + EPSILON)
        return jnp.stack([total[1] * inv, total[0]])

    h_project = jnp.concatenate([h_w[:, 0:1], h_w[:, 2:3]], axis=1)
    return (
        slow_result,
        fast_result.reshape(fast_in.shape),
        slow_grad,
        fast_grad.reshape(fast_in.shape),
        fast_reduce_grad,
        fast_spatial_grad,
        fast_expand_grad,
        lateral_all.reshape(lateral_weight.shape),
        time_all,
        spatial_all.reshape(slow_spatial.shape),
        expand_all,
        project_all,
        norm_grad(h1, g1, fast_count, True),
        norm_grad(h2, g2, fast_count, True),
        norm_grad(h3, g3, fast_count),
        norm_grad(h_l, g_l, slow_count),
        norm_grad(h_n, g_n, slow_count),
        norm_grad(h_m, g_m, slow_count),
        norm_grad(h_w[:, 0:2], g_w[:, 0:2], slow_count),
        norm_grad(h_project, g_w[:, 2:4], slow_count),
    )


def solution(mesh):
    wide = P("dp", None, None, None, "wa")
    fast = P("dp", "wa", None, None, None)
    same = P()
    return jax.shard_map(
        per_device,
        mesh=mesh,
        in_specs=(wide, fast, P("dp")) + (same,) * 16 + (wide, fast),
        out_specs=(wide, fast, wide, fast) + (same,) * 16,
        check_vma=False,
    )
```

time: 2310 us -> 990 us (0.43)
  local copies, waits for them, and re-layouts: 501 us -> 35 us
  blocking collectives: 583 us -> 154 us
  waiting for transfers between devices: 694 us -> 404 us
  matrix products: 283 us -> 6.66 us
  Pallas kernels: 0 us -> 221 us
  other arithmetic: 117 us -> 12.1 us
  starting transfers between devices: 103 us -> 130 us
    psum x14 -> x1, blocking collectives: 583 us -> 2.45 us  [per_device(): area_all = lax.psum(area, 'dp').astype(F32)]
    psum x2 -> x1, waiting for transfers between devices: 326 us -> 0.02 us  [per_device(): second_stage = lax.psum(first_stage, 'wa', axis_index_groups=outer)]
    dot_general x86 -> x6, matrix products: 283 us -> 6.66 us  [time_weight(): lax.dot_general(flat, lax.slice_in_dim(low, begin, begin + frames * cells...]
    pallas_call x0 -> x29, Pallas kernels: none -> 221 us  [launch(): pl.pallas_call(kernel, name=name, grid=grid, in_specs=[spec for _, spec i...]
    unnamed x296 -> x119, local copies, waits for them, and re-layouts: 225 us -> 18.1 us
    all_to_all x4 -> x14, waiting for transfers between devices: 185 us -> 351 us  [the longest x5 308 us: exchange(): return lax.all_to_all(array, 'wa', 0, 0, tiled=True)]
    all_to_all x0 -> x8, blocking collectives: none -> 151 us  [the longest x5 55 us: gather_stats(): return lax.all_to_all(copies, axes, 0, 0, tiled=True)]
    reduce_scatter x1, waiting for transfers between devices: 118 us -> 9.4 us  [per_device(): lax.psum_scatter(weights, 'wa', axis_index_groups=inner, tiled=True)]
  transfers between devices with their start and end apart: 12 -> 35, of which waited for: 10 -> 22; matrix products, arithmetic and copies ran while one was open for 22% -> 4% of each run, Pallas kernels for 0% -> 10%
where the time goes in v1:
time: 990 us; the launch traced here: 978 us
  waiting for transfers between devices  404 us (41%)
  Pallas kernels  221 us (22%)
  blocking collectives  154 us (16%)
  starting transfers between devices  130 us (13%)
  local copies, waits for them, and re-layouts  35 us (4%)
  between operations  16.1 us (2%)
  other arithmetic  12.1 us (1%)
    all_to_all x5, waiting for transfers between devices, exchange(): return lax.all_to_all(array, 'wa', 0, 0, tiled=True)  308 us
    pallas_call x29, Pallas kernels, launch(): pl.pallas_call(kernel, name=name, grid=grid, in_specs=[spec for _, spec i...  221 us
    all_to_all x9, starting transfers between devices, gather_stats(): return lax.all_to_all(copies, axes, 0, 0, tiled=True)  80.5 us
    all_to_all x5, blocking collectives, gather_stats(): return lax.all_to_all(copies, axes, 0, 0, tiled=True)  55 us
    all_to_all x1, blocking collectives, exchange(): return lax.all_to_all(array, 'wa', 0, 0, tiled=True)  53.6 us
    all_to_all x9, waiting for transfers between devices, gather_stats(): return lax.all_to_all(copies, axes, 0, 0, tiled=True)  42.8 us
    all_to_all x2, blocking collectives, gather_wide(): return lax.all_to_all(copies, 'wa', 0, 0, tiled=True)  42.6 us
    all_to_all x5, starting transfers between devices, exchange(): return lax.all_to_all(array, 'wa', 0, 0, tiled=True)  29.1 us
  transfers between devices with their start and end apart: 35, of which 22 were waited for; matrix products, arithmetic and copies ran while one was open for 4% of the time, Pallas kernels for 10%

profile of v1, /device:TPU:0, one launch (start us, length us, event | category | flops | bytes accessed | tf_op | source)
XLA Modules:
  0.0 978.2 jit_solution(10266298217436876893)
XLA Ops:
  7.2 6.3 pack.2
  13.5 8.5 all-to-all-start
  22.9 3.8 fast_first.1
  27.7 3.8 collective-permute-start
  36.9 3.4 collective-permute-done.refs_1_
  40.3 9.5 collective-permute-done.1.refs_2_
  49.8 52.7 %all-to-all-done.refs_4_.refs_0_ = bf16[16,1024,128]{2,1,0:T(8,128)(2,1)} async-done(((bf16[16,1024,128]{2,1,0:T(8,128)(2,1)}), bf16[16,1024,128]{2,1,0:T(8,128)(2,1)}, u32[]{:S(2)}, u32[]{:S(2)}) %all-to-all-start) | async-done | bytes 4194336 | tf_op jit(solution)/shard_map/all_to_all | solution.py:744
  102.5 2.9 fast_join.1
  106.3 25.4 %all-to-all-start.1 = ((f32[32,8,128]{2,1,0:T(8,128)}), f32[32,8,128]{2,1,0:T(8,128)S(1)}, u32[]{:S(2)}, u32[]{:S(2)}) async-start(f32[32,8,128]{2,1,0:T(8,128)} %get-tuple-element.81), calls=%async_computation.1 | async-start | bytes 262144 | tf_op jit(solution)/shard_map/all_to_all | solution.py:747
  134.4 5.2 all-to-all-done.1.refs_2_.refs_8_.refs_3_
  139.6 4.7 fast_plane.1
  147.9 7.7 all-to-all-done.2.refs_2_.refs_9_.refs_3_
  158.7 9.8 %all_to_all.110.refs_4_.refs_6_ = f32[32,8,128]{2,1,0:T(8,128)S(1)} all-to-all(f32[32,8,128]{2,1,0:T(8,128)S(1)} %get-tuple-element.85), channel_id=1, replica_groups=mesh['dp'=2,'wa'=16] {'dp','wa'}, dimensions={0} | all-to-all | bytes 262144 | tf_op jit(solution)/shard_map/all_to_all | solution.py:747
  168.5 4.9 fast_out.1
  173.4 4.6 all-to-all-start.4
  178.6 42.6 %all-to-all-done.4 = bf16[16,512,128]{2,1,0:T(8,128)(2,1)} async-done(((bf16[16,512,128]{2,1,0:T(8,128)(2,1)}), bf16[16,512,128]{2,1,0:T(8,128)(2,1)}, u32[]{:S(2)}, u32[]{:S(2)}) %all-to-all-start.4) | async-done | bytes 2097184 | tf_op jit(solution)/shard_map/all_to_all | solution.py:744
  222.2 4.5 lateral_enter.1
  226.7 9.2 all-to-all-start.5
  236.0 13.2 %slow_enter.1 = (bf16[2,4,256,1024]{3,2,1,0:T(8,128)(2,1)}, f32[10,256,256]{2,1,0:T(8,128)}, bf16[2,4,256,1024]{3,2,1,0:T(8,128)(2,1)}) custom-call(bf16[16,1024,128]{2,1,0:T(8,128)(2,1)} %all-to-all-done.refs_4_.refs_0_, bf16[3,1280,256]{2,1,0:T(8,128)(2,1)S(1)} %copy-done.10, bf16[1280,1024]{1,0:T(8,128)(2,1)} %refs_9_.1), custom_call_target="tpu_custom_call" | custom-call | flops 7516192768 | bytes 19791872 | tf_op jit(solution)/shard_map/slow_enter/pallas_call | solution.py:45
  249.2 5.6 narrow_enter.1
  255.8 13.0 %all_to_all.111.refs_3_.refs_9_.refs_4_ = f32[32,2,256]{2,1,0:T(2,128)S(1)} all-to-all(f32[32,2,256]{2,1,0:T(2,128)S(1)} %get-tuple-element.90), channel_id=1, replica_groups=mesh['dp'=2,'wa'=16] {'dp','wa'}, dimensions={0} | all-to-all | bytes 131072 | tf_op jit(solution)/shard_map/all_to_all | solution.py:747
  268.8 9.1 middle_enter.1
  281.4 6.3 pack.3
  288.7 6.5 all-to-all-start.8
  295.3 10.4 %wide_enter.1 = (bf16[8,256,256]{2,1,0:T(8,128)(2,1)S(1)}, bf16[8,256,1024]{2,1,0:T(8,128)(2,1)}, f32[4,1024]{1,0:T(4,128)S(1)}) custom-call(f32[1,1]{1,0:T(1,128)} %bitcast.refs_0_, s32[1]{0:T(128)} %dynamic_slice.3.refs_0_.refs_1_, f32[8,256,256]{2,1,0:T(8,128)} %get-tuple-element.91.refs_2_.refs_8_.refs_3_, ...), custom_call_target="tpu_custom_call" | custom-call | bytes 15812616 | tf_op jit(solution)/shard_map/wide_enter/pallas_call | solution.py:45
  306.9 68.7 %all-to-all-done.8.refs_4_ = bf16[16,1024,128]{2,1,0:T(8,128)(2,1)} async-done(((bf16[16,1024,128]{2,1,0:T(8,128)(2,1)}), bf16[16,1024,128]{2,1,0:T(8,128)(2,1)}, u32[]{:S(2)}, u32[]{:S(2)}) %all-to-all-start.8) | async-done | bytes 4194336 | tf_op jit(solution)/shard_map/all_to_all | solution.py:744
  375.6 29.0 %all_to_all.112.refs_5_.refs_4_ = f32[16,4,1024]{2,1,0:T(4,128)S(1)} all-to-all(f32[16,4,1024]{2,1,0:T(4,128)S(1)} %broadcast_in_dim.9), channel_id=1, replica_groups=mesh['dp'=2,'wa'=16] {'wa'}, dimensions={0} | all-to-all | bytes 524288 | tf_op jit(solution)/shard_map/all_to_all | solution.py:754
  404.6 13.6 %wide_out.1 = (bf16[16,1024,128]{2,1,0:T(8,128)(2,1)}, f32[2,4,256,1024]{3,2,1,0:T(8,128)}, f32[4,1024]{1,0:T(4,128)S(1)}) custom-call(f32[1,1]{1,0:T(1,128)} %bitcast.refs_0_, s32[1]{0:T(128)} %dynamic_slice.3.refs_0_.refs_1_, bf16[2,4,256,256]{3,2,1,0:T(8,128)(2,1)S(1)} %bitcast.103, bf16[2,4,256,1024]{3,2,1,0:T(8,128)(2,1)} %bitcast.128, ...), custom_call_target="tpu_custom_call" | custom-call | bytes 22839304 | tf_op jit(solution)/shard_map/wide_out/pallas_call | solution.py:45
  419.5 13.5 %all_to_all.113.refs_5_ = f32[16,4,1024]{2,1,0:T(4,128)S(1)} all-to-all(f32[16,4,1024]{2,1,0:T(4,128)S(1)} %broadcast_in_dim.10), channel_id=1, replica_groups=mesh['dp'=2,'wa'=16] {'wa'}, dimensions={0} | all-to-all | bytes 524288 | tf_op jit(solution)/shard_map/all_to_all | solution.py:754
  433.0 13.0 %middle_back.1 = (f32[8,256,256]{2,1,0:T(8,128)}, bf16[1024,256]{1,0:T(8,128)(2,1)}, f32[32,2,256]{2,1,0:T(2,128)}) custom-call(f32[1,1]{1,0:T(1,128)} %bitcast.refs_0_, s32[1]{0:T(128)} %dynamic_slice.3.refs_0_.refs_1_, f32[8,256,1024]{2,1,0:T(8,128)} %bitcast.121, bf16[8,256,256]{2,1,0:T(8,128)(2,1)} %copy-done.5, ...), custom_call_target="tpu_custom_call" | custom-call | bytes 15345672 | tf_op jit(solution)/shard_map/middle_back/pallas_call | solution.py:45
  456.0 9.9 %narrow_back.1 = (bf16[8,256,256]{2,1,0:T(8,128)(2,1)S(1)}, f32[8,256,256]{2,1,0:T(8,128)}, f32[32,2,256]{2,1,0:T(2,128)S(1)}) custom-call(f32[1,1]{1,0:T(1,128)} %bitcast.refs_0_, s32[1]{0:T(128)} %dynamic_slice.3.refs_0_.refs_1_, f32[8,256,256]{2,1,0:T(8,128)} %get-tuple-element.101.refs_2_, f32[8,256,256]{2,1,0:T(8,128)} %get-tuple-element.91.refs_2_.refs_8_.refs_3_, ...), custom_call_target="tpu_custom_call" | custom-call | bytes 10883080 | tf_op jit(solution)/shard_map/narrow_back/pallas_call | solution.py:45
  466.9 10.5 %all_to_all.114.refs_5_ = f32[32,2,256]{2,1,0:T(2,128)} all-to-all(f32[32,2,256]{2,1,0:T(2,128)S(1)} %get-tuple-element.104), channel_id=1, replica_groups=mesh['dp'=2,'wa'=16] {'dp','wa'}, dimensions={0} | all-to-all | bytes 131072 | tf_op jit(solution)/shard_map/all_to_all | solution.py:747
  477.4 4.8 all-to-all-start.10
  482.3 23.2 %project_back.1 = (bf16[8,256,1280]{2,1,0:T(8,128)(2,1)}, bf16[5120,256]{1,0:T(8,128)(2,1)}) custom-call(f32[1,1]{1,0:T(1,128)} %bitcast.refs_0_, s32[1]{0:T(128)} %dynamic_slice.3.refs_0_.refs_1_, f32[8,256,1024]{2,1,0:T(8,128)} %bitcast.122, bf16[8,256,1024]{2,1,0:T(8,128)(2,1)} %get-tuple-element.96.refs_3_, ...), custom_call_target="tpu_custom_call" | custom-call | flops 10737418240 | bytes 28844040 | tf_op jit(solution)/shard_map/project_back/pallas_call | solution.py:45
  505.5 56.4 %all-to-all-done.10.refs_0_.refs_12_ = bf16[16,1024,128]{2,1,0:T(8,128)(2,1)} async-done(((bf16[16,1024,128]{2,1,0:T(8,128)(2,1)}), bf16[16,1024,128]{2,1,0:T(8,128)(2,1)}, u32[]{:S(2)}, u32[]{:S(2)}) %all-to-all-start.10) | async-done | bytes 4194336 | tf_op jit(solution)/shard_map/all_to_all | solution.py:744
  564.5 12.4 %join_back.1 = (bf16[10,256,256]{2,1,0:T(8,128)(2,1)S(1)}, bf16[16,1024,128]{2,1,0:T(8,128)(2,1)}, f32[2,4,256,256]{3,2,1,0:T(8,128)}, f32[32,2,256]{2,1,0:T(2,128)S(1)}) custom-call(f32[1,1]{1,0:T(1,128)} %bitcast.refs_0_, s32[1]{0:T(128)} %dynamic_slice.3.refs_0_.refs_1_, f32[8,256,256]{2,1,0:T(8,128)} %get-tuple-element.103.refs_2_, ...), custom_call_target="tpu_custom_call" | custom-call | bytes 25563144 | tf_op jit(solution)/shard_map/join_back/pallas_call | solution.py:45
  584.8 7.6 plane_weight.1
  594.8 19.0 %all-to-all-start.15 = ((f32[32,2,256]{2,1,0:T(2,128)}), f32[32,2,256]{2,1,0:T(2,128)}, u32[]{:S(2)}, u32[]{:S(2)}) async-start(f32[32,2,256]{2,1,0:T(2,128)} %copy-done.34), calls=%async_computation.15 | async-start | bytes 131072 | tf_op jit(solution)/shard_map/all_to_all | solution.py:747
  615.3 5.8 all-to-all-done.15.refs_5_
  622.9 5.8 lateral_back.1
  632.9 6.9 weight_merge.1
  639.8 53.6 %all_to_all.115 = bf16[16,512,128]{2,1,0:T(8,128)(2,1)} all-to-all(bf16[16,512,128]{2,1,0:T(8,128)(2,1)} %bitcast.134), channel_id=1, replica_groups=mesh['dp'=2,'wa'=16] {'wa'}, dimensions={0} | all-to-all | bytes 4194304 | tf_op jit(solution)/shard_map/all_to_all | solution.py:744
  693.4 9.4 reduce-scatter.2.cloned.1.call-done.refs_9_
  704.0 7.1 fast_back_sum.1
  711.1 11.9 %all_to_all.116.refs_5_ = f32[32,8,128]{2,1,0:T(8,128)S(1)} all-to-all(f32[32,8,128]{2,1,0:T(8,128)S(1)} %get-tuple-element.118), channel_id=1, replica_groups=mesh['dp'=2,'wa'=16] {'dp','wa'}, dimensions={0} | all-to-all | bytes 262144 | tf_op jit(solution)/shard_map/all_to_all | solution.py:747
  722.9 7.9 fast_back_widen.1
  730.9 2.7 all-to-all-start.18
  735.7 5.9 all-to-all-done.18.refs_4_
  741.5 6.3 fast_back_plane.1
  748.7 9.8 %all_to_all.117.refs_4_ = f32[32,8,128]{2,1,0:T(8,128)S(1)} all-to-all(f32[32,8,128]{2,1,0:T(8,128)S(1)} %get-tuple-element.123), channel_id=1, replica_groups=mesh['dp'=2,'wa'=16] {'dp','wa'}, dimensions={0} | all-to-all | bytes 262144 | tf_op jit(solution)/shard_map/all_to_all | solution.py:747
  758.5 4.7 all-to-all-start.14
  766.0 7.2 unpack.2
  774.0 2.6 fast_back_first.1.refs_1_
  776.7 3.7 collective-permute-start.10
  782.5 87.7 %all-to-all-done.14.refs_0_.refs_6_ = bf16[16,1024,128]{2,1,0:T(8,128)(2,1)} async-done(((bf16[16,1024,128]{2,1,0:T(8,128)(2,1)}), bf16[16,1024,128]{2,1,0:T(8,128)(2,1)}, u32[]{:S(2)}, u32[]{:S(2)}) %all-to-all-start.14) | async-done | bytes 4194336 | tf_op jit(solution)/shard_map/all_to_all | solution.py:744
  870.2 7.1 unpack.3
  877.4 6.8 fast_back_out.1
  885.4 6.1 collective-permute-start.13
  900.3 5.4 collective-permute-done.12.refs_2_
  905.8 19.6 %collective-permute-done.13.refs_3_ = bf16[1616,256]{1,0:T(8,128)(2,1)} collective-permute-done((bf16[1616,256]{1,0:T(8,128)(2,1)}, bf16[1616,256]{1,0:T(8,128)(2,1)}, u32[]{:S(2)}, u32[]{:S(2)}) %collective-permute-start.13) | collective-permute-done | bytes 827424 | tf_op jit(solution)/shard_map/ppermute | solution.py:1339
  928.0 13.9 %all-to-all-start.20 = ((f32[32,7,128]{2,1,0:T(8,128)}), f32[32,7,128]{2,1,0:T(8,128)S(1)}, u32[]{:S(2)}, u32[]{:S(2)}) async-start(f32[32,7,128]{2,1,0:T(8,128)} %reshape.259), calls=%async_computation.21 | async-start | bytes 262144 | tf_op jit(solution)/shard_map/all_to_all | solution.py:747
  941.8 7.9 all-to-all-done.20
  954.2 6.8 all-to-all-done.21
  963.3 7.7 weight_split.1
  (259 shorter events, 86.7 us)
Async XLA Ops:
  13.5 8.5 copy-start.54
  13.5 89.0 %all-to-all-start = ((bf16[16,1024,128]{2,1,0:T(8,128)(2,1)}), bf16[16,1024,128]{2,1,0:T(8,128)(2,1)}, u32[]{:S(2)}, u32[]{:S(2)}) async-start(bf16[16,1024,128]{2,1,0:T(8,128)(2,1)} %pack.2), calls=%async_computation | async-start | bytes 8388608 | tf_op jit(solution)/shard_map/all_to_all | solution.py:744
  22.0 10.8 %copy-start.43 = (s32[16]{0:T(128)S(1)}, s32[16]{0:T(128)}, u32[]{:S(2)}) copy-start(s32[16]{0:T(128)} %refs_1_.7) | copy-start | bytes 196
  22.0 14.8 %copy-start.53 = (bf16[3,3,32,32]{3,2,1,0:T(8,128)(2,1)S(1)}, bf16[3,3,32,32]{3,2,1,0:T(8,128)(2,1)}, u32[]{:S(2)}) copy-start(bf16[3,3,32,32]{3,2,1,0:T(8,128)(2,1)} %param.25) | copy-start | bytes 55300
  27.7 12.6 %collective-permute-start = (bf16[4,256,128]{2,1,0:T(8,128)(2,1)S(1)}, bf16[4,256,128]{2,1,0:T(8,128)(2,1)S(1)}, u32[]{:S(2)}, u32[]{:S(2)}) collective-permute-start(bf16[4,256,128]{2,1,0:T(8,128)(2,1)S(1)} %get-tuple-element.78), channel_id=1, source_target_pairs={{0,1},{1,2},{2,3},{3,4},{4,5},{5,6},{6,7},{7,8},{8,9},{9,10},{10,1... | collective-permute-start | bytes 786440 | tf_op jit(solution)/shard_map/ppermute | solution.py:826
  31.5 18.3 %collective-permute-start.1 = (bf16[4,256,128]{2,1,0:T(8,128)(2,1)S(1)}, bf16[4,256,128]{2,1,0:T(8,128)(2,1)S(1)}, u32[]{:S(2)}, u32[]{:S(2)}) collective-permute-start(bf16[4,256,128]{2,1,0:T(8,128)(2,1)S(1)} %get-tuple-element.79), channel_id=1, source_target_pairs={{1,0},{2,1},{3,2},{4,3},{5,4},{6,5},{7,6},{8,7},{9,8},{10,9},{11,1... | collective-permute-start | bytes 786440 | tf_op jit(solution)/shard_map/ppermute | solution.py:827
  106.3 28.0 %copy-start.56 = (f32[2,32]{1,0:T(2,128)S(1)}, f32[2,32]{1,0:T(2,128)}, u32[]{:S(2)}) copy-start(f32[2,32]{1,0:T(2,128)} %param.32) | copy-start | bytes 772
  106.3 33.3 %all-to-all-start.1 = ((f32[32,8,128]{2,1,0:T(8,128)}), f32[32,8,128]{2,1,0:T(8,128)S(1)}, u32[]{:S(2)}, u32[]{:S(2)}) async-start(f32[32,8,128]{2,1,0:T(8,128)} %get-tuple-element.81), calls=%async_computation.1 | async-start | bytes 262144 | tf_op jit(solution)/shard_map/all_to_all | solution.py:747
  133.7 14.0 %copy-start.57 = (f32[2,32]{1,0:T(2,128)S(1)}, f32[2,32]{1,0:T(2,128)}, u32[]{:S(2)}) copy-start(f32[2,32]{1,0:T(2,128)} %param.33) | copy-start | bytes 772
  133.7 14.1 %copy-start.55 = (bf16[32,128]{1,0:T(8,128)(2,1)S(1)}, bf16[32,128]{1,0:T(8,128)(2,1)}, u32[]{:S(2)}) copy-start(bf16[32,128]{1,0:T(8,128)(2,1)} %param.26) | copy-start | bytes 24580
  134.3 34.2 %copy-start.41 = (f32[2,128]{1,0:T(2,128)S(1)}, f32[2,128]{1,0:T(2,128)}, u32[]{:S(2)}) copy-start(f32[2,128]{1,0:T(2,128)} %refs_6_.13) | copy-start | bytes 3076
  145.1 10.5 %all-to-all-start.2 = ((f32[32,8,128]{2,1,0:T(8,128)}), f32[32,8,128]{2,1,0:T(8,128)S(1)}, u32[]{:S(2)}, u32[]{:S(2)}) async-start(f32[32,8,128]{2,1,0:T(8,128)} %get-tuple-element.83), calls=%async_computation.2 | async-start | bytes 262144 | tf_op jit(solution)/shard_map/all_to_all | solution.py:747
  147.8 10.8 %copy-start.39 = (f32[2,128]{1,0:T(2,128)}, f32[2,128]{1,0:T(2,128)S(1)}, u32[]{:S(2)}) copy-start(f32[2,128]{1,0:T(2,128)S(1)} %tile.21.refs_3_.refs_10_.refs_5_) | copy-start | bytes 3076
  155.6 17.7 %copy-start.8 = (f32[32,8,128]{2,1,0:T(8,128)}, f32[32,8,128]{2,1,0:T(8,128)S(1)}, u32[]{:S(2)}) copy-start(f32[32,8,128]{2,1,0:T(8,128)S(1)} %all-to-all-done.2.refs_2_.refs_9_.refs_3_) | copy-start | bytes 393220
  173.4 47.9 %all-to-all-start.4 = ((bf16[16,512,128]{2,1,0:T(8,128)(2,1)}), bf16[16,512,128]{2,1,0:T(8,128)(2,1)}, u32[]{:S(2)}, u32[]{:S(2)}) async-start(bf16[16,512,128]{2,1,0:T(8,128)(2,1)} %bitcast.123), calls=%async_computation.4 | async-start | bytes 4194304 | tf_op jit(solution)/shard_map/all_to_all | solution.py:744
  226.7 22.5 %all-to-all-start.5 = ((f32[32,2,256]{2,1,0:T(2,128)}), f32[32,2,256]{2,1,0:T(2,128)S(1)}, u32[]{:S(2)}, u32[]{:S(2)}) async-start(f32[32,2,256]{2,1,0:T(2,128)} %get-tuple-element.87), calls=%async_computation.5 | async-start | bytes 131072 | tf_op jit(solution)/shard_map/all_to_all | solution.py:747
  236.0 13.2 %copy-start.37 = (f32[2,256]{1,0:T(2,128)S(1)}, f32[2,256]{1,0:T(2,128)}, u32[]{:S(2)}) copy-start(f32[2,256]{1,0:T(2,128)} %refs_6_.12) | copy-start | bytes 6148
  249.2 5.6 copy-start.13
  249.2 19.5 %copy-start.38 = (f32[2,256]{1,0:T(2,128)S(1)}, f32[2,256]{1,0:T(2,128)}, u32[]{:S(2)}) copy-start(f32[2,256]{1,0:T(2,128)} %refs_6_.11) | copy-start | bytes 6148
  268.8 187.2 %copy-start.19 = (f32[32,2,256]{2,1,0:T(2,128)}, f32[32,2,256]{2,1,0:T(2,128)S(1)}, u32[]{:S(2)}) copy-start(f32[32,2,256]{2,1,0:T(2,128)S(1)} %all_to_all.111.refs_3_.refs_9_.refs_4_) | copy-start | bytes 196612
  278.8 9.9 %all-to-all-start.7 = ((f32[32,2,256]{2,1,0:T(2,128)}), f32[32,2,256]{2,1,0:T(2,128)S(1)}, u32[]{:S(2)}, u32[]{:S(2)}) async-start(f32[32,2,256]{2,1,0:T(2,128)} %get-tuple-element.92), calls=%async_computation.7 | async-start | bytes 131072 | tf_op jit(solution)/shard_map/all_to_all | solution.py:747
  287.7 7.6 copy-start.4
  287.7 7.6 copy-start.36
  288.7 167.2 %copy-start.17 = (f32[32,2,256]{2,1,0:T(2,128)}, f32[32,2,256]{2,1,0:T(2,128)S(1)}, u32[]{:S(2)}) copy-start(f32[32,2,256]{2,1,0:T(2,128)S(1)} %all-to-all-done.7.refs_3_.refs_9_.refs_4_) | copy-start | bytes 196612
  288.7 86.8 %all-to-all-start.8 = ((bf16[16,1024,128]{2,1,0:T(8,128)(2,1)}), bf16[16,1024,128]{2,1,0:T(8,128)(2,1)}, u32[]{:S(2)}, u32[]{:S(2)}) async-start(bf16[16,1024,128]{2,1,0:T(8,128)(2,1)} %pack.3), calls=%async_computation.8 | async-start | bytes 8388608 | tf_op jit(solution)/shard_map/all_to_all | solution.py:744
  295.2 109.4 %copy-start.35 = (f32[2,1024]{1,0:T(2,128)S(1)}, f32[2,1024]{1,0:T(2,128)}, u32[]{:S(2)}) copy-start(f32[2,1024]{1,0:T(2,128)} %refs_6_.8) | copy-start | bytes 24580
  295.3 109.4 %copy-start.45 = (f32[2,1024]{1,0:T(2,128)S(1)}, f32[2,1024]{1,0:T(2,128)}, u32[]{:S(2)}) copy-start(f32[2,1024]{1,0:T(2,128)} %refs_6_.10) | copy-start | bytes 24580
  305.7 112.5 %copy-start.5 = (bf16[8,256,256]{2,1,0:T(8,128)(2,1)}, bf16[8,256,256]{2,1,0:T(8,128)(2,1)S(1)}, u32[]{:S(2)}) copy-start(bf16[8,256,256]{2,1,0:T(8,128)(2,1)S(1)} %get-tuple-element.95.refs_3_) | copy-start | bytes 3145732
  305.7 1.2 collective-permute-start.2
  418.2 1.2 collective-permute-start.3
  433.0 49.3 %copy-start.11 = (f32[16,4,1024]{2,1,0:T(4,128)}, f32[16,4,1024]{2,1,0:T(4,128)S(1)}, u32[]{:S(2)}) copy-start(f32[16,4,1024]{2,1,0:T(4,128)S(1)} %all_to_all.113.refs_5_) | copy-start | bytes 786436
  446.0 9.9 %all-to-all-start.12 = ((f32[32,2,256]{2,1,0:T(2,128)}), f32[32,2,256]{2,1,0:T(2,128)S(1)}, u32[]{:S(2)}, u32[]{:S(2)}) async-start(f32[32,2,256]{2,1,0:T(2,128)} %get-tuple-element.102), calls=%async_computation.12 | async-start | bytes 131072 | tf_op jit(solution)/shard_map/all_to_all | solution.py:747
  455.9 9.9 %copy-start.26 = (f32[32,2,256]{2,1,0:T(2,128)}, f32[32,2,256]{2,1,0:T(2,128)S(1)}, u32[]{:S(2)}) copy-start(f32[32,2,256]{2,1,0:T(2,128)S(1)} %all-to-all-done.12.refs_5_) | copy-start | bytes 196612
  477.4 84.5 %all-to-all-start.10 = ((bf16[16,1024,128]{2,1,0:T(8,128)(2,1)}), bf16[16,1024,128]{2,1,0:T(8,128)(2,1)}, u32[]{:S(2)}, u32[]{:S(2)}) async-start(bf16[16,1024,128]{2,1,0:T(8,128)(2,1)} %get-tuple-element.98), calls=%async_computation.10 | async-start | bytes 8388608 | tf_op jit(solution)/shard_map/all_to_all | solution.py:744
  505.5 125.8 %collective-permute-start.4 = (bf16[5120,256]{1,0:T(8,128)(2,1)}, bf16[5120,256]{1,0:T(8,128)(2,1)}, u32[]{:S(2)}, u32[]{:S(2)}) collective-permute-start(bf16[5120,256]{1,0:T(8,128)(2,1)} %get-tuple-element.111.refs_1_), channel_id=1, source_target_pairs={{0,16},{16,0},{1,17},{17,1},{2,18},{18,2},{3,19},{19,3},{4,20},{20... | collective-permute-start | bytes 7864328 | tf_op jit(solution)/shard_map/ppermute | solution.py:1206
  584.3 48.5 %collective-permute-start.7 = (bf16[3072,256]{1,0:T(8,128)(2,1)}, bf16[3072,256]{1,0:T(8,128)(2,1)}, u32[]{:S(2)}, u32[]{:S(2)}) collective-permute-start(bf16[3072,256]{1,0:T(8,128)(2,1)} %bitcast.38.refs_4_), channel_id=1, source_target_pairs={{0,16},{16,0},{1,17},{17,1},{2,18},{18,2},{3,19},{19,3},{4,20},{20... | collective-permute-start | bytes 4718600 | tf_op jit(solution)/shard_map/ppermute | solution.py:1206
  584.3 46.8 %collective-permute-start.5 = (bf16[1024,256]{1,0:T(8,128)(2,1)}, bf16[1024,256]{1,0:T(8,128)(2,1)}, u32[]{:S(2)}, u32[]{:S(2)}) collective-permute-start(bf16[1024,256]{1,0:T(8,128)(2,1)} %get-tuple-element.112.refs_2_), channel_id=1, source_target_pairs={{0,16},{16,0},{1,17},{17,1},{2,18},{18,2},{3,19},{19,3},{4,20},{20... | collective-permute-start | bytes 1572872 | tf_op jit(solution)/shard_map/ppermute | solution.py:1206
  592.5 38.8 %collective-permute-start.6 = (bf16[2304,256]{1,0:T(8,128)(2,1)}, bf16[2304,256]{1,0:T(8,128)(2,1)}, u32[]{:S(2)}, u32[]{:S(2)}) collective-permute-start(bf16[2304,256]{1,0:T(8,128)(2,1)} %bitcast.137), channel_id=1, source_target_pairs={{0,16},{16,0},{1,17},{17,1},{2,18},{18,2},{3,19},{19,3},{4,20},{20... | collective-permute-start | bytes 3538952 | tf_op jit(solution)/shard_map/ppermute | solution.py:1206
  594.8 26.3 %all-to-all-start.15 = ((f32[32,2,256]{2,1,0:T(2,128)}), f32[32,2,256]{2,1,0:T(2,128)}, u32[]{:S(2)}, u32[]{:S(2)}) async-start(f32[32,2,256]{2,1,0:T(2,128)} %copy-done.34), calls=%async_computation.15 | async-start | bytes 131072 | tf_op jit(solution)/shard_map/all_to_all | solution.py:747
  613.8 89.0 %reduce-scatter.2.cloned.1.call-start = ((), (), s32[]{:S(2)}) async-start(), calls=%async_computation.23 | async-start | bytes 4136960 | tf_op jit(solution)/shard_map/reduce_scatter | solution.py:1218
  615.1 16.2 %collective-permute-start.8 = (bf16[768,256]{1,0:T(8,128)(2,1)S(1)}, bf16[768,256]{1,0:T(8,128)(2,1)S(1)}, u32[]{:S(2)}, u32[]{:S(2)}) collective-permute-start(bf16[768,256]{1,0:T(8,128)(2,1)S(1)} %bitcast.108), channel_id=1, source_target_pairs={{0,16},{16,0},{1,17},{17,1},{2,18},{18,2},{3,19},{19,3},{4,20},{20... | collective-permute-start | bytes 1179656 | tf_op jit(solution)/shard_map/ppermute | solution.py:1206
  631.2 1.7 collective-permute-start.9
  639.8 63.0 %copy-start.42 = (f32[2,128]{1,0:T(2,128)S(1)}, f32[2,128]{1,0:T(2,128)}, u32[]{:S(2)}) copy-start(f32[2,128]{1,0:T(2,128)} %refs_6_.13) | copy-start | bytes 3076
  639.8 63.0 %copy-start.44 = (s32[16]{0:T(128)S(1)}, s32[16]{0:T(128)}, u32[]{:S(2)}) copy-start(s32[16]{0:T(128)} %refs_1_.7) | copy-start | bytes 196
  704.0 19.0 %copy-start.9 = (f32[32,8,128]{2,1,0:T(8,128)S(1)}, f32[32,8,128]{2,1,0:T(8,128)}, u32[]{:S(2)}) copy-start(f32[32,8,128]{2,1,0:T(8,128)} %copy-done.8) | copy-start | bytes 393220
  704.0 19.0 %copy-start.40 = (f32[2,128]{1,0:T(2,128)S(1)}, f32[2,128]{1,0:T(2,128)}, u32[]{:S(2)}) copy-start(f32[2,128]{1,0:T(2,128)} %copy-done.39) | copy-start | bytes 3076
  730.9 10.6 %copy-start.33 = (bf16[4,2,256,128]{3,2,1,0:T(8,128)(2,1)S(1)}, bf16[4,2,256,128]{3,2,1,0:T(8,128)(2,1)}, u32[]{:S(2)}) copy-start(bf16[4,2,256,128]{3,2,1,0:T(8,128)(2,1)} %copy-done.32) | copy-start | bytes 1572868
  730.9 10.6 %all-to-all-start.18 = ((f32[32,8,128]{2,1,0:T(8,128)}), f32[32,8,128]{2,1,0:T(8,128)S(1)}, u32[]{:S(2)}, u32[]{:S(2)}) async-start(f32[32,8,128]{2,1,0:T(8,128)} %get-tuple-element.120), calls=%async_computation.19 | async-start | bytes 262144 | tf_op jit(solution)/shard_map/all_to_all | solution.py:747
  758.5 111.7 %all-to-all-start.14 = ((bf16[16,1024,128]{2,1,0:T(8,128)(2,1)}), bf16[16,1024,128]{2,1,0:T(8,128)(2,1)}, u32[]{:S(2)}, u32[]{:S(2)}) async-start(bf16[16,1024,128]{2,1,0:T(8,128)(2,1)} %get-tuple-element.107), calls=%async_computation.14 | async-start | bytes 8388608 | tf_op jit(solution)/shard_map/all_to_all | solution.py:744
  763.2 114.1 %all-reduce.3.cloned.1.call-start = ((), (), s32[]{:S(2)}) async-start(), calls=%async_computation.24 | async-start | bytes 1654784 | tf_op jit(solution)/shard_map/psum | solution.py:1219
  766.0 8.1 copy-start.24
  776.7 100.7 %collective-permute-start.10 = (bf16[4,256,128]{2,1,0:T(8,128)(2,1)S(1)}, bf16[4,256,128]{2,1,0:T(8,128)(2,1)S(1)}, u32[]{:S(2)}, u32[]{:S(2)}) collective-permute-start(bf16[4,256,128]{2,1,0:T(8,128)(2,1)S(1)} %get-tuple-element.200), channel_id=1, source_target_pairs={{0,1},{1,2},{2,3},{3,4},{4,5},{5,6},{6,7},{7,8},{8,9},{9,10},{10,1... | collective-permute-start | bytes 786440 | tf_op jit(solution)/shard_map/ppermute | solution.py:1313
  780.3 97.0 %collective-permute-start.11 = (bf16[4,256,128]{2,1,0:T(8,128)(2,1)S(1)}, bf16[4,256,128]{2,1,0:T(8,128)(2,1)S(1)}, u32[]{:S(2)}, u32[]{:S(2)}) collective-permute-start(bf16[4,256,128]{2,1,0:T(8,128)(2,1)S(1)} %get-tuple-element.199), channel_id=1, source_target_pairs={{1,0},{2,1},{3,2},{4,3},{5,4},{6,5},{7,6},{8,7},{9,8},{10,9},{11,1... | collective-permute-start | bytes 786440 | tf_op jit(solution)/shard_map/ppermute | solution.py:1314
  877.3 16.2 %copy-start.31 = (f32[3,384,128]{2,1,0:T(8,128)S(1)}, f32[3,384,128]{2,1,0:T(8,128)}, u32[]{:S(2)}) copy-start(f32[3,384,128]{2,1,0:T(8,128)} %copy-done.30) | copy-start | bytes 1769476
  884.2 21.6 %collective-permute-start.12 = (bf16[1616,256]{1,0:T(8,128)(2,1)}, bf16[1616,256]{1,0:T(8,128)(2,1)S(1)}, u32[]{:S(2)}, u32[]{:S(2)}) collective-permute-start(bf16[1616,256]{1,0:T(8,128)(2,1)} %get-tuple-element.128.refs_1_), channel_id=1, source_target_pairs={{0,1},{1,0},{2,3},{3,2},{4,5},{5,4},{6,7},{7,6},{8,9},{9,8},{10,11... | collective-permute-start | bytes 2482184 | tf_op jit(solution)/shard_map/ppermute | solution.py:1339
  885.4 40.0 %collective-permute-start.13 = (bf16[1616,256]{1,0:T(8,128)(2,1)}, bf16[1616,256]{1,0:T(8,128)(2,1)}, u32[]{:S(2)}, u32[]{:S(2)}) collective-permute-start(bf16[1616,256]{1,0:T(8,128)(2,1)} %get-tuple-element.128.refs_1_), channel_id=1, source_target_pairs={{0,2},{1,3},{2,0},{3,1},{4,6},{5,7},{6,4},{7,5},{8,10},{9,11},{10,... | collective-permute-start | bytes 2482184 | tf_op jit(solution)/shard_map/ppermute | solution.py:1339
  891.5 35.8 %collective-permute-start.14 = (bf16[1616,256]{1,0:T(8,128)(2,1)}, bf16[1616,256]{1,0:T(8,128)(2,1)}, u32[]{:S(2)}, u32[]{:S(2)}) collective-permute-start(bf16[1616,256]{1,0:T(8,128)(2,1)} %get-tuple-element.128.refs_1_), channel_id=1, source_target_pairs={{0,3},{1,2},{2,1},{3,0},{4,7},{5,6},{6,5},{7,4},{8,11},{9,10},{10,... | collective-permute-start | bytes 2482184 | tf_op jit(solution)/shard_map/ppermute | solution.py:1339
  893.4 5.2 copy-start.7
  898.6 64.6 %collective-permute-start.15 = (bf16[1616,256]{1,0:T(8,128)(2,1)S(1)}, bf16[1616,256]{1,0:T(8,128)(2,1)}, u32[]{:S(2)}, u32[]{:S(2)}) collective-permute-start(bf16[1616,256]{1,0:T(8,128)(2,1)S(1)} %copy-done.7), channel_id=1, source_target_pairs={{0,16},{16,0},{1,17},{17,1},{2,18},{18,2},{3,19},{19,3},{4,20},{20... | collective-permute-start | bytes 2482184 | tf_op jit(solution)/shard_map/ppermute | solution.py:1343
  905.8 57.5 %collective-permute-start.16 = (bf16[1616,256]{1,0:T(8,128)(2,1)S(1)}, bf16[1616,256]{1,0:T(8,128)(2,1)}, u32[]{:S(2)}, u32[]{:S(2)}) collective-permute-start(bf16[1616,256]{1,0:T(8,128)(2,1)S(1)} %collective-permute-done.12.refs_2_), channel_id=1, source_target_pairs={{0,16},{16,0},{1,17},{17,1},{2,18},{18,2},{3,19},{19,3},{4,20},{20... | collective-permute-start | bytes 2482184 | tf_op jit(solution)/shard_map/ppermute | solution.py:1343
  925.4 37.8 %collective-permute-start.17 = (bf16[1616,256]{1,0:T(8,128)(2,1)}, bf16[1616,256]{1,0:T(8,128)(2,1)}, u32[]{:S(2)}, u32[]{:S(2)}) collective-permute-start(bf16[1616,256]{1,0:T(8,128)(2,1)} %collective-permute-done.13.refs_3_), channel_id=1, source_target_pairs={{0,16},{16,0},{1,17},{17,1},{2,18},{18,2},{3,19},{19,3},{4,20},{20... | collective-permute-start | bytes 2482184 | tf_op jit(solution)/shard_map/ppermute | solution.py:1343
  927.3 36.0 %collective-permute-start.18 = (bf16[1616,256]{1,0:T(8,128)(2,1)}, bf16[1616,256]{1,0:T(8,128)(2,1)}, u32[]{:S(2)}, u32[]{:S(2)}) collective-permute-start(bf16[1616,256]{1,0:T(8,128)(2,1)} %collective-permute-done.14.refs_4_), channel_id=1, source_target_pairs={{0,16},{16,0},{1,17},{17,1},{2,18},{18,2},{3,19},{19,3},{4,20},{20... | collective-permute-start | bytes 2482184 | tf_op jit(solution)/shard_map/ppermute | solution.py:1343
  928.0 21.8 %all-to-all-start.20 = ((f32[32,7,128]{2,1,0:T(8,128)}), f32[32,7,128]{2,1,0:T(8,128)S(1)}, u32[]{:S(2)}, u32[]{:S(2)}) async-start(f32[32,7,128]{2,1,0:T(8,128)} %reshape.259), calls=%async_computation.21 | async-start | bytes 262144 | tf_op jit(solution)/shard_map/all_to_all | solution.py:747
  950.4 10.5 %all-to-all-start.21 = ((f32[32,7,128]{2,1,0:T(8,128)}), f32[32,7,128]{2,1,0:T(8,128)S(1)}, u32[]{:S(2)}, u32[]{:S(2)}) async-start(f32[32,7,128]{2,1,0:T(8,128)} %broadcast_in_dim.11), calls=%async_computation.22 | async-start | bytes 262144 | tf_op jit(solution)/shard_map/all_to_all | solution.py:747
  (30 other events, 44.3 us)
Sparse Core Ops, SparseCore 0:
  639.9 62.8 reduce-scatter.1
  766.4 92.5 all-reduce.2

commit v2 on v1

--- a/solution.py
+++ b/solution.py
@@ -68,17 +68,13 @@
     return lax.dot_general(a, b, (((0,), (0,)), ((), ())), preferred_element_type=F32)
 
 
-def logistic(u):
-    return 0.5 * jnp.tanh(0.5 * u) + 0.5
-
-
-def silu(u):
-    return u * logistic(u)
-
-
-def silu_slope(u):
-    g = logistic(u)
-    return g + u * g * (1.0 - g)
+def silu_half(v):
+    return v * (1.0 + jnp.tanh(v))
+
+
+def slope_half(v):
+    h = 1.0 + jnp.tanh(v)
+    return h + v * h * (2.0 - h)
 
 
 def cell_ids(rows):
@@ -112,8 +108,8 @@
     mean = total[0:1] / count
     variance = total[1:2] / count - mean * mean
     inv = lax.rsqrt(variance + EPSILON)
-    scale = params[0:1] * inv
-    return mean, inv, scale, params[1:2] - mean * scale
+    scale = 0.5 * params[0:1] * inv
+    return mean, inv, scale, 0.5 * params[1:2] - mean * scale
 
 
 def back_terms(gathered, params, count, mean, inv, folded=False):
@@ -121,7 +117,7 @@
     if folded:
         total = fold(total)
     a = params[0:1] * inv
-    b = -a * inv * inv * total[1:2] / count
+    b = -a * inv * inv * (total[1:2] - mean * total[0:1]) / count
     return a, b, -a * total[0:1] / count - b * mean
 
 
@@ -150,27 +146,32 @@
         out[block * rows : (block + 1) * rows, :] = wide[:, block * width : (block + 1) * width].astype(BF)
 
 
-def plane_windows(values, cells):
+def fill_windows(scratch, values, first, cells):
     rows = values.shape[0]
     w = lax.broadcasted_iota(jnp.int32, (rows, 1), 0) & (cells - 1)
     left = jnp.where(w == 0, 0.0, pltpu.roll(values, 1, 0))
     right = jnp.where(w == cells - 1, 0.0, pltpu.roll(values, rows - 1, 0))
-    return jnp.concatenate([left.astype(BF), values.astype(BF), right.astype(BF)], axis=1)
-
-
-def fill_windows(scratch, windows, cells):
-    rows = windows.shape[0]
-    zeros = jnp.zeros((cells, windows.shape[1]), BF)
-    scratch[0:cells, :] = zeros
-    scratch[cells : cells + rows, :] = windows
-    scratch[cells + rows : 2 * cells + rows, :] = zeros
-
-
-def plane_dot(scratch, weight, rows, cells):
+    scratch[first : first + rows, :] = jnp.concatenate(
+        [left.astype(BF), values.astype(BF), right.astype(BF)], axis=1
+    )
+
+
+def clear_gaps(scratch, frames, cells):
+    pitch = cells * (cells + 1)
+    for frame in range(frames + 1):
+        scratch[frame * pitch : frame * pitch + cells, :] = jnp.zeros((cells, scratch.shape[1]), BF)
+
+
+def plane_dot(scratch, weight, frames, cells):
+    rows = frames * cells * (cells + 1) - cells
     out = dot(scratch[0:rows, :], weight[0])
     for tap in (1, 2):
         out = out + dot(scratch[tap * cells : tap * cells + rows, :], weight[tap])
     return out
+
+
+def window_shape(frames, width):
+    return pltpu.VMEM((frames * 272 + 16, width), BF)
 
 
 def fast_first(x, w, y, to_next, to_prev):
@@ -202,32 +203,35 @@
     i = pl.program_id(0)
     _, _, scale, shift = norm_terms(g1[...], params[...], count[0, 0], True)
     mask = packed_mask(sides[0], 256)
-    sums, squares = [], []
+
+    @pl.when(i == 0)
+    def _():
+        clear_gaps(win, 2, 16)
+
     for frame in range(2):
-        a = mask * silu(pre[0, frame] * scale + shift)
+        a = mask * silu_half(pre[0, frame] * scale + shift)
         act[0, frame] = a.astype(BF)
-        fill_windows(win, plane_windows(a, 16), 16)
-        v = plane_dot(win, w, 256, 16)
-        out[0, frame] = v
-        mv = mask * v
-        sums.append(mv)
-        squares.append(mv * v)
-    add_stats(acc, i == 0, (0, 1), (col_sum(sums[0] + sums[1]), col_sum(squares[0] + squares[1])))
+        fill_windows(win, a, 16 + 272 * frame, 16)
+    both = plane_dot(win, w, 2, 16)
+    v0, v1 = both[0:256], both[272:528]
+    out[0, 0] = v0
+    out[0, 1] = v1
+    m0, m1 = mask * v0, mask * v1
+    add_stats(acc, i == 0, (0, 1), (col_sum(m0 + m1), col_sum(m0 * v0 + m1 * v1)))
     send_stats(i == pl.num_programs(0) - 1, acc, stats)
 
 
 def fast_widen(count, pre, g2, params, sides, w, act, stats, acc):
     i = pl.program_id(0)
     _, _, scale, shift = norm_terms(g2[...], params[...], count[0, 0], True)
-    mask = packed_mask(sides[0], 256)
+    mask = packed_mask(sides[0], 512)
+    a = (mask * silu_half(pre[0].reshape(512, LANES) * scale + shift)).astype(BF)
+    act[0] = a.reshape(2, 256, LANES)
     total, square = None, None
-    for frame in range(2):
-        a = (mask * silu(pre[0, frame] * scale + shift)).astype(BF)
-        act[0, frame] = a
-        for g in range(GROUPS):
-            v = dot(a, w[g])
-            total = v if total is None else total + v
-            square = v * v if square is None else square + v * v
+    for g in range(GROUPS):
+        v = dot(a, w[g])
+        total = v if total is None else total + v
+        square = v * v if square is None else square + v * v
     add_stats(acc, i == 0, (0, 1), (col_sum(total), col_sum(square)))
     send_stats(i == pl.num_programs(0) - 1, acc, stats)
 
@@ -235,27 +239,27 @@
 def fast_out(count, sides, x, act, g3, params, w, result):
     i = pl.program_id(0)
     _, _, scale, shift = norm_terms(g3[...], params[...], count[0, 0])
+    a = act[0].reshape(512, LANES)
     for g in range(GROUPS):
-        mask = clip_mask(sides[i * GROUPS + g], 256)
-        for frame in range(2):
-            u = x[g, frame].astype(F32) + dot(act[0, frame], w[g]) * scale + shift
-            result[g, frame] = (mask * silu(u)).astype(BF)
+        mask = clip_mask(sides[i * GROUPS + g], 512)
+        v = 0.5 * x[g].reshape(512, LANES).astype(F32) + (dot(a, w[g]) * scale + shift)
+        result[g] = (mask * silu_half(v)).astype(BF).reshape(2, 256, LANES)
 
 
 def fast_back_sum(count, sides, cot, back, x, act, g3, params, w, grad, stats, acc):
     i = pl.program_id(0)
-    mean, _, scale, shift = norm_terms(g3[...], params[...], count[0, 0])
+    _, _, scale, shift = norm_terms(g3[...], params[...], count[0, 0])
+    a = act[0].reshape(512, LANES)
     total, cross = None, None
     for g in range(GROUPS):
-        mask = clip_mask(sides[i * GROUPS + g], 256)
-        for frame in range(2):
-            v = dot(act[0, frame], w[g])
-            u = x[g, frame].astype(F32) + v * scale + shift
-            e = (cot[g, frame].astype(F32) + back[g, frame].astype(F32)) * mask * silu_slope(u)
-            grad[g, frame] = e
-            total = e if total is None else total + e
-            c = e * (v - mean)
-            cross = c if cross is None else cross + c
+        mask = 0.5 * clip_mask(sides[i * GROUPS + g], 512)
+        v = dot(a, w[g])
+        u = 0.5 * x[g].reshape(512, LANES).astype(F32) + (v * scale + shift)
+        given = cot[g].reshape(512, LANES).astype(F32) + back[g].reshape(512, LANES).astype(F32)
+        e = given * (mask * slope_half(u))
+        grad[g] = e.reshape(2, 256, LANES)
+        total = e if total is None else total + e
+        cross = e * v if cross is None else cross + e * v
     add_stats(acc, i == 0, (0, 1), (col_sum(total), col_sum(cross)))
     send_stats(i == pl.num_programs(0) - 1, acc, stats)
 
@@ -267,62 +271,60 @@
     c = count[0, 0]
     mean3, inv3, _, _ = norm_terms(g3[...], params3[...], c)
     a, b, d = back_terms(h3[...], params3[...], c, mean3, inv3)
-    mean2, _, scale2, shift2 = norm_terms(g2[...], params2[...], c, True)
-    lane_mask = packed_mask(lane_sides[0], 256)
+    _, _, scale2, shift2 = norm_terms(g2[...], params2[...], c, True)
+    lane_mask = 0.5 * packed_mask(lane_sides[0], 512)
 
     @pl.when(i == 0)
     def _():
         w_grad[...] = jnp.zeros_like(w_grad)
 
-    total, cross = None, None
-    for frame in range(2):
-        s = act[0, frame]
-        back = None
-        for g in range(GROUPS):
-            mask = clip_mask(sides[i * GROUPS + g], 256)
-            v = dot(s, w[g])
-            low = (mask * (grad[g, frame] * a + v * b + d)).astype(BF)
-            part = dot_nt(low, w[g])
-            back = part if back is None else back + part
-            w_grad[g] += dot_tn(s, low)
-        p = pre[0, frame]
-        e = back * lane_mask * silu_slope(p * scale2 + shift2)
-        out[0, frame] = e
-        total = e if total is None else total + e
-        x = e * (p - mean2)
-        cross = x if cross is None else cross + x
-    add_stats(acc, i == 0, (0, 1), (col_sum(total), col_sum(cross)))
+    s = act[0].reshape(512, LANES)
+    back = None
+    for g in range(GROUPS):
+        mask = clip_mask(sides[i * GROUPS + g], 512)
+        v = dot(s, w[g])
+        low = (mask * (grad[g].reshape(512, LANES) * a + v * b + d)).astype(BF)
+        part = dot_nt(low, w[g])
+        back = part if back is None else back + part
+        w_grad[g] += dot_tn(s, low)
+    p = pre[0].reshape(512, LANES)
+    e = back * (lane_mask * slope_half(p * scale2 + shift2))
+    out[0] = e.reshape(2, 256, LANES)
+    add_stats(acc, i == 0, (0, 1), (col_sum(e), col_sum(e * p)))
     send_stats(i == pl.num_programs(0) - 1, acc, stats)
 
 
 def fast_back_plane(
-    count, e2, pre2, g2, h2, params2, act1, pre1, g1, params1, lane_sides, w, out, w_grad, stats, acc, win
+    count, e2, pre2, g2, h2, params2, act1, pre1, g1, params1, lane_sides, w, out, w_grad, stats, acc, win, low
 ):
     i = pl.program_id(0)
     c = count[0, 0]
     mean2, inv2, _, _ = norm_terms(g2[...], params2[...], c, True)
     a, b, d = back_terms(h2[...], params2[...], c, mean2, inv2, True)
-    mean1, _, scale1, shift1 = norm_terms(g1[...], params1[...], c, True)
+    _, _, scale1, shift1 = norm_terms(g1[...], params1[...], c, True)
     mask = packed_mask(lane_sides[0], 256)
 
     @pl.when(i == 0)
     def _():
         w_grad[...] = jnp.zeros_like(w_grad)
-
+        clear_gaps(win, 2, 16)
+        low[256:272, :] = jnp.zeros((16, LANES), BF)
+
+    for frame in range(2):
+        part = mask * (e2[0, frame] * a + pre2[0, frame] * b + d)
+        low[272 * frame : 272 * frame + 256, :] = part.astype(BF)
+        fill_windows(win, part, 16 + 272 * frame, 16)
+    both = plane_dot(win, w, 2, 16)
     total, cross = None, None
     for frame in range(2):
-        low = mask * (e2[0, frame] * a + pre2[0, frame] * b + d)
-        fill_windows(win, plane_windows(low, 16), 16)
         p = pre1[0, frame]
-        e = plane_dot(win, w, 256, 16) * mask * silu_slope(p * scale1 + shift1)
+        e = both[272 * frame : 272 * frame + 256] * (0.5 * mask * slope_half(p * scale1 + shift1))
         out[0, frame] = e
         total = e if total is None else total + e
-        x = e * (p - mean1)
-        cross = x if cross is None else cross + x
-        low = low.astype(BF)
-        fill_windows(win, plane_windows(act1[0, frame].astype(F32), 16), 16)
-        for tap in range(3):
-            w_grad[tap] += dot_tn(win[16 * tap : 16 * tap + 256, :], low)
+        cross = e * p if cross is None else cross + e * p
+        fill_windows(win, act1[0, frame].astype(F32), 16 + 272 * frame, 16)
+    for tap in range(3):
+        w_grad[tap] += dot_tn(win[16 * tap : 16 * tap + 528, :], low[...])
     add_stats(acc, i == 0, (0, 1), (col_sum(total), col_sum(cross)))
     send_stats(i == pl.num_programs(0) - 1, acc, stats)
 
@@ -352,21 +354,27 @@
             w_grad[g] += dot_tn(x[g, frame], joined)
 
 
-def pack_kernel(x, out):
+def pack_kernel(spot, x, *pieces):
     half = x.shape[1] // 2
-    for clip in range(x.shape[0]):
-        out[clip] = jnp.concatenate([x[clip, :half], x[clip, half:]], axis=1)
-
-
-def unpack_kernel(x, out):
-    half = x.shape[1]
-    width = x.shape[2] // 2
-    for clip in range(x.shape[0]):
-        out[clip, :half] = x[clip, :, :width]
-        out[clip, half:] = x[clip, :, width:]
-
-
-def gather_halves(x):
+    for step, piece in enumerate(pieces):
+        clip = spot[0] ^ step
+        piece[...] = jnp.concatenate([x[clip, :half], x[clip, half:]], axis=1)
+
+
+def unpack_pieces(spot, *refs):
+    out = refs[-1]
+    whole_array = len(refs) == 2
+    for k in range(out.shape[0]):
+        clip = k if whole_array else spot[0] ^ k
+        piece = refs[0][k] if whole_array else refs[k][...]
+        half, width = piece.shape[0], piece.shape[1] // 2
+        out[clip, :half] = piece[:, :width]
+        out[clip, half:] = piece[:, width:]
+
+
+def gather_halves(spot, pieces, x):
+    for step, piece in enumerate(pieces):
+        x[spot[0] ^ step] = piece[...]
     devices, _, lanes = x.shape
     width = lanes // 2
     low, high = [], []
@@ -386,7 +394,8 @@
         )
 
 
-def slow_enter(x, w_time, w_project, own, narrow, project):
+def slow_enter(spot, w_time, w_project, *refs):
+    *pieces, own, narrow, project, packed = refs
     i = pl.program_id(0)
     frames = narrow.shape[0] - 2
 
@@ -394,7 +403,7 @@
     def _():
         narrow[...] = jnp.zeros_like(narrow)
 
-    for half, frame in enumerate(gather_halves(x)):
+    for half, frame in enumerate(gather_halves(spot, pieces, packed)):
         own[half, 0] = frame
         depth = frame.shape[1]
         project[half, 0] = dot(frame, w_project[:depth]).astype(BF)
@@ -422,7 +431,7 @@
     _, _, scale, shift = norm_terms(gl[...], params[...], count[0, 0])
     mask = clip_mask(side[0], 256)
     for t in range(frames):
-        act[t] = (mask * silu(lateral[t] * scale + shift)).astype(BF)
+        act[t] = (mask * silu_half(lateral[t] * scale + shift)).astype(BF)
     width = act.shape[2]
     for t in range(frames):
         taps = [k for k in range(3) if 0 <= t - 1 + k < frames]
@@ -436,56 +445,79 @@
 
 def middle_enter(count, side, pre, gn, params, w, act, out, stats, acc, win):
     i = pl.program_id(0)
+    frames = pre.shape[0]
     _, _, scale, shift = norm_terms(gn[...], params[...], count[0, 0])
     mask = clip_mask(side[0], 256)
-    a = mask * silu(pre[0] * scale + shift)
-    act[0] = a.astype(BF)
-    fill_windows(win, plane_windows(a, 16), 16)
-    v = plane_dot(win, w, 256, 16)
-    out[0] = v
-    mv = mask * v
-    add_stats(acc, i == 0, (0, 1), (col_sum(mv), col_sum(mv * v)))
+
+    @pl.when(i == 0)
+    def _():
+        clear_gaps(win, frames, 16)
+
+    for frame in range(frames):
+        a = mask * silu_half(pre[frame] * scale + shift)
+        act[frame] = a.astype(BF)
+        fill_windows(win, a, 16 + 272 * frame, 16)
+    v = plane_dot(win, w, frames, 16)
+    total, square = None, None
+    for frame in range(frames):
+        part = v[272 * frame : 272 * frame + 256]
+        out[frame] = part
+        masked = mask * part
+        total = masked if total is None else total + masked
+        square = masked * part if square is None else square + masked * part
+    add_stats(acc, i == 0, (0, 1), (col_sum(total), col_sum(square)))
     send_stats(i == pl.num_programs(0) - 1, acc, stats)
 
 
+def flat(ref):
+    block = ref[...]
+    return block.reshape(block.shape[0] * block.shape[1], block.shape[2])
+
+
 def wide_enter(count, side, pre, gm, params, base, lateral, w, w_project, act, project, acc):
     i = pl.program_id(0)
     _, _, scale, shift = norm_terms(gm[...], params[...], count[0, 0])
-    mask = clip_mask(side[0], 256)
-    a = (mask * silu(pre[0] * scale + shift)).astype(BF)
-    act[0] = a
+    rows = pre.shape[0] * pre.shape[1]
+    mask = clip_mask(side[0], rows)
+    a = (mask * silu_half(flat(pre) * scale + shift)).astype(BF)
+    act[...] = a.reshape(act.shape)
     v = dot(a, w[...])
-    p = base[0].astype(F32) + dot(lateral[0], w_project[...])
-    project[0] = p.astype(BF)
+    p = flat(base).astype(F32) + dot(flat(lateral), w_project[...])
+    project[...] = p.astype(BF).reshape(project.shape)
     mp = mask * p
     add_stats(
         acc, i == 0, (0, 1, 2, 3), (col_sum(v), col_sum(v * v), col_sum(mp), col_sum(mp * p))
     )
 
 
-def wide_out(count, side, act, project, cot, g, params_w, params_p, w, result, grad, acc):
+def wide_out(count, side, spot, act, project, g, params_w, params_p, w, *refs):
+    devices = (len(refs) - 3) // 2
+    cots, pieces, (grad, acc, packed) = refs[:devices], refs[devices : 2 * devices], refs[2 * devices :]
     i = pl.program_id(0)
     c = count[0, 0]
     gathered = g[...]
-    mean_w, _, scale_w, shift_w = norm_terms(gathered[:, 0:2], params_w[...], c)
-    mean_p, _, scale_p, shift_p = norm_terms(gathered[:, 2:4], params_p[...], c)
+    _, _, scale_w, shift_w = norm_terms(gathered[:, 0:2], params_w[...], c)
+    _, _, scale_p, shift_p = norm_terms(gathered[:, 2:4], params_p[...], c)
     mask = clip_mask(side[0], 256)
+    half_mask = 0.5 * mask
     shift = shift_w + shift_p
     halves = []
     sums = [None, None, None]
-    for half, cot_half in enumerate(gather_halves(cot)):
+    for half, cot_half in enumerate(gather_halves(spot, cots, packed)):
         v = dot(act[half, 0], w[...])
         p = project[half, 0].astype(F32)
-        u = v * scale_w + p * scale_p + shift
-        gate = logistic(u)
-        s = u * gate
+        u = v * scale_w + (p * scale_p + shift)
+        h = 1.0 + jnp.tanh(u)
+        s = u * h
         halves.append((mask * s).astype(BF))
-        e = mask * cot_half.astype(F32) * (gate + s * (1.0 - gate))
+        e = (half_mask * cot_half.astype(F32)) * (h + s * (2.0 - h))
         grad[half, 0] = e
-        for k, value in enumerate((e, e * (v - mean_w), e * (p - mean_p))):
+        for k, value in enumerate((e, e * v, e * p)):
             value = col_sum(value)
             sums[k] = value if sums[k] is None else sums[k] + value
-    scatter_halves(halves[0], halves[1], result)
+    scatter_halves(halves[0], halves[1], packed)
+    for step, piece in enumerate(pieces):
+        piece[...] = packed[spot[0] ^ step]
     add_stats(acc, i == 0, (0, 1, 2), sums)
 
 
@@ -496,15 +528,15 @@
     c = count[0, 0]
     mean_w, inv_w, _, _ = norm_terms(g[...][:, 0:2], params_w[...], c)
     a, b, d = back_terms(h[...][:, 0:2], params_w[...], c, mean_w, inv_w)
-    mean_m, _, scale_m, shift_m = norm_terms(gm[...], params_m[...], c)
-    mask = clip_mask(side[0], 256)
-    s = act[0]
+    _, _, scale_m, shift_m = norm_terms(gm[...], params_m[...], c)
+    mask = clip_mask(side[0], pre.shape[0] * pre.shape[1])
+    s = flat(act)
     v = dot(s, w[...])
-    low = (mask * (grad[0] * a + v * b + d)).astype(BF)
-    p = pre[0]
-    e = dot_nt(low, w[...]) * mask * silu_slope(p * scale_m + shift_m)
-    out[0] = e
-    add_stats(acc, i == 0, (0, 1), (col_sum(e), col_sum(e * (p - mean_m))))
+    low = (mask * (flat(grad) * a + v * b + d)).astype(BF)
+    p = flat(pre)
+    e = dot_nt(low, w[...]) * (0.5 * mask * slope_half(p * scale_m + shift_m))
+    out[...] = e.reshape(out.shape)
+    add_stats(acc, i == 0, (0, 1), (col_sum(e), col_sum(e * p)))
     send_stats(i == pl.num_programs(0) - 1, acc, stats)
 
     @pl.when(i == 0)
@@ -527,17 +559,17 @@
     rows = h[...]
     total = jnp.concatenate([rows[:, 0:1], rows[:, 2:3]], axis=1)
     a, b, d = back_terms(total, params_p[...], c, mean_p, inv_p)
-    mask = clip_mask(side[0], 256)
-    low = (mask * (grad[0] * a + project[0].astype(F32) * b + d)).astype(BF)
-    joined[0] = dot_nt(low, w[...]).astype(BF)
+    mask = clip_mask(side[0], grad.shape[0] * grad.shape[1])
+    low = (mask * (flat(grad) * a + flat(project).astype(F32) * b + d)).astype(BF)
+    joined[...] = dot_nt(low, w[...]).astype(BF).reshape(joined.shape)
 
     @pl.when(i == 0)
     def _():
         w_acc[...] = jnp.zeros_like(w_acc)
 
     width = own.shape[2]
-    w_acc[0:width, :] += dot_tn(own[0], low)
-    w_acc[width:, :] += dot_tn(lateral[0], low)
+    w_acc[0:width, :] += dot_tn(flat(own), low)
+    w_acc[width:, :] += dot_tn(flat(lateral), low)
 
     @pl.when(i == pl.num_programs(0) - 1)
     def _():
@@ -548,31 +580,50 @@
     count, side, grad, pre_m, gm, hm, params_m, w, pre_n, gn, params_n, low_out, out, stats, acc, win
 ):
     i = pl.program_id(0)
+    frames = grad.shape[0]
     c = count[0, 0]
     mean_m, inv_m, _, _ = norm_terms(gm[...], params_m[...], c)
     a, b, d = back_terms(hm[...], params_m[...], c, mean_m, inv_m)
-    mean_n, _, scale_n, shift_n = norm_terms(gn[...], params_n[...], c)
+    _, _, scale_n, shift_n = norm_terms(gn[...], params_n[...], c)
     mask = clip_mask(side[0], 256)
-    low = mask * (grad[0] * a + pre_m[0] * b + d)
-    low_out[0] = low.astype(BF)
-    fill_windows(win, plane_windows(low, 16), 16)
-    p = pre_n[0]
-    e = plane_dot(win, w, 256, 16) * mask * silu_slope(p * scale_n + shift_n)
-    out[0] = e
-    add_stats(acc, i == 0, (0, 1), (col_sum(e), col_sum(e * (p - mean_n))))
+
+    @pl.when(i == 0)
+    def _():
+        clear_gaps(win, frames, 16)
+
+    for frame in range(frames):
+        low = mask * (grad[frame] * a + pre_m[frame] * b + d)
+        low_out[frame] = low.astype(BF)
+        fill_windows(win, low, 16 + 272 * frame, 16)
+    back = plane_dot(win, w, frames, 16)
+    half_mask = 0.5 * mask
+    total, cross = None, None
+    for frame in range(frames):
+        p = pre_n[frame]
+        e = back[272 * frame : 272 * frame + 256] * (half_mask * slope_half(p * scale_n + shift_n))
+        out[frame] = e
+        total = e if total is None else total + e
+        cross = e * p if cross is None else cross + e * p
+    add_stats(acc, i == 0, (0, 1), (col_sum(total), col_sum(cross)))
     send_stats(i == pl.num_programs(0) - 1, acc, stats)
 
 
-def plane_weight(act, low, w_grad, w_acc, win):
-    i = pl.program_id(0)
+def plane_weight(act, low, w_grad, w_acc, win, low_win):
+    i = pl.program_id(0)
+    frames = act.shape[0]
 
     @pl.when(i == 0)
     def _():
         w_acc[...] = jnp.zeros_like(w_acc)
-
-    fill_windows(win, plane_windows(act[0].astype(F32), 16), 16)
+        clear_gaps(win, frames, 16)
+        low_win[...] = jnp.zeros_like(low_win)
+
+    for frame in range(frames):
+        fill_windows(win, act[frame].astype(F32), 16 + 272 * frame, 16)
+        low_win[272 * frame : 272 * frame + 256, :] = low[frame]
+    rows = low_win.shape[0]
     for tap in range(3):
-        w_acc[tap] += dot_tn(win[16 * tap : 16 * tap + 256, :], low[0])
+        w_acc[tap] += dot_tn(win[16 * tap : 16 * tap + rows, :], low_win[...])
 
     @pl.when(i == pl.num_programs(0) - 1)
     def _():
@@ -598,24 +649,25 @@
         for t in range(frames):
             low[t + 1] = (mask * (grad[t] * a + pre_n[t] * b + d)).astype(BF)
 
-    mean_l, _, scale_l, shift_l = norm_terms(gl[...], params_l[...], c)
-    halves = []
-    sums = [None, None]
+    _, _, scale_l, shift_l = norm_terms(gl[...], params_l[...], c)
+    other = i + frames // 2
+    j = jnp.concatenate([joined[0, 0], joined[1, 0]], axis=0).astype(F32)
+    for tap in range(3):
+        both = jnp.concatenate([low[i + 2 - tap], low[other + 2 - tap]], axis=0)
+        j = j + dot_nt(both, w[tap])
+    slow_width = j.shape[1] - out.shape[3]
+    top = j[:, :slow_width].astype(BF)
+    scatter_halves(top[0:256], top[256:512], slow)
+    half_mask = 0.5 * mask
+    total, cross = None, None
     for half in range(2):
-        t = i + half * (frames // 2)
-        j = joined[half, 0].astype(F32)
-        for tap in range(3):
-            j = j + dot_nt(low[t + 2 - tap], w[tap])
-        slow_width = j.shape[1] - out.shape[3]
-        halves.append(j[:, :slow_width].astype(BF))
         p = pre_l[half, 0]
-        e = j[:, slow_width:] * mask * silu_slope(p * scale_l + shift_l)
+        part = j[256 * half : 256 * half + 256, slow_width:]
+        e = part * (half_mask * slope_half(p * scale_l + shift_l))
         out[half, 0] = e
-        for k, value in enumerate((e, e * (p - mean_l))):
-            value = col_sum(value)
-            sums[k] = value if sums[k] is None else sums[k] + value
-    scatter_halves(halves[0], halves[1], slow)
-    add_stats(acc, i == 0, (0, 1), sums)
+        total = e if total is None else total + e
+        cross = e * p if cross is None else cross + e * p
+    add_stats(acc, i == 0, (0, 1), (col_sum(total), col_sum(cross)))
     send_stats(i == steps - 1, acc, stats)
 
 
@@ -627,18 +679,21 @@
     mask = clip_mask(side[0], 256)
     for t in range(frames):
         low[t] = (mask * (grad[t] * a + pre_l[t] * b + d)).astype(BF)
-    for t in range(frames):
-        here = low[t]
-        out[4 * t] = dot_nt(here, w[2]).astype(BF)
-        out[4 * t + 1] = dot_nt(here, w[3]).astype(BF)
-        third = dot_nt(here, w[4])
-        if t + 1 < frames:
-            after = low[t + 1]
-            third = third + dot_nt(after, w[0])
-            out[4 * t + 3] = dot_nt(after, w[1]).astype(BF)
-        else:
-            out[4 * t + 3] = jnp.zeros(out.shape[1:], BF)
-        out[4 * t + 2] = third.astype(BF)
+    for t in range(0, frames, 2):
+        pair = jnp.concatenate([low[t], low[t + 1]], axis=0)
+        last = t + 2 == frames
+        after = jnp.zeros(low.shape[1:], BF) if last else low[t + 2]
+        shifted = jnp.concatenate([low[t + 1], after], axis=0)
+        results = (
+            dot_nt(pair, w[2]),
+            dot_nt(pair, w[3]),
+            dot_nt(pair, w[4]) + dot_nt(shifted, w[0]),
+            dot_nt(shifted, w[1]),
+        )
+        for k, result in enumerate(results):
+            result = result.astype(BF)
+            out[4 * t + k] = result[0:256]
+            out[4 * t + 4 + k] = result[256:512]
 
 
 def lateral_weight_back(fast, low, w_grad, w_acc):
@@ -671,18 +726,30 @@
                 begin = end
 
 
+def lateral_merge(place, mine, other, *outs):
+    rows = outs[0].shape[0]
+    near = len(outs)
+    for step, out in enumerate(outs):
+        begin = pl.multiple_of((place[0] * near + (place[1] ^ step)) * rows, 16)
+        part = pl.ds(begin, rows)
+        out[...] = (mine[part, :].astype(F32) + other[part, :].astype(F32)).astype(BF)
+
+
 def weight_split(place, *refs):
     project, expand, spatial, time, lateral, full = refs[-6:]
     pieces = refs[:-6]
     near = 4
-    rows = pieces[0].shape[0]
+    share = lateral.shape[0] // len(pieces)
+    rows = pieces[0].shape[0] - share
     for k, piece in enumerate(pieces):
         half = place[0] if k < near else 1 - place[0]
         if len(pieces) == near:
             half = 0
         spot = place[1] ^ (k % near)
         begin = pl.multiple_of((half * near + spot) * rows, 16)
-        full[pl.ds(begin, rows), :] = piece[...]
+        full[pl.ds(begin, rows), :] = piece[:rows, :]
+        begin = pl.multiple_of((half * near + spot) * share, 8)
+        lateral[pl.ds(begin, share), :] = piece[rows:, :].astype(F32)
     begin = 0
     for out in (project, expand):
         height, width = out.shape[0], full.shape[1]
@@ -699,7 +766,6 @@
     for tap in range(3):
         time[tap, height:] = full[begin : begin + rest, :].astype(F32)
         begin += rest
-    lateral[...] = full[begin : begin + lateral.shape[0], :].astype(F32)
 
 
 def per_device(
@@ -777,31 +843,39 @@
     w_middle = slow_spatial.reshape(3, 3 * b_s, b_s)
     w_middle_back = slow_spatial[::-1, ::-1].transpose(0, 1, 3, 2).reshape(3, 3 * b_s, b_s)
 
+    spot = place.reshape(1)
+    piece_shape = (half * cells, 2 * slow_in.shape[4])
+    piece_spec = pl.BlockSpec((cells, piece_shape[1]), lambda i: (i, 0))
+    flat_shape = (clips, frames * cells, slow_in.shape[4])
+
     def pack(array):
-        rows = frames * cells
-        width = array.shape[4]
-        flat = array.reshape(clips, rows, width)
-        return launch(
-            pack_kernel,
-            "pack",
-            (packs,),
-            [(flat, pl.BlockSpec((GROUPS, rows, width), lambda i: (i, 0, 0)))],
-            [((clips, rows // 2, 2 * width), BF, pl.BlockSpec((GROUPS, rows // 2, 2 * width), lambda i: (i, 0, 0)))],
-        )[0]
-
-    def unpack(array, shape):
-        rows = frames * cells
-        width = shape[4]
-        return launch(
-            unpack_kernel,
+        flat = array.reshape(flat_shape)
+        out = (piece_shape, BF, pl.BlockSpec(piece_shape, lambda *_: (0, 0)))
+        return launch(pack_kernel, "pack", (), [(spot, smem), (flat, whole(flat))], [out] * wa_count)
+
+    def exchange_pieces(pieces, begin=0, end=wa_count):
+        return [
+            lax.ppermute(pieces[step], "wa", [(i, i ^ step) for i in range(wa_count)])
+            if step
+            else pieces[0]
+            for step in range(begin, end)
+        ]
+
+    def gate(arrays, ready):
+        return list(launch(lambda: None, "gate", (), [], [], after=(ready,), carry=tuple(arrays)))
+
+    def unpack(pieces):
+        (flat,) = launch(
+            unpack_pieces,
             "unpack",
-            (packs,),
-            [(array, pl.BlockSpec((GROUPS, rows // 2, 2 * width), lambda i: (i, 0, 0)))],
-            [((clips, rows, width), BF, pl.BlockSpec((GROUPS, rows, width), lambda i: (i, 0, 0)))],
-        )[0].reshape(shape)
-
-    slow_got = exchange(pack(slow_in))
-    cot_got = exchange(pack(slow_cot))
+            (),
+            [(spot, smem)] + [(piece, whole(piece)) for piece in pieces],
+            [(flat_shape, BF, pl.BlockSpec(flat_shape, lambda *_: (0, 0, 0)))],
+        )
+        return flat.reshape(slow_in.shape)
+
+    slow_pieces = exchange_pieces(pack(slow_in))
+    cot_out = pack(slow_cot)
 
     x = fast_in.reshape(clips, 2, cells, c_f)
     x_spec = pl.BlockSpec((GROUPS, 2, cells, c_f), lambda i: (i, 0, 0, 0))
@@ -812,7 +886,8 @@
     sides_spec = pl.BlockSpec((1, 1, LANES), lambda i: (i, 0, 0))
     stat8 = ((devices, 8, LANES), F32, pl.BlockSpec((devices, 8, LANES), lambda *_: (0, 0, 0)))
     acc8 = pltpu.VMEM((8, LANES), F32)
-    fast_win = pltpu.VMEM((cells + 32, 3 * LANES), BF)
+    fast_win = window_shape(2, 3 * LANES)
+    fast_low = pltpu.VMEM((528, LANES), BF)
 
     y, to_next, to_prev = launch(
         fast_first,
@@ -832,7 +907,7 @@
         [(y, packed_spec), (from_prev, rim_spec), (from_next, rim_spec), (lane_sides, sides_spec)],
         [(packed_shape, F32, packed_spec), stat8],
         [acc8],
-        after=(slow_got,),
+        after=tuple(slow_pieces[1:4]),
     )
     g1 = gather_stats(s1)
     act1, pre2, s2 = launch(
@@ -849,6 +924,7 @@
         ],
         [(packed_shape, BF, packed_spec), (packed_shape, F32, packed_spec), stat8],
         [acc8, fast_win],
+        after=tuple(slow_pieces[4:8]),
     )
     g2 = gather_stats(s2)
     act2, s3 = launch(
@@ -865,6 +941,7 @@
         ],
         [(packed_shape, BF, packed_spec), stat8],
         [acc8],
+        after=tuple(slow_pieces[8:12]),
     )
     g3 = gather_stats(s3)
     (fast_result,) = launch(
@@ -881,6 +958,7 @@
             (w_widen, whole(w_widen)),
         ],
         [(x.shape, BF, x_spec)],
+        after=tuple(slow_pieces[12:]),
     )
 
     fast_got = exchange(fast_result.reshape(clips, 2 * cells, c_f)).reshape(4 * frames, cells, c_f)
@@ -888,26 +966,11 @@
     def stat(rows, width):
         return ((devices, rows, width), F32, pl.BlockSpec((devices, rows, width), lambda *_: (0, 0, 0)))
 
-    pre_l, s_l = launch(
-        lateral_enter,
-        "lateral_enter",
-        (),
-        [(own_side, smem), (fast_got, whole(fast_got)), (lateral_weight, whole(lateral_weight))],
-        [
-            ((frames, cells, c_l), F32, pl.BlockSpec((frames, cells, c_l), lambda *_: (0, 0, 0))),
-            stat(2, c_l),
-        ],
-        [pltpu.VMEM((2, c_l), F32)],
-    )
-    g_l = gather_stats(s_l)
-
-    got_spec = pl.BlockSpec((wa_count, cells, LANES), lambda i: (0, i, 0))
-
     def pair_spec(width):
         return pl.BlockSpec((2, 1, cells, width), lambda i: (0, i, 0, 0))
 
-    def frame_spec(width):
-        return pl.BlockSpec((1, cells, width), lambda i: (i, 0, 0))
+    def frame_spec(width, count):
+        return pl.BlockSpec((count, cells, width), lambda i: (i, 0, 0))
 
     def pairs(array):
         return array.reshape((2, half) + array.shape[1:])
@@ -916,7 +979,8 @@
         slow_enter,
         "slow_enter",
         (half,),
-        [(slow_got, got_spec), (slow_reduce, whole(slow_reduce)), (slow_project, whole(slow_project))],
+        [(spot, smem), (slow_reduce, whole(slow_reduce)), (slow_project, whole(slow_project))]
+        + [(piece, piece_spec) for piece in slow_pieces],
         [
             ((2, half, cells, c_s), BF, pair_spec(c_s)),
             (
@@ -926,10 +990,26 @@
             ),
             ((2, half, cells, c_s), BF, pair_spec(c_s)),
         ],
+        [pltpu.VMEM((wa_count, cells, LANES), BF)],
         flops=2 * frames * cells * c_s * (3 * b_s + c_s),
     )
     own = own.reshape(frames, cells, c_s)
     base_p = base_p.reshape(frames, cells, c_s)
+    pre_l, s_l = launch(
+        lateral_enter,
+        "lateral_enter",
+        (),
+        [(own_side, smem), (fast_got, whole(fast_got)), (lateral_weight, whole(lateral_weight))],
+        [
+            ((frames, cells, c_l), F32, pl.BlockSpec((frames, cells, c_l), lambda *_: (0, 0, 0))),
+            stat(2, c_l),
+        ],
+        [pltpu.VMEM((2, c_l), F32)],
+        after=(base_n,),
+    )
+    g_l = gather_stats(s_l)
+    cot_pieces = exchange_pieces(gate(cot_out, g_l))
+
     lateral_act, pre_n, s_n = launch(
         narrow_enter,
         "narrow_enter",
@@ -951,118 +1031,124 @@
         [pltpu.VMEM((2, b_s), F32)],
     )
     g_n = gather_stats(s_n)
-    slow_win = pltpu.VMEM((cells + 32, 3 * b_s), BF)
+    slow_win = window_shape(4, 3 * b_s)
+    slow_low = pltpu.VMEM((4 * 272 - 16, b_s), BF)
     act_n, pre_m, s_m = launch(
         middle_enter,
         "middle_enter",
-        (frames,),
+        (frames // 4,),
         [
             (slow_count, smem),
             (own_side, smem),
-            (pre_n, frame_spec(b_s)),
+            (pre_n, frame_spec(b_s, 4)),
             (g_n, whole(g_n)),
             (slow_reduce_norm, whole(slow_reduce_norm)),
             (w_middle, whole(w_middle)),
         ],
         [
-            ((frames, cells, b_s), BF, frame_spec(b_s)),
-            ((frames, cells, b_s), F32, frame_spec(b_s)),
+            ((frames, cells, b_s), BF, frame_spec(b_s, 4)),
+            ((frames, cells, b_s), F32, frame_spec(b_s, 4)),
             stat(2, b_s),
         ],
         [pltpu.VMEM((2, b_s), F32), slow_win],
+        after=tuple(cot_pieces[1:5]),
     )
     g_m = gather_stats(s_m)
     act_m, project, s_w = launch(
         wide_enter,
         "wide_enter",
-        (frames,),
+        (frames // 2,),
         [
             (slow_count, smem),
             (own_side, smem),
-            (pre_m, frame_spec(b_s)),
+            (pre_m, frame_spec(b_s, 2)),
             (g_m, whole(g_m)),
             (slow_spatial_norm, whole(slow_spatial_norm)),
-            (base_p, frame_spec(c_s)),
-            (lateral_act, frame_spec(c_l)),
+            (base_p, frame_spec(c_s, 2)),
+            (lateral_act, frame_spec(c_l, 2)),
             (slow_expand, whole(slow_expand)),
             (slow_project, pl.BlockSpec((c_l, c_s), lambda i: (c_s // c_l, 0))),
         ],
         [
-            ((frames, cells, b_s), BF, frame_spec(b_s)),
-            ((frames, cells, c_s), BF, frame_spec(c_s)),
+            ((frames, cells, b_s), BF, frame_spec(b_s, 2)),
+            ((frames, cells, c_s), BF, frame_spec(c_s, 2)),
             ((4, c_s), F32, pl.BlockSpec((4, c_s), lambda *_: (0, 0))),
         ],
+        after=tuple(cot_pieces[5:10]),
     )
     g_w = gather_wide(s_w)
-    out_packed, wide_grad, t_w = launch(
+    *out_pieces, wide_grad, t_w = launch(
         wide_out,
         "wide_out",
         (half,),
         [
             (slow_count, smem),
             (own_side, smem),
+            (spot, smem),
             (pairs(act_m), pair_spec(b_s)),
             (pairs(project), pair_spec(c_s)),
-            (cot_got, got_spec),
             (g_w, whole(g_w)),
             (slow_expand_norm, whole(slow_expand_norm)),
             (slow_project_norm, whole(slow_project_norm)),
             (slow_expand, whole(slow_expand)),
-        ],
-        [
-            ((wa_count, half * cells, LANES), BF, got_spec),
+            *[(piece, piece_spec) for piece in cot_pieces],
+        ],
+        [
+            *[(piece_shape, BF, piece_spec)] * wa_count,
             ((2, half, cells, c_s), F32, pair_spec(c_s)),
             ((4, c_s), F32, pl.BlockSpec((4, c_s), lambda *_: (0, 0))),
         ],
+        [pltpu.VMEM((wa_count, cells, LANES), BF)],
     )
     wide_grad = wide_grad.reshape(frames, cells, c_s)
     h_w = gather_wide(t_w)
-    result_got = exchange(out_packed)
-    slow_result = unpack(result_got, slow_in.shape)
+    result_pieces = exchange_pieces(out_pieces)
+    slow_result = unpack(result_pieces)
 
     middle_grad, expand_w_grad, t_m = launch(
         middle_back,
         "middle_back",
-        (frames,),
+        (frames // 2,),
         [
             (slow_count, smem),
             (own_side, smem),
-            (wide_grad, frame_spec(c_s)),
-            (act_m, frame_spec(b_s)),
+            (wide_grad, frame_spec(c_s, 2)),
+            (act_m, frame_spec(b_s, 2)),
             (g_w, whole(g_w)),
             (h_w, whole(h_w)),
             (slow_expand_norm, whole(slow_expand_norm)),
             (slow_expand, whole(slow_expand)),
-            (pre_m, frame_spec(b_s)),
+            (pre_m, frame_spec(b_s, 2)),
             (g_m, whole(g_m)),
             (slow_spatial_norm, whole(slow_spatial_norm)),
         ],
         [
-            ((frames, cells, b_s), F32, frame_spec(b_s)),
+            ((frames, cells, b_s), F32, frame_spec(b_s, 2)),
             ((c_s, b_s), BF, pl.BlockSpec((c_s, b_s), lambda *_: (0, 0))),
             stat(2, b_s),
         ],
         [pltpu.VMEM((2, b_s), F32), pltpu.VMEM((b_s, c_s), F32)],
+        after=tuple(result_pieces[1:3]),
     )
     h_m = gather_stats(t_m)
     joined_part, project_w_grad = launch(
         project_back,
         "project_back",
-        (frames,),
+        (frames // 2,),
         [
             (slow_count, smem),
             (own_side, smem),
-            (wide_grad, frame_spec(c_s)),
-            (project, frame_spec(c_s)),
+            (wide_grad, frame_spec(c_s, 2)),
+            (project, frame_spec(c_s, 2)),
             (g_w, whole(g_w)),
             (h_w, whole(h_w)),
             (slow_project_norm, whole(slow_project_norm)),
-            (own, frame_spec(c_s)),
-            (lateral_act, frame_spec(c_l)),
+            (own, frame_spec(c_s, 2)),
+            (lateral_act, frame_spec(c_l, 2)),
             (slow_project, whole(slow_project)),
         ],
         [
-            ((frames, cells, c_cat), BF, frame_spec(c_cat)),
+            ((frames, cells, c_cat), BF, frame_spec(c_cat, 2)),
             ((c_cat * c_s // b_s, b_s), BF, pl.BlockSpec((c_cat * c_s // b_s, b_s), lambda *_: (0, 0))),
         ],
         [pltpu.VMEM((c_cat, c_s), F32)],
@@ -1071,35 +1157,36 @@
     middle_low, narrow_grad, t_n = launch(
         narrow_back,
         "narrow_back",
-        (frames,),
+        (frames // 4,),
         [
             (slow_count, smem),
             (own_side, smem),
-            (middle_grad, frame_spec(b_s)),
-            (pre_m, frame_spec(b_s)),
+            (middle_grad, frame_spec(b_s, 4)),
+            (pre_m, frame_spec(b_s, 4)),
             (g_m, whole(g_m)),
             (h_m, whole(h_m)),
             (slow_spatial_norm, whole(slow_spatial_norm)),
             (w_middle_back, whole(w_middle_back)),
-            (pre_n, frame_spec(b_s)),
+            (pre_n, frame_spec(b_s, 4)),
             (g_n, whole(g_n)),
             (slow_reduce_norm, whole(slow_reduce_norm)),
         ],
         [
-            ((frames, cells, b_s), BF, frame_spec(b_s)),
-            ((frames, cells, b_s), F32, frame_spec(b_s)),
+            ((frames, cells, b_s), BF, frame_spec(b_s, 4)),
+            ((frames, cells, b_s), F32, frame_spec(b_s, 4)),
             stat(2, b_s),
         ],
         [pltpu.VMEM((2, b_s), F32), slow_win],
+        after=tuple(result_pieces[3:7]),
     )
     h_n = gather_stats(t_n)
     (spatial_w_grad,) = launch(
         plane_weight,
         "plane_weight",
-        (frames,),
-        [(act_n, frame_spec(b_s)), (middle_low, frame_spec(b_s))],
+        (frames // 4,),
+        [(act_n, frame_spec(b_s, 4)), (middle_low, frame_spec(b_s, 4))],
         [((3, 3 * b_s, b_s), BF, pl.BlockSpec((3, 3 * b_s, b_s), lambda *_: (0, 0, 0)))],
-        [pltpu.VMEM((3, 3 * b_s, b_s), F32), slow_win],
+        [pltpu.VMEM((3, 3 * b_s, b_s), F32), slow_win, slow_low],
         flops=18 * frames * cells * b_s * b_s,
     )
     narrow_low, grad_packed, lateral_grad, t_l = launch(
@@ -1126,17 +1213,21 @@
                 BF,
                 pl.BlockSpec((frames + 2, cells, b_s), lambda *_: (0, 0, 0)),
             ),
-            ((wa_count, half * cells, LANES), BF, got_spec),
+            (
+                (wa_count,) + piece_shape,
+                BF,
+                pl.BlockSpec((wa_count, cells, piece_shape[1]), lambda i: (0, i, 0)),
+            ),
             ((2, half, cells, c_l), F32, pair_spec(c_l)),
             stat(2, c_l),
         ],
         [pltpu.VMEM((2, c_l), F32)],
-        after=(result_got,),
+        after=tuple(result_pieces[7:13]),
     )
     lateral_grad = lateral_grad.reshape(frames, cells, c_l)
     h_l = gather_stats(t_l)
     grad_got = exchange(grad_packed)
-    slow_grad = unpack(grad_got, slow_in.shape)
+    slow_grad = unpack([grad_got])
 
     def time_weight(values):
         flat = values.reshape(frames * cells, values.shape[2])
@@ -1172,6 +1263,7 @@
             ((frames, cells, c_l), BF, pl.BlockSpec((frames, cells, c_l), lambda *_: (0, 0, 0))),
             ((4 * frames, cells, c_f), BF, pl.BlockSpec((4 * frames, cells, c_f), lambda *_: (0, 0, 0))),
         ],
+        after=tuple(result_pieces[13:]),
     )
     back_got = exchange(frames_back.reshape(wa_count, 2 * cells, c_f)).reshape(x.shape)
     (lateral_w_grad,) = launch(
@@ -1191,7 +1283,6 @@
             spatial_w_grad,
             time_weight(own),
             time_weight(lateral_act),
-            lateral_w_grad,
         )
     ]
     sizes = [part.shape[0] for part in weight_parts]
@@ -1216,7 +1307,34 @@
     else:
         weights = jnp.concatenate(weight_parts, axis=0)
     first_stage = lax.psum_scatter(weights, "wa", axis_index_groups=inner, tiled=True)
-    second_stage = lax.psum(first_stage, "wa", axis_index_groups=outer)
+    spot_in = place % near
+    if paired:
+        other = lax.ppermute(lateral_w_grad, "dp", swap)
+        share = lateral_w_grad.shape[0] // (2 * near)
+        out = ((share, c_l), BF, pl.BlockSpec((share, c_l), lambda *_: (0, 0)))
+        lateral_out = launch(
+            lateral_merge,
+            "lateral_merge",
+            (),
+            [(jnp.stack([core, spot_in]), smem)]
+            + [(part, whole(part)) for part in (lateral_w_grad, other)],
+            [out] * near,
+        )
+    else:
+        share = lateral_w_grad.shape[0] // near
+        lateral_out = [
+            lax.dynamic_slice_in_dim(lateral_w_grad, (spot_in ^ step) * share, share)
+            for step in range(near)
+        ]
+    lateral_sum = lateral_out[0].astype(F32)
+    for step in range(1, near):
+        got = lax.ppermute(lateral_out[step], "wa", [(i, i ^ step) for i in range(wa_count)])
+        lateral_sum = lateral_sum + got.astype(F32)
+    second_stage = lax.psum(
+        jnp.concatenate([first_stage, lateral_sum.astype(BF)], axis=0),
+        "wa",
+        axis_index_groups=outer,
+    )
 
     cot = fast_cot.reshape(x.shape)
     fast_grad3, t3 = launch(
@@ -1236,7 +1354,6 @@
         ],
         [(x.shape, F32, x_spec), stat8],
         [acc8],
-        after=(first_stage,),
     )
     h3 = gather_stats(t3)
     fast_grad2, widen_blocks, t2 = launch(
@@ -1263,8 +1380,13 @@
             stat8,
         ],
         [acc8],
+        after=(second_stage,),
     )
     h2 = gather_stats(t2)
+    pieces = [second_stage] + [
+        lax.ppermute(second_stage, "wa", [(i, i ^ step) for i in range(wa_count)])
+        for step in range(1, near)
+    ]
     fast_grad1, plane_blocks, t1 = launch(
         fast_back_plane,
         "fast_back_plane",
@@ -1292,7 +1414,8 @@
             ),
             stat8,
         ],
-        [acc8, fast_win],
+        [acc8, fast_win, fast_low],
+        after=tuple(pieces),
     )
     h1 = gather_stats(t1)
     (low1,) = launch(
@@ -1312,7 +1435,7 @@
     )
     low_prev = lax.ppermute(low1[1], "wa", forward)
     low_next = lax.ppermute(low1[0], "wa", backward)
-    fast_grad, first_blocks, second_stage = launch(
+    fast_grad, first_blocks = launch(
         fast_back_out,
         "fast_back_out",
         (packs,),
@@ -1333,17 +1456,24 @@
             ),
         ],
         after=(grad_got,),
-        carry=(second_stage,),
-    )
-    pieces = [second_stage] + [
-        lax.ppermute(second_stage, "wa", [(i, i ^ step) for i in range(wa_count)])
-        for step in range(1, near)
-    ]
+    )
+    expand_part = sum(widen_blocks[g, g * b_f : (g + 1) * b_f] for g in range(GROUPS))
+    plane_view = plane_blocks.reshape(3, 3, GROUPS, b_f, GROUPS, b_f)
+    spatial_part = sum(plane_view[:, :, g, :, g] for g in range(GROUPS))
+    first_view = first_blocks.reshape(GROUPS, c_f, 3, GROUPS, b_f)
+    reduce_part = sum(first_view[g, :, :, g] for g in range(GROUPS)).transpose(1, 0, 2)
+
+    small = jnp.concatenate(
+        [reduce_part.reshape(-1), spatial_part.reshape(-1), expand_part.reshape(-1)]
+    )
+    share = -(-small.shape[0] // (devices * LANES)) * LANES
+    padded = jnp.pad(small, (0, share * devices - small.shape[0])).reshape(devices, share // LANES, LANES)
+    mine = jnp.sum(gather_stats(padded), axis=0)
+    small_all = gather_stats(jnp.broadcast_to(mine[None], padded.shape)).reshape(-1)
     if paired:
         pieces = pieces + [lax.ppermute(piece, "dp", swap) for piece in pieces]
     else:
         pieces = [lax.psum(piece, "dp") for piece in pieces]
-
     final = [
         ((c_cat, c_s), F32),
         ((b_s, c_s), F32),
@@ -1362,19 +1492,6 @@
         ],
         [pltpu.VMEM((sum(sizes), b_s), BF)],
     )
-    expand_part = sum(widen_blocks[g, g * b_f : (g + 1) * b_f] for g in range(GROUPS))
-    plane_view = plane_blocks.reshape(3, 3, GROUPS, b_f, GROUPS, b_f)
-    spatial_part = sum(plane_view[:, :, g, :, g] for g in range(GROUPS))
-    first_view = first_blocks.reshape(GROUPS, c_f, 3, GROUPS, b_f)
-    reduce_part = sum(first_view[g, :, :, g] for g in range(GROUPS)).transpose(1, 0, 2)
-
-    small = jnp.concatenate(
-        [reduce_part.reshape(-1), spatial_part.reshape(-1), expand_part.reshape(-1)]
-    )
-    share = -(-small.shape[0] // (devices * LANES)) * LANES
-    padded = jnp.pad(small, (0, share * devices - small.shape[0])).reshape(devices, share // LANES, LANES)
-    mine = jnp.sum(gather_stats(padded), axis=0)
-    small_all = gather_stats(jnp.broadcast_to(mine[None], padded.shape)).reshape(-1)
     first_size, plane_size = reduce_part.size, spatial_part.size
     fast_reduce_grad = small_all[:first_size].reshape(fast_reduce.shape)
     fast_spatial_grad = small_all[first_size : first_size + plane_size].reshape(fast_spatial.shape)
@@ -1387,7 +1504,7 @@
             moment = moment.reshape(moment.shape[0], GROUPS, -1).sum(axis=1)
         mean = moment[0] / count[0, 0]
         inv = lax.rsqrt(moment[1] / count[0, 0] - mean * mean + EPSILON)
-        return jnp.stack([total[1] * inv, total[0]])
+        return jnp.stack([(total[1] - mean * total[0]) * inv, total[0]])
 
     h_project = jnp.concatenate([h_w[:, 0:1], h_w[:, 2:3]], axis=1)
     return (

time: 990 us -> 891 us (0.900)
  blocking collectives: 154 us -> 51.5 us
  waiting for transfers between devices: 404 us -> 304 us
  starting transfers between devices: 130 us -> 204 us
  local copies, waits for them, and re-layouts: 35 us -> 56.2 us
  other arithmetic: 12.1 us -> 24 us
    all_to_all x5 -> x3, waiting for transfers between devices: 308 us -> 57 us  [exchange(): return lax.all_to_all(array, 'wa', 0, 0, tiled=True)]
    ppermute x0 -> x49, starting transfers between devices: none -> 101 us  [the longest x45 96.9 us: exchange_pieces(): lax.ppermute(pieces[step], 'wa', [(i, i ^ step) for i in range(wa_count)])]
    ppermute x0 -> x49, waiting for transfers between devices: none -> 100 us  [the longest x45 86.2 us: exchange_pieces(): lax.ppermute(pieces[step], 'wa', [(i, i ^ step) for i in range(wa_count)])]
    all_to_all x3 -> x0, blocking collectives: 96.2 us -> none  [the longest x1 53.6 us: exchange(): return lax.all_to_all(array, 'wa', 0, 0, tiled=True)]
    ppermute x3, waiting for transfers between devices: 26.9 us -> 70.7 us  [per_device(): lax.ppermute(second_stage, 'wa', [(i, i ^ step) for i in range(wa_count)])]
    all_to_all x9 -> x11, starting transfers between devices: 80.5 us -> 46.2 us  [gather_stats(): return lax.all_to_all(copies, axes, 0, 0, tiled=True)]
    all_to_all x0 -> x2, starting transfers between devices: none -> 27.3 us  [gather_wide(): return lax.all_to_all(copies, 'wa', 0, 0, tiled=True)]
    all_to_all x9 -> x11, waiting for transfers between devices: 42.8 us -> 61.6 us  [gather_stats(): return lax.all_to_all(copies, axes, 0, 0, tiled=True)]
  transfers between devices with their start and end apart: 35 -> 85, of which waited for: 22 -> 28; matrix products, arithmetic and copies ran while one was open for 4% -> 6% of each run, Pallas kernels for 10% -> 20%
where the time goes in v2:
time: 891 us; the launch traced here: 879 us
  waiting for transfers between devices  304 us (34%)
  Pallas kernels  218 us (24%)
  starting transfers between devices  204 us (23%)
  local copies, waits for them, and re-layouts  56.2 us (6%)
  blocking collectives  51.5 us (6%)
  other arithmetic  24 us (3%)
  between operations  16.1 us (2%)
    pallas_call x31, Pallas kernels, launch(): pl.pallas_call(kernel, name=name, grid=grid, in_specs=[spec for _, spec i...  218 us
    ppermute x45, starting transfers between devices, exchange_pieces(): lax.ppermute(pieces[step], 'wa', [(i, i ^ step) for i in range(wa_count)])  96.9 us
    ppermute x45, waiting for transfers between devices, exchange_pieces(): lax.ppermute(pieces[step], 'wa', [(i, i ^ step) for i in range(wa_count)])  86.2 us
    ppermute x3, waiting for transfers between devices, per_device(): lax.ppermute(second_stage, 'wa', [(i, i ^ step) for i in range(wa_count)])  70.7 us
    all_to_all x11, waiting for transfers between devices, gather_stats(): return lax.all_to_all(copies, axes, 0, 0, tiled=True)  61.6 us
    all_to_all x3, waiting for transfers between devices, exchange(): return lax.all_to_all(array, 'wa', 0, 0, tiled=True)  57 us
    all_to_all x3, blocking collectives, gather_stats(): return lax.all_to_all(copies, axes, 0, 0, tiled=True)  49 us
    all_to_all x11, starting transfers between devices, gather_stats(): return lax.all_to_all(copies, axes, 0, 0, tiled=True)  46.2 us
  transfers between devices with their start and end apart: 85, of which 28 were waited for; matrix products, arithmetic and copies ran while one was open for 6% of the time, Pallas kernels for 20%

profile of v2, /device:TPU:0, one launch (start us, length us, event | category | flops | bytes accessed | tf_op | source)
XLA Modules:
  0.0 879.3 jit_solution(5440140462392226568)
XLA Ops:
  7.2 5.5 pack.2
  19.4 4.5 fast_first.1
  24.8 3.9 collective-permute-start
  30.0 4.6 collective-permute-start.5
  40.4 6.0 collective-permute-done.1.refs_2_
  71.4 13.8 %all-to-all-done.refs_2_.refs_8_.refs_3_ = f32[32,8,128]{2,1,0:T(8,128)S(1)} async-done(((f32[32,8,128]{2,1,0:T(8,128)}), f32[32,8,128]{2,1,0:T(8,128)S(1)}, u32[]{:S(2)}, u32[]{:S(2)}) %all-to-all-start) | async-done | bytes 131104 | tf_op jit(solution)/shard_map/all_to_all | solution.py:813
  85.2 5.3 fast_plane.1
  99.5 4.4 collective-permute-start.15
  104.3 22.0 %collective-permute-done.9.refs_6_.refs_11_ = bf16[1024,128]{1,0:T(8,128)(2,1)} collective-permute-done((bf16[1024,128]{1,0:T(8,128)(2,1)}, bf16[1024,128]{1,0:T(8,128)(2,1)}, u32[]{:S(2)}, u32[]{:S(2)}) %collective-permute-start.9) | collective-permute-done | bytes 262176 | tf_op jit(solution)/shard_map/ppermute | solution.py:858
  129.1 3.9 fast_widen.1
  136.0 16.5 %all-to-all-done.2.refs_4_.refs_6_ = f32[32,8,128]{2,1,0:T(8,128)S(1)} async-done(((f32[32,8,128]{2,1,0:T(8,128)}), f32[32,8,128]{2,1,0:T(8,128)S(1)}, u32[]{:S(2)}, u32[]{:S(2)}) %all-to-all-start.2) | async-done | bytes 131104 | tf_op jit(solution)/shard_map/all_to_all | solution.py:813
  152.5 4.9 fast_out.1
  157.5 4.6 all-to-all-start.3
  163.6 14.1 %slow_enter.1 = (bf16[2,4,256,1024]{3,2,1,0:T(8,128)(2,1)}, f32[10,256,256]{2,1,0:T(8,128)}, bf16[2,4,256,1024]{3,2,1,0:T(8,128)(2,1)}) custom-call(s32[1]{0:T(128)} %bitcast.refs_0_.refs_2_, bf16[3,1280,256]{2,1,0:T(8,128)(2,1)} %refs_7_.9, bf16[1280,1024]{1,0:T(8,128)(2,1)} %refs_9_.1, bf16[1024,128]{1,0:T(8,128)(2,1)S(1)} %copy-done.91, ...), custom_call_target="tpu_custom_call" | custom-call | flops 7516192768 | bytes 19791876 | tf_op jit(solution)/shard_map/slow_enter/pallas_call | solution.py:45
  177.8 27.6 %all-to-all-done.3 = bf16[16,512,128]{2,1,0:T(8,128)(2,1)} async-done(((bf16[16,512,128]{2,1,0:T(8,128)(2,1)}), bf16[16,512,128]{2,1,0:T(8,128)(2,1)}, u32[]{:S(2)}, u32[]{:S(2)}) %all-to-all-start.3) | async-done | bytes 2097184 | tf_op jit(solution)/shard_map/all_to_all | solution.py:810
  205.3 4.5 lateral_enter.1
  209.8 9.7 %all-to-all-start.4 = ((f32[32,2,256]{2,1,0:T(2,128)}), f32[32,2,256]{2,1,0:T(2,128)S(1)}, u32[]{:S(2)}, u32[]{:S(2)}) async-start(f32[32,2,256]{2,1,0:T(2,128)} %get-tuple-element.170), calls=%async_computation.4 | async-start | bytes 131072 | tf_op jit(solution)/shard_map/all_to_all | solution.py:813
  219.6 5.5 pack.3
  241.3 7.6 collective-permute-done.19.refs_8_.refs_12_
  253.0 5.4 narrow_enter.1
  259.5 15.7 %all_to_all.95.refs_3_.refs_9_.refs_4_ = f32[32,2,256]{2,1,0:T(2,128)S(1)} all-to-all(f32[32,2,256]{2,1,0:T(2,128)S(1)} %get-tuple-element.172), channel_id=1, replica_groups=mesh['dp'=2,'wa'=16] {'dp','wa'}, dimensions={0} | all-to-all | bytes 131072 | tf_op jit(solution)/shard_map/all_to_all | solution.py:813
  275.2 7.0 middle_enter.1
  282.3 4.7 all-to-all-start.6
  290.7 3.8 all-to-all-done.6.refs_3_.refs_9_.refs_4_
  294.5 8.9 %wide_enter.1 = (bf16[8,256,256]{2,1,0:T(8,128)(2,1)}, bf16[8,256,1024]{2,1,0:T(8,128)(2,1)}, f32[4,1024]{1,0:T(4,128)S(1)}) custom-call(f32[1,1]{1,0:T(1,128)} %bitcast.1.refs_0_, s32[1]{0:T(128)} %dynamic_slice.3.refs_0_.refs_1_, f32[8,256,256]{2,1,0:T(8,128)} %get-tuple-element.193.refs_2_.refs_8_.refs_3_, ...), custom_call_target="tpu_custom_call" | custom-call | bytes 17123336 | tf_op jit(solution)/shard_map/wide_enter/pallas_call | solution.py:45
  308.9 4.6 collective-permute-start.28
  318.7 4.2 collective-permute-start.32
  323.0 31.6 %collective-permute-done.28.refs_20_ = bf16[1024,128]{1,0:T(8,128)(2,1)S(1)} collective-permute-done((bf16[1024,128]{1,0:T(8,128)(2,1)}, bf16[1024,128]{1,0:T(8,128)(2,1)S(1)}, u32[]{:S(2)}, u32[]{:S(2)}) %collective-permute-start.28) | collective-permute-done | bytes 262176 | tf_op jit(solution)/shard_map/ppermute | solution.py:858
  355.6 13.8 %wide_out.1 = (bf16[1024,128]{1,0:T(8,128)(2,1)S(1)}, bf16[1024,128]{1,0:T(8,128)(2,1)}, bf16[1024,128]{1,0:T(8,128)(2,1)S(1)}, bf16[1024,128]{1,0:T(8,128)(2,1)...) custom-call(f32[1,1]{1,0:T(1,128)} %bitcast.1.refs_0_, ...), custom_call_target="tpu_custom_call" | custom-call | bytes 22839308 | tf_op jit(solution)/shard_map/wide_out/pallas_call | solution.py:45
  372.1 23.8 %all-to-all-start.8 = ((f32[16,4,1024]{2,1,0:T(4,128)}), f32[16,4,1024]{2,1,0:T(4,128)S(1)}, u32[]{:S(2)}, u32[]{:S(2)}) async-start(f32[16,4,1024]{2,1,0:T(4,128)} %broadcast_in_dim.10), calls=%async_computation.8 | async-start | bytes 524288 | tf_op jit(solution)/shard_map/all_to_all | solution.py:820
  402.8 5.2 collective-permute-done.33.refs_2_.refs_11_
  408.0 3.7 collective-permute-start.38
  415.6 11.2 %middle_back.1 = (f32[8,256,256]{2,1,0:T(8,128)}, bf16[1024,256]{1,0:T(8,128)(2,1)}, f32[32,2,256]{2,1,0:T(2,128)}) custom-call(f32[1,1]{1,0:T(1,128)} %bitcast.1.refs_0_, s32[1]{0:T(128)} %dynamic_slice.3.refs_0_.refs_1_, f32[8,256,1024]{2,1,0:T(8,128)} %bitcast.120, bf16[8,256,256]{2,1,0:T(8,128)(2,1)} %get-tuple-element.202.refs_3_, ...), custom_call_target="tpu_custom_call" | custom-call | bytes 15869960 | tf_op jit(solution)/shard_map/middle_back/pallas_call | solution.py:45
  447.5 8.4 narrow_back.1
  456.5 5.8 all-to-all-start.10
  466.3 22.0 %project_back.1 = (bf16[8,256,1280]{2,1,0:T(8,128)(2,1)}, bf16[5120,256]{1,0:T(8,128)(2,1)}) custom-call(f32[1,1]{1,0:T(1,128)} %bitcast.1.refs_0_, s32[1]{0:T(128)} %dynamic_slice.3.refs_0_.refs_1_, f32[8,256,1024]{2,1,0:T(8,128)} %bitcast.121, bf16[8,256,1024]{2,1,0:T(8,128)(2,1)} %get-tuple-element.203.refs_3_, f32[16,4,1024]{2,1,0:T(4,128)S(1)} %copy-done.7, ...), custom_call_target="tpu_custom_call" | custom-call | flops 10737418240 | bytes 28844040 | tf_op jit(solution)/shard_map/project_back/pallas_call | solution.py:45
  488.4 5.3 collective-permute-done.43.refs_12_.refs_16_
  495.4 13.2 %join_back.1 = (bf16[10,256,256]{2,1,0:T(8,128)(2,1)}, bf16[16,1024,128]{2,1,0:T(8,128)(2,1)}, f32[2,4,256,256]{3,2,1,0:T(8,128)}, f32[32,2,256]{2,1,0:T(2,128)}) custom-call(f32[1,1]{1,0:T(1,128)} %bitcast.1.refs_0_, s32[1]{0:T(128)} %dynamic_slice.3.refs_0_.refs_1_, f32[8,256,256]{2,1,0:T(8,128)} %get-tuple-element.232.refs_2_, ...), custom_call_target="tpu_custom_call" | custom-call | bytes 22941704 | tf_op jit(solution)/shard_map/join_back/pallas_call | solution.py:45
  517.6 6.4 plane_weight.1
  527.5 6.8 weight_merge.1
  538.0 4.5 collective-permute-start.47
  542.5 4.4 all-to-all-start.12
  546.9 4.2 collective-permute-done.46.refs_15_.refs_9_
  551.1 6.6 collective-permute-done.47.refs_16_.refs_10_
  557.7 17.7 %all-to-all-done.12.refs_5_ = f32[32,2,256]{2,1,0:T(2,128)S(1)} async-done(((f32[32,2,256]{2,1,0:T(2,128)}), f32[32,2,256]{2,1,0:T(2,128)S(1)}, u32[]{:S(2)}, u32[]{:S(2)}) %all-to-all-start.12) | async-done | bytes 65568 | tf_op jit(solution)/shard_map/all_to_all | solution.py:813
  575.4 5.8 lateral_back.1
  581.2 4.7 all-to-all-start.13
  598.4 9.9 %collective-permute-done.56 = bf16[80,256]{1,0:T(8,128)(2,1)S(1)} collective-permute-done((bf16[80,256]{1,0:T(8,128)(2,1)S(1)}, bf16[80,256]{1,0:T(8,128)(2,1)S(1)}, u32[]{:S(2)}, u32[]{:S(2)}) %collective-permute-start.56) | collective-permute-done | bytes 40992 | tf_op jit(solution)/shard_map/ppermute | solution.py:1331
  610.5 29.4 %all-to-all-done.13 = bf16[16,512,128]{2,1,0:T(8,128)(2,1)} async-done(((bf16[16,512,128]{2,1,0:T(8,128)(2,1)}), bf16[16,512,128]{2,1,0:T(8,128)(2,1)}, u32[]{:S(2)}, u32[]{:S(2)}) %all-to-all-start.13) | async-done | bytes 2097184 | tf_op jit(solution)/shard_map/all_to_all | solution.py:810
  639.9 7.2 fast_back_sum.1
  647.1 23.3 %all_to_all.96.refs_5_ = f32[32,8,128]{2,1,0:T(8,128)S(1)} all-to-all(f32[32,8,128]{2,1,0:T(8,128)S(1)} %get-tuple-element.241), channel_id=1, replica_groups=mesh['dp'=2,'wa'=16] {'dp','wa'}, dimensions={0} | all-to-all | bytes 262144 | tf_op jit(solution)/shard_map/all_to_all | solution.py:813
  670.4 6.6 fast_back_widen.1
  677.0 10.0 %all_to_all.97.refs_4_ = f32[32,8,128]{2,1,0:T(8,128)S(1)} all-to-all(f32[32,8,128]{2,1,0:T(8,128)S(1)} %get-tuple-element.253), channel_id=1, replica_groups=mesh['dp'=2,'wa'=16] {'dp','wa'}, dimensions={0} | all-to-all | bytes 262144 | tf_op jit(solution)/shard_map/all_to_all | solution.py:813
  687.0 5.1 all-to-all-start.11
  703.3 7.9 unpack.2
  719.9 36.1 %collective-permute-done.58.refs_13_.refs_2_ = bf16[1616,256]{1,0:T(8,128)(2,1)S(1)} collective-permute-done((bf16[1616,256]{1,0:T(8,128)(2,1)S(1)}, bf16[1616,256]{1,0:T(8,128)(2,1)S(1)}, u32[]{:S(2)}, u32[]{:S(2)}) %collective-permute-start.58) | collective-permute-done | bytes 827424 | tf_op jit(solution)/shard_map/ppermute | solution.py:1387
  756.0 34.7 %collective-permute-done.60.refs_15_.refs_4_ = bf16[1616,256]{1,0:T(8,128)(2,1)} collective-permute-done((bf16[1616,256]{1,0:T(8,128)(2,1)S(1)}, bf16[1616,256]{1,0:T(8,128)(2,1)}, u32[]{:S(2)}, u32[]{:S(2)}) %collective-permute-start.60) | collective-permute-done | bytes 827424 | tf_op jit(solution)/shard_map/ppermute | solution.py:1387
  793.7 7.2 fast_back_plane.1
  806.0 7.8 unpack.3
  818.5 3.8 collective-permute-start.61
  836.1 6.8 fast_back_out.1
  845.2 4.6 all-to-all-start.17
  850.6 7.1 all-to-all-done.17
  862.2 7.7 weight_split.1
  (453 shorter events, 219.4 us)
Async XLA Ops:
  12.8 17.3 %collective-permute-start.2 = (bf16[1024,128]{1,0:T(8,128)(2,1)S(1)}, bf16[1024,128]{1,0:T(8,128)(2,1)S(1)}, u32[]{:S(2)}, u32[]{:S(2)}) collective-permute-start(bf16[1024,128]{1,0:T(8,128)(2,1)S(1)} %get-tuple-element.146), channel_id=1, source_target_pairs={{0,1},{1,0},{2,3},{3,2},{4,5},{5,4},{6,7},{7,6},{8,9},{9,8},{10,11... | collective-permute-start | bytes 786440 | tf_op jit(solution)/shard_map/ppermute | solution.py:858
  15.8 18.9 %collective-permute-start.3 = (bf16[1024,128]{1,0:T(8,128)(2,1)S(1)}, bf16[1024,128]{1,0:T(8,128)(2,1)S(1)}, u32[]{:S(2)}, u32[]{:S(2)}) collective-permute-start(bf16[1024,128]{1,0:T(8,128)(2,1)S(1)} %get-tuple-element.147), channel_id=1, source_target_pairs={{0,2},{1,3},{2,0},{3,1},{4,6},{5,7},{6,4},{7,5},{8,10},{9,11},{10,... | collective-permute-start | bytes 786440 | tf_op jit(solution)/shard_map/ppermute | solution.py:858
  17.3 17.3 %collective-permute-start.4 = (bf16[1024,128]{1,0:T(8,128)(2,1)S(1)}, bf16[1024,128]{1,0:T(8,128)(2,1)S(1)}, u32[]{:S(2)}, u32[]{:S(2)}) collective-permute-start(bf16[1024,128]{1,0:T(8,128)(2,1)S(1)} %get-tuple-element.148), channel_id=1, source_target_pairs={{0,3},{1,2},{2,1},{3,0},{4,7},{5,6},{6,5},{7,4},{8,11},{9,10},{10,... | collective-permute-start | bytes 786440 | tf_op jit(solution)/shard_map/ppermute | solution.py:858
  28.7 17.6 %collective-permute-start.1 = (bf16[4,256,128]{2,1,0:T(8,128)(2,1)S(1)}, bf16[4,256,128]{2,1,0:T(8,128)(2,1)S(1)}, u32[]{:S(2)}, u32[]{:S(2)}) collective-permute-start(bf16[4,256,128]{2,1,0:T(8,128)(2,1)S(1)} %get-tuple-element.145), channel_id=1, source_target_pairs={{1,0},{2,1},{3,2},{4,3},{5,4},{6,5},{7,6},{8,7},{9,8},{10,9},{11,1... | collective-permute-start | bytes 786440 | tf_op jit(solution)/shard_map/ppermute | solution.py:902
  30.0 25.3 %collective-permute-start.5 = (bf16[1024,128]{1,0:T(8,128)(2,1)}, bf16[1024,128]{1,0:T(8,128)(2,1)S(1)}, u32[]{:S(2)}, u32[]{:S(2)}) collective-permute-start(bf16[1024,128]{1,0:T(8,128)(2,1)} %get-tuple-element.151), channel_id=1, source_target_pairs={{0,4},{1,5},{2,6},{3,7},{4,0},{5,1},{6,2},{7,3},{8,12},{9,13},{10,... | collective-permute-start | bytes 786440 | tf_op jit(solution)/shard_map/ppermute | solution.py:858
  34.6 24.4 %collective-permute-start.6 = (bf16[1024,128]{1,0:T(8,128)(2,1)S(1)}, bf16[1024,128]{1,0:T(8,128)(2,1)S(1)}, u32[]{:S(2)}, u32[]{:S(2)}) collective-permute-start(bf16[1024,128]{1,0:T(8,128)(2,1)S(1)} %get-tuple-element.152), channel_id=1, source_target_pairs={{0,5},{1,4},{2,7},{3,6},{4,1},{5,0},{6,3},{7,2},{8,13},{9,12},{10,... | collective-permute-start | bytes 786440 | tf_op jit(solution)/shard_map/ppermute | solution.py:858
  34.6 25.8 %collective-permute-start.7 = (bf16[1024,128]{1,0:T(8,128)(2,1)S(1)}, bf16[1024,128]{1,0:T(8,128)(2,1)S(1)}, u32[]{:S(2)}, u32[]{:S(2)}) collective-permute-start(bf16[1024,128]{1,0:T(8,128)(2,1)S(1)} %get-tuple-element.153), channel_id=1, source_target_pairs={{0,6},{1,7},{2,4},{3,5},{4,2},{5,3},{6,0},{7,1},{8,14},{9,15},{10,... | collective-permute-start | bytes 786440 | tf_op jit(solution)/shard_map/ppermute | solution.py:858
  37.7 33.6 %collective-permute-start.8 = (bf16[1024,128]{1,0:T(8,128)(2,1)}, bf16[1024,128]{1,0:T(8,128)(2,1)S(1)}, u32[]{:S(2)}, u32[]{:S(2)}) collective-permute-start(bf16[1024,128]{1,0:T(8,128)(2,1)} %get-tuple-element.154), channel_id=1, source_target_pairs={{0,7},{1,6},{2,5},{3,4},{4,3},{5,2},{6,1},{7,0},{8,15},{9,14},{10,... | collective-permute-start | bytes 786440 | tf_op jit(solution)/shard_map/ppermute | solution.py:858
  46.3 50.5 %collective-permute-start.10 = (bf16[1024,128]{1,0:T(8,128)(2,1)}, bf16[1024,128]{1,0:T(8,128)(2,1)S(1)}, u32[]{:S(2)}, u32[]{:S(2)}) collective-permute-start(bf16[1024,128]{1,0:T(8,128)(2,1)} %get-tuple-element.158), channel_id=1, source_target_pairs={{0,9},{1,8},{2,11},{3,10},{4,13},{5,12},{6,15},{7,14},{8,1},{9,0},... | collective-permute-start | bytes 786440 | tf_op jit(solution)/shard_map/ppermute | solution.py:858
  52.5 32.7 %all-to-all-start = ((f32[32,8,128]{2,1,0:T(8,128)}), f32[32,8,128]{2,1,0:T(8,128)S(1)}, u32[]{:S(2)}, u32[]{:S(2)}) async-start(f32[32,8,128]{2,1,0:T(8,128)} %get-tuple-element.150), calls=%async_computation | async-start | bytes 262144 | tf_op jit(solution)/shard_map/all_to_all | solution.py:813
  55.4 43.5 %collective-permute-start.11 = (bf16[1024,128]{1,0:T(8,128)(2,1)}, bf16[1024,128]{1,0:T(8,128)(2,1)S(1)}, u32[]{:S(2)}, u32[]{:S(2)}) collective-permute-start(bf16[1024,128]{1,0:T(8,128)(2,1)} %get-tuple-element.159), channel_id=1, source_target_pairs={{0,10},{1,11},{2,8},{3,9},{4,14},{5,15},{6,12},{7,13},{8,2},{9,3},... | collective-permute-start | bytes 786440 | tf_op jit(solution)/shard_map/ppermute | solution.py:858
  59.0 44.9 %collective-permute-start.12 = (bf16[1024,128]{1,0:T(8,128)(2,1)}, bf16[1024,128]{1,0:T(8,128)(2,1)}, u32[]{:S(2)}, u32[]{:S(2)}) collective-permute-start(bf16[1024,128]{1,0:T(8,128)(2,1)} %get-tuple-element.160), channel_id=1, source_target_pairs={{0,11},{1,10},{2,9},{3,8},{4,15},{5,14},{6,13},{7,12},{8,3},{9,2},... | collective-permute-start | bytes 786440 | tf_op jit(solution)/shard_map/ppermute | solution.py:858
  60.5 65.9 %collective-permute-start.9 = (bf16[1024,128]{1,0:T(8,128)(2,1)}, bf16[1024,128]{1,0:T(8,128)(2,1)}, u32[]{:S(2)}, u32[]{:S(2)}) collective-permute-start(bf16[1024,128]{1,0:T(8,128)(2,1)} %get-tuple-element.157), channel_id=1, source_target_pairs={{0,8},{1,9},{2,10},{3,11},{4,12},{5,13},{6,14},{7,15},{8,0},{9,1},... | collective-permute-start | bytes 786440 | tf_op jit(solution)/shard_map/ppermute | solution.py:858
  90.6 36.6 %all-to-all-start.1 = ((f32[32,8,128]{2,1,0:T(8,128)}), f32[32,8,128]{2,1,0:T(8,128)S(1)}, u32[]{:S(2)}, u32[]{:S(2)}) async-start(f32[32,8,128]{2,1,0:T(8,128)} %get-tuple-element.156), calls=%async_computation.1 | async-start | bytes 262144 | tf_op jit(solution)/shard_map/all_to_all | solution.py:813
  93.2 42.7 %collective-permute-start.13 = (bf16[1024,128]{1,0:T(8,128)(2,1)}, bf16[1024,128]{1,0:T(8,128)(2,1)S(1)}, u32[]{:S(2)}, u32[]{:S(2)}) collective-permute-start(bf16[1024,128]{1,0:T(8,128)(2,1)} %get-tuple-element.163), channel_id=1, source_target_pairs={{0,12},{1,13},{2,14},{3,15},{4,8},{5,9},{6,10},{7,11},{8,4},{9,5},... | collective-permute-start | bytes 786440 | tf_op jit(solution)/shard_map/ppermute | solution.py:858
  97.6 38.4 %collective-permute-start.14 = (bf16[1024,128]{1,0:T(8,128)(2,1)}, bf16[1024,128]{1,0:T(8,128)(2,1)S(1)}, u32[]{:S(2)}, u32[]{:S(2)}) collective-permute-start(bf16[1024,128]{1,0:T(8,128)(2,1)} %get-tuple-element.164), channel_id=1, source_target_pairs={{0,13},{1,12},{2,15},{3,14},{4,9},{5,8},{6,11},{7,10},{8,5},{9,4},... | collective-permute-start | bytes 786440 | tf_op jit(solution)/shard_map/ppermute | solution.py:858
  99.5 36.4 %collective-permute-start.15 = (bf16[1024,128]{1,0:T(8,128)(2,1)}, bf16[1024,128]{1,0:T(8,128)(2,1)S(1)}, u32[]{:S(2)}, u32[]{:S(2)}) collective-permute-start(bf16[1024,128]{1,0:T(8,128)(2,1)} %get-tuple-element.165), channel_id=1, source_target_pairs={{0,14},{1,15},{2,12},{3,13},{4,10},{5,11},{6,8},{7,9},{8,6},{9,7},... | collective-permute-start | bytes 786440 | tf_op jit(solution)/shard_map/ppermute | solution.py:858
  103.9 32.0 %collective-permute-start.16 = (bf16[1024,128]{1,0:T(8,128)(2,1)}, bf16[1024,128]{1,0:T(8,128)(2,1)}, u32[]{:S(2)}, u32[]{:S(2)}) collective-permute-start(bf16[1024,128]{1,0:T(8,128)(2,1)} %get-tuple-element.166), channel_id=1, source_target_pairs={{0,15},{1,14},{2,13},{3,12},{4,11},{5,10},{6,9},{7,8},{8,7},{9,6},... | collective-permute-start | bytes 786440 | tf_op jit(solution)/shard_map/ppermute | solution.py:858
  133.0 19.5 %all-to-all-start.2 = ((f32[32,8,128]{2,1,0:T(8,128)}), f32[32,8,128]{2,1,0:T(8,128)S(1)}, u32[]{:S(2)}, u32[]{:S(2)}) async-start(f32[32,8,128]{2,1,0:T(8,128)} %get-tuple-element.162), calls=%async_computation.2 | async-start | bytes 262144 | tf_op jit(solution)/shard_map/all_to_all | solution.py:813
  157.5 47.8 %all-to-all-start.3 = ((bf16[16,512,128]{2,1,0:T(8,128)(2,1)}), bf16[16,512,128]{2,1,0:T(8,128)(2,1)}, u32[]{:S(2)}, u32[]{:S(2)}) async-start(bf16[16,512,128]{2,1,0:T(8,128)(2,1)} %bitcast.122), calls=%async_computation.3 | async-start | bytes 4194304 | tf_op jit(solution)/shard_map/all_to_all | solution.py:810
  209.8 17.0 %all-to-all-start.4 = ((f32[32,2,256]{2,1,0:T(2,128)}), f32[32,2,256]{2,1,0:T(2,128)S(1)}, u32[]{:S(2)}, u32[]{:S(2)}) async-start(f32[32,2,256]{2,1,0:T(2,128)} %get-tuple-element.170), calls=%async_computation.4 | async-start | bytes 131072 | tf_op jit(solution)/shard_map/all_to_all | solution.py:813
  229.9 19.0 %collective-permute-start.19 = (bf16[1024,128]{1,0:T(8,128)(2,1)}, bf16[1024,128]{1,0:T(8,128)(2,1)S(1)}, u32[]{:S(2)}, u32[]{:S(2)}) collective-permute-start(bf16[1024,128]{1,0:T(8,128)(2,1)} %get-tuple-element.191), channel_id=1, source_target_pairs={{0,3},{1,2},{2,1},{3,0},{4,7},{5,6},{6,5},{7,4},{8,11},{9,10},{10,... | collective-permute-start | bytes 786440 | tf_op jit(solution)/shard_map/ppermute | solution.py:858
  231.8 18.6 %collective-permute-start.20 = (bf16[1024,128]{1,0:T(8,128)(2,1)}, bf16[1024,128]{1,0:T(8,128)(2,1)S(1)}, u32[]{:S(2)}, u32[]{:S(2)}) collective-permute-start(bf16[1024,128]{1,0:T(8,128)(2,1)} %copy-done.51), channel_id=1, source_target_pairs={{0,4},{1,5},{2,6},{3,7},{4,0},{5,1},{6,2},{7,3},{8,12},{9,13},{10,... | collective-permute-start | bytes 786440 | tf_op jit(solution)/shard_map/ppermute | solution.py:858
  232.6 54.4 %collective-permute-start.21 = (bf16[1024,128]{1,0:T(8,128)(2,1)}, bf16[1024,128]{1,0:T(8,128)(2,1)S(1)}, u32[]{:S(2)}, u32[]{:S(2)}) collective-permute-start(bf16[1024,128]{1,0:T(8,128)(2,1)} %copy-done.52), channel_id=1, source_target_pairs={{0,5},{1,4},{2,7},{3,6},{4,1},{5,0},{6,3},{7,2},{8,13},{9,12},{10,... | collective-permute-start | bytes 786440 | tf_op jit(solution)/shard_map/ppermute | solution.py:858
  237.5 53.2 %collective-permute-start.22 = (bf16[1024,128]{1,0:T(8,128)(2,1)}, bf16[1024,128]{1,0:T(8,128)(2,1)}, u32[]{:S(2)}, u32[]{:S(2)}) collective-permute-start(bf16[1024,128]{1,0:T(8,128)(2,1)} %copy-done.53), channel_id=1, source_target_pairs={{0,6},{1,7},{2,4},{3,5},{4,2},{5,3},{6,0},{7,1},{8,14},{9,15},{10,... | collective-permute-start | bytes 786440 | tf_op jit(solution)/shard_map/ppermute | solution.py:858
  238.5 52.2 %collective-permute-start.23 = (bf16[1024,128]{1,0:T(8,128)(2,1)}, bf16[1024,128]{1,0:T(8,128)(2,1)}, u32[]{:S(2)}, u32[]{:S(2)}) collective-permute-start(bf16[1024,128]{1,0:T(8,128)(2,1)} %get-tuple-element.199), channel_id=1, source_target_pairs={{0,7},{1,6},{2,5},{3,4},{4,3},{5,2},{6,1},{7,0},{8,15},{9,14},{10,... | collective-permute-start | bytes 786440 | tf_op jit(solution)/shard_map/ppermute | solution.py:858
  248.9 41.7 %collective-permute-start.24 = (bf16[1024,128]{1,0:T(8,128)(2,1)}, bf16[1024,128]{1,0:T(8,128)(2,1)}, u32[]{:S(2)}, u32[]{:S(2)}) collective-permute-start(bf16[1024,128]{1,0:T(8,128)(2,1)} %get-tuple-element.200), channel_id=1, source_target_pairs={{0,8},{1,9},{2,10},{3,11},{4,12},{5,13},{6,14},{7,15},{8,0},{9,1},... | collective-permute-start | bytes 786440 | tf_op jit(solution)/shard_map/ppermute | solution.py:858
  250.4 40.3 %collective-permute-start.25 = (bf16[1024,128]{1,0:T(8,128)(2,1)}, bf16[1024,128]{1,0:T(8,128)(2,1)}, u32[]{:S(2)}, u32[]{:S(2)}) collective-permute-start(bf16[1024,128]{1,0:T(8,128)(2,1)} %get-tuple-element.201), channel_id=1, source_target_pairs={{0,9},{1,8},{2,11},{3,10},{4,13},{5,12},{6,15},{7,14},{8,1},{9,0},... | collective-permute-start | bytes 786440 | tf_op jit(solution)/shard_map/ppermute | solution.py:858
  287.0 31.7 %collective-permute-start.27 = (bf16[1024,128]{1,0:T(8,128)(2,1)}, bf16[1024,128]{1,0:T(8,128)(2,1)S(1)}, u32[]{:S(2)}, u32[]{:S(2)}) collective-permute-start(bf16[1024,128]{1,0:T(8,128)(2,1)} %get-tuple-element.206), channel_id=1, source_target_pairs={{0,10},{1,11},{2,8},{3,9},{4,14},{5,15},{6,12},{7,13},{8,2},{9,3},... | collective-permute-start | bytes 786440 | tf_op jit(solution)/shard_map/ppermute | solution.py:858
  305.4 49.2 %all-to-all-start.7 = ((f32[16,4,1024]{2,1,0:T(4,128)}), f32[16,4,1024]{2,1,0:T(4,128)S(1)}, u32[]{:S(2)}, u32[]{:S(2)}) async-start(f32[16,4,1024]{2,1,0:T(4,128)} %broadcast_in_dim.9), calls=%async_computation.7 | async-start | bytes 524288 | tf_op jit(solution)/shard_map/all_to_all | solution.py:820
  308.9 45.6 %collective-permute-start.28 = (bf16[1024,128]{1,0:T(8,128)(2,1)}, bf16[1024,128]{1,0:T(8,128)(2,1)S(1)}, u32[]{:S(2)}, u32[]{:S(2)}) collective-permute-start(bf16[1024,128]{1,0:T(8,128)(2,1)} %get-tuple-element.207), channel_id=1, source_target_pairs={{0,11},{1,10},{2,9},{3,8},{4,15},{5,14},{6,13},{7,12},{8,3},{9,2},... | collective-permute-start | bytes 786440 | tf_op jit(solution)/shard_map/ppermute | solution.py:858
  313.5 41.0 %collective-permute-start.29 = (bf16[1024,128]{1,0:T(8,128)(2,1)}, bf16[1024,128]{1,0:T(8,128)(2,1)S(1)}, u32[]{:S(2)}, u32[]{:S(2)}) collective-permute-start(bf16[1024,128]{1,0:T(8,128)(2,1)} %get-tuple-element.208), channel_id=1, source_target_pairs={{0,12},{1,13},{2,14},{3,15},{4,8},{5,9},{6,10},{7,11},{8,4},{9,5},... | collective-permute-start | bytes 786440 | tf_op jit(solution)/shard_map/ppermute | solution.py:858
  314.9 39.6 %collective-permute-start.30 = (bf16[1024,128]{1,0:T(8,128)(2,1)}, bf16[1024,128]{1,0:T(8,128)(2,1)S(1)}, u32[]{:S(2)}, u32[]{:S(2)}) collective-permute-start(bf16[1024,128]{1,0:T(8,128)(2,1)} %get-tuple-element.209), channel_id=1, source_target_pairs={{0,13},{1,12},{2,15},{3,14},{4,9},{5,8},{6,11},{7,10},{8,5},{9,4},... | collective-permute-start | bytes 786440 | tf_op jit(solution)/shard_map/ppermute | solution.py:858
  317.3 37.3 %collective-permute-start.31 = (bf16[1024,128]{1,0:T(8,128)(2,1)}, bf16[1024,128]{1,0:T(8,128)(2,1)S(1)}, u32[]{:S(2)}, u32[]{:S(2)}) collective-permute-start(bf16[1024,128]{1,0:T(8,128)(2,1)} %get-tuple-element.210), channel_id=1, source_target_pairs={{0,14},{1,15},{2,12},{3,13},{4,10},{5,11},{6,8},{7,9},{8,6},{9,7},... | collective-permute-start | bytes 786440 | tf_op jit(solution)/shard_map/ppermute | solution.py:858
  318.7 35.9 %collective-permute-start.32 = (bf16[1024,128]{1,0:T(8,128)(2,1)}, bf16[1024,128]{1,0:T(8,128)(2,1)}, u32[]{:S(2)}, u32[]{:S(2)}) collective-permute-start(bf16[1024,128]{1,0:T(8,128)(2,1)} %get-tuple-element.211), channel_id=1, source_target_pairs={{0,15},{1,14},{2,13},{3,12},{4,11},{5,10},{6,9},{7,8},{8,7},{9,6},... | collective-permute-start | bytes 786440 | tf_op jit(solution)/shard_map/ppermute | solution.py:858
  372.1 42.6 %all-to-all-start.8 = ((f32[16,4,1024]{2,1,0:T(4,128)}), f32[16,4,1024]{2,1,0:T(4,128)S(1)}, u32[]{:S(2)}, u32[]{:S(2)}) async-start(f32[16,4,1024]{2,1,0:T(4,128)} %broadcast_in_dim.10), calls=%async_computation.8 | async-start | bytes 524288 | tf_op jit(solution)/shard_map/all_to_all | solution.py:820
  399.3 35.6 %collective-permute-start.35 = (bf16[1024,128]{1,0:T(8,128)(2,1)}, bf16[1024,128]{1,0:T(8,128)(2,1)S(1)}, u32[]{:S(2)}, u32[]{:S(2)}) collective-permute-start(bf16[1024,128]{1,0:T(8,128)(2,1)} %get-tuple-element.215), channel_id=1, source_target_pairs={{0,3},{1,2},{2,1},{3,0},{4,7},{5,6},{6,5},{7,4},{8,11},{9,10},{10,... | collective-permute-start | bytes 786440 | tf_op jit(solution)/shard_map/ppermute | solution.py:858
  399.4 38.8 %collective-permute-start.36 = (bf16[1024,128]{1,0:T(8,128)(2,1)}, bf16[1024,128]{1,0:T(8,128)(2,1)S(1)}, u32[]{:S(2)}, u32[]{:S(2)}) collective-permute-start(bf16[1024,128]{1,0:T(8,128)(2,1)} %get-tuple-element.216), channel_id=1, source_target_pairs={{0,4},{1,5},{2,6},{3,7},{4,0},{5,1},{6,2},{7,3},{8,12},{9,13},{10,... | collective-permute-start | bytes 786440 | tf_op jit(solution)/shard_map/ppermute | solution.py:858
  401.3 39.1 %collective-permute-start.37 = (bf16[1024,128]{1,0:T(8,128)(2,1)}, bf16[1024,128]{1,0:T(8,128)(2,1)S(1)}, u32[]{:S(2)}, u32[]{:S(2)}) collective-permute-start(bf16[1024,128]{1,0:T(8,128)(2,1)} %get-tuple-element.217), channel_id=1, source_target_pairs={{0,5},{1,4},{2,7},{3,6},{4,1},{5,0},{6,3},{7,2},{8,13},{9,12},{10,... | collective-permute-start | bytes 786440 | tf_op jit(solution)/shard_map/ppermute | solution.py:858
  408.0 36.5 %collective-permute-start.38 = (bf16[1024,128]{1,0:T(8,128)(2,1)}, bf16[1024,128]{1,0:T(8,128)(2,1)}, u32[]{:S(2)}, u32[]{:S(2)}) collective-permute-start(bf16[1024,128]{1,0:T(8,128)(2,1)} %get-tuple-element.218), channel_id=1, source_target_pairs={{0,6},{1,7},{2,4},{3,5},{4,2},{5,3},{6,0},{7,1},{8,14},{9,15},{10,... | collective-permute-start | bytes 786440 | tf_op jit(solution)/shard_map/ppermute | solution.py:858
  411.7 50.9 %collective-permute-start.39 = (bf16[1024,128]{1,0:T(8,128)(2,1)}, bf16[1024,128]{1,0:T(8,128)(2,1)S(1)}, u32[]{:S(2)}, u32[]{:S(2)}) collective-permute-start(bf16[1024,128]{1,0:T(8,128)(2,1)} %get-tuple-element.219), channel_id=1, source_target_pairs={{0,7},{1,6},{2,5},{3,4},{4,3},{5,2},{6,1},{7,0},{8,15},{9,14},{10,... | collective-permute-start | bytes 786440 | tf_op jit(solution)/shard_map/ppermute | solution.py:858
  426.9 17.8 %all-to-all-start.9 = ((f32[32,2,256]{2,1,0:T(2,128)}), f32[32,2,256]{2,1,0:T(2,128)S(1)}, u32[]{:S(2)}, u32[]{:S(2)}) async-start(f32[32,2,256]{2,1,0:T(2,128)} %get-tuple-element.231), calls=%async_computation.9 | async-start | bytes 131072 | tf_op jit(solution)/shard_map/all_to_all | solution.py:813
  435.6 52.7 %collective-permute-start.40 = (bf16[1024,128]{1,0:T(8,128)(2,1)}, bf16[1024,128]{1,0:T(8,128)(2,1)}, u32[]{:S(2)}, u32[]{:S(2)}) collective-permute-start(bf16[1024,128]{1,0:T(8,128)(2,1)} %get-tuple-element.220), channel_id=1, source_target_pairs={{0,8},{1,9},{2,10},{3,11},{4,12},{5,13},{6,14},{7,15},{8,0},{9,1},... | collective-permute-start | bytes 786440 | tf_op jit(solution)/shard_map/ppermute | solution.py:858
  439.0 49.4 %collective-permute-start.41 = (bf16[1024,128]{1,0:T(8,128)(2,1)}, bf16[1024,128]{1,0:T(8,128)(2,1)}, u32[]{:S(2)}, u32[]{:S(2)}) collective-permute-start(bf16[1024,128]{1,0:T(8,128)(2,1)} %get-tuple-element.221), channel_id=1, source_target_pairs={{0,9},{1,8},{2,11},{3,10},{4,13},{5,12},{6,15},{7,14},{8,1},{9,0},... | collective-permute-start | bytes 786440 | tf_op jit(solution)/shard_map/ppermute | solution.py:858
  441.1 47.3 %collective-permute-start.42 = (bf16[1024,128]{1,0:T(8,128)(2,1)}, bf16[1024,128]{1,0:T(8,128)(2,1)}, u32[]{:S(2)}, u32[]{:S(2)}) collective-permute-start(bf16[1024,128]{1,0:T(8,128)(2,1)} %get-tuple-element.222), channel_id=1, source_target_pairs={{0,10},{1,11},{2,8},{3,9},{4,14},{5,15},{6,12},{7,13},{8,2},{9,3},... | collective-permute-start | bytes 786440 | tf_op jit(solution)/shard_map/ppermute | solution.py:858
  444.4 49.3 %collective-permute-start.43 = (bf16[1024,128]{1,0:T(8,128)(2,1)}, bf16[1024,128]{1,0:T(8,128)(2,1)}, u32[]{:S(2)}, u32[]{:S(2)}) collective-permute-start(bf16[1024,128]{1,0:T(8,128)(2,1)} %get-tuple-element.223), channel_id=1, source_target_pairs={{0,11},{1,10},{2,9},{3,8},{4,15},{5,14},{6,13},{7,12},{8,3},{9,2},... | collective-permute-start | bytes 786440 | tf_op jit(solution)/shard_map/ppermute | solution.py:858
  456.5 37.9 %all-to-all-start.10 = ((f32[32,2,256]{2,1,0:T(2,128)}), f32[32,2,256]{2,1,0:T(2,128)S(1)}, u32[]{:S(2)}, u32[]{:S(2)}) async-start(f32[32,2,256]{2,1,0:T(2,128)} %copy-done.68), calls=%async_computation.10 | async-start | bytes 131072 | tf_op jit(solution)/shard_map/all_to_all | solution.py:813
  462.4 146.0 %reduce-scatter.2.cloned.1.call-start = ((), (), s32[]{:S(2)}) async-start(), calls=%async_computation.20 | async-start | bytes 3932160 | tf_op jit(solution)/shard_map/reduce_scatter | solution.py:1309
  462.6 31.1 %collective-permute-start.44 = (bf16[1024,128]{1,0:T(8,128)(2,1)}, bf16[1024,128]{1,0:T(8,128)(2,1)S(1)}, u32[]{:S(2)}, u32[]{:S(2)}) collective-permute-start(bf16[1024,128]{1,0:T(8,128)(2,1)} %get-tuple-element.224), channel_id=1, source_target_pairs={{0,12},{1,13},{2,14},{3,15},{4,8},{5,9},{6,10},{7,11},{8,4},{9,5},... | collective-permute-start | bytes 786440 | tf_op jit(solution)/shard_map/ppermute | solution.py:858
  488.3 39.1 %collective-permute-start.49 = (bf16[5120,256]{1,0:T(8,128)(2,1)}, bf16[5120,256]{1,0:T(8,128)(2,1)}, u32[]{:S(2)}, u32[]{:S(2)}) collective-permute-start(bf16[5120,256]{1,0:T(8,128)(2,1)} %get-tuple-element.242.refs_1_), channel_id=1, source_target_pairs={{0,16},{16,0},{1,17},{17,1},{2,18},{18,2},{3,19},{19,3},{4,20},{20... | collective-permute-start | bytes 7864328 | tf_op jit(solution)/shard_map/ppermute | solution.py:1297
  538.0 19.7 %collective-permute-start.47 = (bf16[1024,128]{1,0:T(8,128)(2,1)S(1)}, bf16[1024,128]{1,0:T(8,128)(2,1)S(1)}, u32[]{:S(2)}, u32[]{:S(2)}) collective-permute-start(bf16[1024,128]{1,0:T(8,128)(2,1)S(1)} %copy-done.104), channel_id=1, source_target_pairs={{0,15},{1,14},{2,13},{3,12},{4,11},{5,10},{6,9},{7,8},{8,7},{9,6},... | collective-permute-start | bytes 786440 | tf_op jit(solution)/shard_map/ppermute | solution.py:858
  542.5 32.9 %all-to-all-start.12 = ((f32[32,2,256]{2,1,0:T(2,128)}), f32[32,2,256]{2,1,0:T(2,128)S(1)}, u32[]{:S(2)}, u32[]{:S(2)}) async-start(f32[32,2,256]{2,1,0:T(2,128)} %get-tuple-element.238), calls=%async_computation.12 | async-start | bytes 131072 | tf_op jit(solution)/shard_map/all_to_all | solution.py:813
  581.2 58.6 %all-to-all-start.13 = ((bf16[16,512,128]{2,1,0:T(8,128)(2,1)}), bf16[16,512,128]{2,1,0:T(8,128)(2,1)}, u32[]{:S(2)}, u32[]{:S(2)}) async-start(bf16[16,512,128]{2,1,0:T(8,128)(2,1)} %bitcast.133), calls=%async_computation.13 | async-start | bytes 4194304 | tf_op jit(solution)/shard_map/all_to_all | solution.py:810
  586.0 84.4 %all-reduce.3.cloned.1.call-start = ((), (), s32[]{:S(2)}) async-start(), calls=%async_computation.21 | async-start | bytes 1654784 | tf_op jit(solution)/shard_map/psum | solution.py:1333
  594.0 14.3 %collective-permute-start.56 = (bf16[80,256]{1,0:T(8,128)(2,1)S(1)}, bf16[80,256]{1,0:T(8,128)(2,1)S(1)}, u32[]{:S(2)}, u32[]{:S(2)}) collective-permute-start(bf16[80,256]{1,0:T(8,128)(2,1)S(1)} %get-tuple-element.250), channel_id=1, source_target_pairs={{0,2},{1,3},{2,0},{3,1},{4,6},{5,7},{6,4},{7,5},{8,10},{9,11},{10,... | collective-permute-start | bytes 122888 | tf_op jit(solution)/shard_map/ppermute | solution.py:1331
  687.0 114.8 %all-to-all-start.11 = ((bf16[16,1024,128]{2,1,0:T(8,128)(2,1)}), bf16[16,1024,128]{2,1,0:T(8,128)(2,1)}, u32[]{:S(2)}, u32[]{:S(2)}) async-start(bf16[16,1024,128]{2,1,0:T(8,128)(2,1)} %get-tuple-element.236), calls=%async_computation.11 | async-start | bytes 8388608 | tf_op jit(solution)/shard_map/all_to_all | solution.py:810
  712.2 43.8 %collective-permute-start.58 = (bf16[1616,256]{1,0:T(8,128)(2,1)S(1)}, bf16[1616,256]{1,0:T(8,128)(2,1)S(1)}, u32[]{:S(2)}, u32[]{:S(2)}) collective-permute-start(bf16[1616,256]{1,0:T(8,128)(2,1)S(1)} %copy-done.2), channel_id=1, source_target_pairs={{0,1},{1,0},{2,3},{3,2},{4,5},{5,4},{6,7},{7,6},{8,9},{9,8},{10,11... | collective-permute-start | bytes 2482184 | tf_op jit(solution)/shard_map/ppermute | solution.py:1387
  714.1 41.9 %collective-permute-start.59 = (bf16[1616,256]{1,0:T(8,128)(2,1)S(1)}, bf16[1616,256]{1,0:T(8,128)(2,1)}, u32[]{:S(2)}, u32[]{:S(2)}) collective-permute-start(bf16[1616,256]{1,0:T(8,128)(2,1)S(1)} %copy-done.2), channel_id=1, source_target_pairs={{0,2},{1,3},{2,0},{3,1},{4,6},{5,7},{6,4},{7,5},{8,10},{9,11},{10,... | collective-permute-start | bytes 2482184 | tf_op jit(solution)/shard_map/ppermute | solution.py:1387
  715.6 75.1 %collective-permute-start.60 = (bf16[1616,256]{1,0:T(8,128)(2,1)S(1)}, bf16[1616,256]{1,0:T(8,128)(2,1)}, u32[]{:S(2)}, u32[]{:S(2)}) collective-permute-start(bf16[1616,256]{1,0:T(8,128)(2,1)S(1)} %copy-done.2), channel_id=1, source_target_pairs={{0,3},{1,2},{2,1},{3,0},{4,7},{5,6},{6,5},{7,4},{8,11},{9,10},{10,... | collective-permute-start | bytes 2482184 | tf_op jit(solution)/shard_map/ppermute | solution.py:1387
  818.5 15.6 %collective-permute-start.61 = (bf16[4,256,128]{2,1,0:T(8,128)(2,1)}, bf16[4,256,128]{2,1,0:T(8,128)(2,1)S(1)}, u32[]{:S(2)}, u32[]{:S(2)}) collective-permute-start(bf16[4,256,128]{2,1,0:T(8,128)(2,1)} %get-tuple-element.332), channel_id=1, source_target_pairs={{0,1},{1,2},{2,3},{3,4},{4,5},{5,6},{6,7},{7,8},{8,9},{9,10},{10,1... | collective-permute-start | bytes 786440 | tf_op jit(solution)/shard_map/ppermute | solution.py:1436
  824.4 37.7 %collective-permute-start.63 = (bf16[1616,256]{1,0:T(8,128)(2,1)S(1)}, bf16[1616,256]{1,0:T(8,128)(2,1)}, u32[]{:S(2)}, u32[]{:S(2)}) collective-permute-start(bf16[1616,256]{1,0:T(8,128)(2,1)S(1)} %copy-done.3), channel_id=1, source_target_pairs={{0,16},{16,0},{1,17},{17,1},{2,18},{18,2},{3,19},{19,3},{4,20},{20... | collective-permute-start | bytes 2482184 | tf_op jit(solution)/shard_map/ppermute | solution.py:1474
  830.6 31.6 %collective-permute-start.64 = (bf16[1616,256]{1,0:T(8,128)(2,1)S(1)}, bf16[1616,256]{1,0:T(8,128)(2,1)}, u32[]{:S(2)}, u32[]{:S(2)}) collective-permute-start(bf16[1616,256]{1,0:T(8,128)(2,1)S(1)} %copy-done.9), channel_id=1, source_target_pairs={{0,16},{16,0},{1,17},{17,1},{2,18},{18,2},{3,19},{19,3},{4,20},{20... | collective-permute-start | bytes 2482184 | tf_op jit(solution)/shard_map/ppermute | solution.py:1474
  831.2 31.0 %collective-permute-start.65 = (bf16[1616,256]{1,0:T(8,128)(2,1)}, bf16[1616,256]{1,0:T(8,128)(2,1)}, u32[]{:S(2)}, u32[]{:S(2)}) collective-permute-start(bf16[1616,256]{1,0:T(8,128)(2,1)} %collective-permute-done.59.refs_14_.refs_3_), channel_id=1, source_target_pairs={{0,16},{16,0},{1,17},{17,1},{2,18},{18,2},{3,19},{19,3},{4,20},{20... | collective-permute-start | bytes 2482184 | tf_op jit(solution)/shard_map/ppermute | solution.py:1474
  834.2 28.0 %collective-permute-start.66 = (bf16[1616,256]{1,0:T(8,128)(2,1)}, bf16[1616,256]{1,0:T(8,128)(2,1)}, u32[]{:S(2)}, u32[]{:S(2)}) collective-permute-start(bf16[1616,256]{1,0:T(8,128)(2,1)} %collective-permute-done.60.refs_15_.refs_4_), channel_id=1, source_target_pairs={{0,16},{16,0},{1,17},{17,1},{2,18},{18,2},{3,19},{19,3},{4,20},{20... | collective-permute-start | bytes 2482184 | tf_op jit(solution)/shard_map/ppermute | solution.py:1474
  (127 other events, 1901.6 us)
Sparse Core Ops, SparseCore 0:
  534.4 72.1 reduce-scatter.1
  610.6 58.7 all-reduce.2

commit v3 on v2

--- a/solution.py
+++ b/solution.py
@@ -13,6 +13,11 @@
 LANES = 128
 GROUPS = 4
 VMEM_BYTES = 52 * 1024 * 1024
+CUT_SLOW = (3, 7, 11, 15)
+CUT_COT = (0, 4, 10)
+CUT_RESULT = (0, 3, 9)
+GATE_COT = 8
+GATE_RESULT = 5
 
 
 def whole(array):
@@ -861,8 +866,30 @@
             for step in range(begin, end)
         ]
 
+    far, close = list(range(wa_count // 2, wa_count)), list(range(1, wa_count // 2))
+    turns = [step for pair in zip(far, close) for step in pair] + [far[-1]]
+
+    def turn(pieces, begin, end):
+        return tuple(pieces[step] for step in turns[begin:end])
+
     def gate(arrays, ready):
         return list(launch(lambda: None, "gate", (), [], [], after=(ready,), carry=tuple(arrays)))
+
+    def send(piece, step):
+        return lax.ppermute(piece, "wa", [(i, i ^ step) for i in range(wa_count)])
+
+    def send_turns(pieces, begin, end):
+        sent = {step: send(pieces[step], step) for step in turns[begin:end]}
+        sent[0] = pieces[0]
+        return sent
+
+    def send_late(pieces, begin, ready):
+        steps = turns[begin:]
+        held = gate([pieces[step] for step in steps], ready) if steps else []
+        return {step: send(piece, step) for step, piece in zip(steps, held)}
+
+    def by_step(pieces):
+        return [pieces[step] for step in range(wa_count)]
 
     def unpack(pieces):
         (flat,) = launch(
@@ -907,7 +934,7 @@
         [(y, packed_spec), (from_prev, rim_spec), (from_next, rim_spec), (lane_sides, sides_spec)],
         [(packed_shape, F32, packed_spec), stat8],
         [acc8],
-        after=tuple(slow_pieces[1:4]),
+        after=turn(slow_pieces, 0, CUT_SLOW[0]),
     )
     g1 = gather_stats(s1)
     act1, pre2, s2 = launch(
@@ -924,7 +951,7 @@
         ],
         [(packed_shape, BF, packed_spec), (packed_shape, F32, packed_spec), stat8],
         [acc8, fast_win],
-        after=tuple(slow_pieces[4:8]),
+        after=turn(slow_pieces, CUT_SLOW[0], CUT_SLOW[1]),
     )
     g2 = gather_stats(s2)
     act2, s3 = launch(
@@ -941,7 +968,7 @@
         ],
         [(packed_shape, BF, packed_spec), stat8],
         [acc8],
-        after=tuple(slow_pieces[8:12]),
+        after=turn(slow_pieces, CUT_SLOW[1], CUT_SLOW[2]),
     )
     g3 = gather_stats(s3)
     (fast_result,) = launch(
@@ -958,7 +985,7 @@
             (w_widen, whole(w_widen)),
         ],
         [(x.shape, BF, x_spec)],
-        after=tuple(slow_pieces[12:]),
+        after=turn(slow_pieces, CUT_SLOW[2], CUT_SLOW[3]),
     )
 
     fast_got = exchange(fast_result.reshape(clips, 2 * cells, c_f)).reshape(4 * frames, cells, c_f)
@@ -1008,7 +1035,8 @@
         after=(base_n,),
     )
     g_l = gather_stats(s_l)
-    cot_pieces = exchange_pieces(gate(cot_out, g_l))
+    cot_out = gate(cot_out, g_l)
+    cot_pieces = send_turns(cot_out, 0, GATE_COT)
 
     lateral_act, pre_n, s_n = launch(
         narrow_enter,
@@ -1029,8 +1057,10 @@
             stat(2, b_s),
         ],
         [pltpu.VMEM((2, b_s), F32)],
+        after=turn(cot_pieces, 0, CUT_COT[0]),
     )
     g_n = gather_stats(s_n)
+    cot_pieces.update(send_late(cot_out, GATE_COT, g_n))
     slow_win = window_shape(4, 3 * b_s)
     slow_low = pltpu.VMEM((4 * 272 - 16, b_s), BF)
     act_n, pre_m, s_m = launch(
@@ -1051,7 +1081,7 @@
             stat(2, b_s),
         ],
         [pltpu.VMEM((2, b_s), F32), slow_win],
-        after=tuple(cot_pieces[1:5]),
+        after=turn(cot_pieces, CUT_COT[0], CUT_COT[1]),
     )
     g_m = gather_stats(s_m)
     act_m, project, s_w = launch(
@@ -1074,7 +1104,7 @@
             ((frames, cells, c_s), BF, frame_spec(c_s, 2)),
             ((4, c_s), F32, pl.BlockSpec((4, c_s), lambda *_: (0, 0))),
         ],
-        after=tuple(cot_pieces[5:10]),
+        after=turn(cot_pieces, CUT_COT[1], CUT_COT[2]),
     )
     g_w = gather_wide(s_w)
     *out_pieces, wide_grad, t_w = launch(
@@ -1091,7 +1121,7 @@
             (slow_expand_norm, whole(slow_expand_norm)),
             (slow_project_norm, whole(slow_project_norm)),
             (slow_expand, whole(slow_expand)),
-            *[(piece, piece_spec) for piece in cot_pieces],
+            *[(piece, piece_spec) for piece in by_step(cot_pieces)],
         ],
         [
             *[(piece_shape, BF, piece_spec)] * wa_count,
@@ -1102,8 +1132,7 @@
     )
     wide_grad = wide_grad.reshape(frames, cells, c_s)
     h_w = gather_wide(t_w)
-    result_pieces = exchange_pieces(out_pieces)
-    slow_result = unpack(result_pieces)
+    result_pieces = send_turns(out_pieces, 0, GATE_RESULT)
 
     middle_grad, expand_w_grad, t_m = launch(
         middle_back,
@@ -1128,9 +1157,11 @@
             stat(2, b_s),
         ],
         [pltpu.VMEM((2, b_s), F32), pltpu.VMEM((b_s, c_s), F32)],
-        after=tuple(result_pieces[1:3]),
+        after=turn(result_pieces, 0, CUT_RESULT[0]),
     )
     h_m = gather_stats(t_m)
+    result_pieces.update(send_late(out_pieces, GATE_RESULT, h_m))
+    slow_result = unpack(by_step(result_pieces))
     joined_part, project_w_grad = launch(
         project_back,
         "project_back",
@@ -1177,7 +1208,7 @@
             stat(2, b_s),
         ],
         [pltpu.VMEM((2, b_s), F32), slow_win],
-        after=tuple(result_pieces[3:7]),
+        after=turn(result_pieces, CUT_RESULT[0], CUT_RESULT[1]),
     )
     h_n = gather_stats(t_n)
     (spatial_w_grad,) = launch(
@@ -1222,7 +1253,7 @@
             stat(2, c_l),
         ],
         [pltpu.VMEM((2, c_l), F32)],
-        after=tuple(result_pieces[7:13]),
+        after=turn(result_pieces, CUT_RESULT[1], CUT_RESULT[2]),
     )
     lateral_grad = lateral_grad.reshape(frames, cells, c_l)
     h_l = gather_stats(t_l)
@@ -1263,7 +1294,7 @@
             ((frames, cells, c_l), BF, pl.BlockSpec((frames, cells, c_l), lambda *_: (0, 0, 0))),
             ((4 * frames, cells, c_f), BF, pl.BlockSpec((4 * frames, cells, c_f), lambda *_: (0, 0, 0))),
         ],
-        after=tuple(result_pieces[13:]),
+        after=turn(result_pieces, CUT_RESULT[2], 15),
     )
     back_got = exchange(frames_back.reshape(wa_count, 2 * cells, c_f)).reshape(x.shape)
     (lateral_w_grad,) = launch(
@@ -1418,58 +1449,6 @@
         after=tuple(pieces),
     )
     h1 = gather_stats(t1)
-    (low1,) = launch(
-        fast_back_first,
-        "fast_back_first",
-        (packs,),
-        [
-            (fast_count, smem),
-            (fast_grad1, packed_spec),
-            (pre1, packed_spec),
-            (g1, whole(g1)),
-            (h1, whole(h1)),
-            (params1, whole(params1)),
-            (lane_sides, sides_spec),
-        ],
-        [((2, packs, cells, LANES), BF, pl.BlockSpec((2, 1, cells, LANES), lambda i: (0, i, 0, 0)))],
-    )
-    low_prev = lax.ppermute(low1[1], "wa", forward)
-    low_next = lax.ppermute(low1[0], "wa", backward)
-    fast_grad, first_blocks = launch(
-        fast_back_out,
-        "fast_back_out",
-        (packs,),
-        [
-            (fast_grad3, x_spec),
-            (low1, pl.BlockSpec((2, 1, cells, LANES), lambda i: (0, i, 0, 0))),
-            (low_prev, rim_spec),
-            (low_next, rim_spec),
-            (x, x_spec),
-            (w_first_back, whole(w_first_back)),
-        ],
-        [
-            (x.shape, BF, x_spec),
-            (
-                (GROUPS, c_f, 3 * LANES),
-                F32,
-                pl.BlockSpec((GROUPS, c_f, 3 * LANES), lambda *_: (0, 0, 0)),
-            ),
-        ],
-        after=(grad_got,),
-    )
-    expand_part = sum(widen_blocks[g, g * b_f : (g + 1) * b_f] for g in range(GROUPS))
-    plane_view = plane_blocks.reshape(3, 3, GROUPS, b_f, GROUPS, b_f)
-    spatial_part = sum(plane_view[:, :, g, :, g] for g in range(GROUPS))
-    first_view = first_blocks.reshape(GROUPS, c_f, 3, GROUPS, b_f)
-    reduce_part = sum(first_view[g, :, :, g] for g in range(GROUPS)).transpose(1, 0, 2)
-
-    small = jnp.concatenate(
-        [reduce_part.reshape(-1), spatial_part.reshape(-1), expand_part.reshape(-1)]
-    )
-    share = -(-small.shape[0] // (devices * LANES)) * LANES
-    padded = jnp.pad(small, (0, share * devices - small.shape[0])).reshape(devices, share // LANES, LANES)
-    mine = jnp.sum(gather_stats(padded), axis=0)
-    small_all = gather_stats(jnp.broadcast_to(mine[None], padded.shape)).reshape(-1)
     if paired:
         pieces = pieces + [lax.ppermute(piece, "dp", swap) for piece in pieces]
     else:
@@ -1492,6 +1471,60 @@
         ],
         [pltpu.VMEM((sum(sizes), b_s), BF)],
     )
+    (low1,) = launch(
+        fast_back_first,
+        "fast_back_first",
+        (packs,),
+        [
+            (fast_count, smem),
+            (fast_grad1, packed_spec),
+            (pre1, packed_spec),
+            (g1, whole(g1)),
+            (h1, whole(h1)),
+            (params1, whole(params1)),
+            (lane_sides, sides_spec),
+        ],
+        [((2, packs, cells, LANES), BF, pl.BlockSpec((2, 1, cells, LANES), lambda i: (0, i, 0, 0)))],
+    )
+    low_prev = lax.ppermute(low1[1], "wa", forward)
+    low_next = lax.ppermute(low1[0], "wa", backward)
+    fast_grad, first_blocks = launch(
+        fast_back_out,
+        "fast_back_out",
+        (packs,),
+        [
+            (fast_grad3, x_spec),
+            (low1, pl.BlockSpec((2, 1, cells, LANES), lambda i: (0, i, 0, 0))),
+            (low_prev, rim_spec),
+            (low_next, rim_spec),
+            (x, x_spec),
+            (w_first_back, whole(w_first_back)),
+        ],
+        [
+            (x.shape, BF, x_spec),
+            (
+                (GROUPS, c_f, 3 * LANES),
+                F32,
+                pl.BlockSpec((GROUPS, c_f, 3 * LANES), lambda *_: (0, 0, 0)),
+            ),
+        ],
+        after=(grad_got,),
+    )
+    expand_part = sum(widen_blocks[g, g * b_f : (g + 1) * b_f] for g in range(GROUPS))
+    plane_view = plane_blocks.reshape(3, 3, GROUPS, b_f, GROUPS, b_f)
+    spatial_part = sum(plane_view[:, :, g, :, g] for g in range(GROUPS))
+    first_view = first_blocks.reshape(GROUPS, c_f, 3, GROUPS, b_f)
+    reduce_part = sum(first_view[g, :, :, g] for g in range(GROUPS)).transpose(1, 0, 2)
+
+    small = jnp.concatenate(
+        [reduce_part.reshape(-1), spatial_part.reshape(-1), expand_part.reshape(-1)]
+    )
+    share = -(-small.shape[0] // (devices * LANES)) * LANES
+    padded = jnp.pad(small, (0, share * devices - small.shape[0])).reshape(devices, share // LANES, LANES)
+    mine = jnp.sum(gather_stats(padded), axis=0)
+    copies = jnp.broadcast_to(mine[None], padded.shape)
+    (small_all,) = gate([gather_stats(copies)], slow_grad)
+    small_all = small_all.reshape(-1)
     first_size, plane_size = reduce_part.size, spatial_part.size
     fast_reduce_grad = small_all[:first_size].reshape(fast_reduce.shape)
     fast_spatial_grad = small_all[first_size : first_size + plane_size].reshape(fast_spatial.shape)

time: 891 us -> 858 us (0.963)
  waiting for transfers between devices: 304 us -> 280 us
  starting transfers between devices: 204 us -> 191 us
  blocking collectives: 51.5 us -> 61.7 us
    ppermute x45 -> x15, starting transfers between devices: 96.9 us -> 34.1 us  [exchange_pieces(): lax.ppermute(pieces[step], 'wa', [(i, i ^ step) for i in range(wa_count)])]
    ppermute x0 -> x30, waiting for transfers between devices: none -> 62.8 us  [send(): return lax.ppermute(piece, 'wa', [(i, i ^ step) for i in range(wa_count)])]
    ppermute x0 -> x30, starting transfers between devices: none -> 59.6 us  [send(): return lax.ppermute(piece, 'wa', [(i, i ^ step) for i in range(wa_count)])]
    ppermute x45 -> x15, waiting for transfers between devices: 86.2 us -> 33.7 us  [exchange_pieces(): lax.ppermute(pieces[step], 'wa', [(i, i ^ step) for i in range(wa_count)])]
    all_to_all x11, waiting for transfers between devices: 61.6 us -> 20.7 us  [gather_stats(): return lax.all_to_all(copies, axes, 0, 0, tiled=True)]
    all_to_all x2, waiting for transfers between devices: 0.01 us -> 15.8 us  [gather_wide(): return lax.all_to_all(copies, 'wa', 0, 0, tiled=True)]
    all_to_all x2, starting transfers between devices: 27.3 us -> 13.8 us  [gather_wide(): return lax.all_to_all(copies, 'wa', 0, 0, tiled=True)]
    all_to_all x3, blocking collectives: 49 us -> 59.2 us  [gather_stats(): return lax.all_to_all(copies, axes, 0, 0, tiled=True)]
  transfers between devices with their start and end apart: 85 -> 85, of which waited for: 28 -> 37; matrix products, arithmetic and copies ran while one was open for 6% -> 5% of each run, Pallas kernels for 20% -> 19%
where the time goes in v3:
time: 858 us; the launch traced here: 846 us
  waiting for transfers between devices  280 us (33%)
  Pallas kernels  218 us (25%)
  starting transfers between devices  191 us (22%)
  blocking collectives  61.7 us (7%)
  local copies, waits for them, and re-layouts  57.5 us (7%)
  other arithmetic  16.7 us (2%)
  between operations  16.3 us (2%)
    pallas_call x34, Pallas kernels, launch(): pl.pallas_call(kernel, name=name, grid=grid, in_specs=[spec for _, spec i...  218 us
    ppermute x3, waiting for transfers between devices, per_device(): lax.ppermute(second_stage, 'wa', [(i, i ^ step) for i in range(wa_count)])  68.6 us
    ppermute x30, waiting for transfers between devices, send(): return lax.ppermute(piece, 'wa', [(i, i ^ step) for i in range(wa_count)])  62.8 us
    ppermute x30, starting transfers between devices, send(): return lax.ppermute(piece, 'wa', [(i, i ^ step) for i in range(wa_count)])  59.6 us
    all_to_all x3, blocking collectives, gather_stats(): return lax.all_to_all(copies, axes, 0, 0, tiled=True)  59.2 us
    all_to_all x3, waiting for transfers between devices, exchange(): return lax.all_to_all(array, 'wa', 0, 0, tiled=True)  57 us
    all_to_all x11, starting transfers between devices, gather_stats(): return lax.all_to_all(copies, axes, 0, 0, tiled=True)  49.5 us
    ppermute x15, starting transfers between devices, exchange_pieces(): lax.ppermute(pieces[step], 'wa', [(i, i ^ step) for i in range(wa_count)])  34.1 us
  transfers between devices with their start and end apart: 85, of which 37 were waited for; matrix products, arithmetic and copies ran while one was open for 5% of the time, Pallas kernels for 19%

profile of v3, /device:TPU:0, one launch (start us, length us, event | category | flops | bytes accessed | tf_op | source)
XLA Modules:
  0.0 846.2 jit_solution(18151505610770159781)
XLA Ops:
  7.2 5.7 pack.2
  13.7 4.1 collective-permute-start.2
  30.0 6.5 collective-permute-done.2.refs_4_.refs_11_
  38.2 10.6 %collective-permute-done.4.refs_6_.refs_12_ = bf16[1024,128]{1,0:T(8,128)(2,1)S(1)} collective-permute-done((bf16[1024,128]{1,0:T(8,128)(2,1)}, bf16[1024,128]{1,0:T(8,128)(2,1)S(1)}, u32[]{:S(2)}, u32[]{:S(2)}) %collective-permute-start.4) | collective-permute-done | bytes 262176 | tf_op jit(solution)/shard_map/ppermute | solution.py:863
  52.0 5.5 collective-permute-start.10
  61.1 5.6 all-to-all-start
  69.5 8.4 collective-permute-start.12
  90.2 5.3 fast_plane.1
  95.5 6.1 all-to-all-start.1
  119.3 5.1 all-to-all-start.2
  127.7 13.2 %collective-permute-done.16.refs_10_.refs_18_ = bf16[1024,128]{1,0:T(8,128)(2,1)S(1)} collective-permute-done((bf16[1024,128]{1,0:T(8,128)(2,1)}, bf16[1024,128]{1,0:T(8,128)(2,1)S(1)}, u32[]{:S(2)}, u32[]{:S(2)}) %collective-permute-start.16) | collective-permute-done | bytes 262176 | tf_op jit(solution)/shard_map/ppermute | solution.py:863
  142.9 4.9 fast_out.1
  147.9 4.6 all-to-all-start.3
  153.1 14.1 %slow_enter.1 = (bf16[2,4,256,1024]{3,2,1,0:T(8,128)(2,1)}, f32[10,256,256]{2,1,0:T(8,128)}, bf16[2,4,256,1024]{3,2,1,0:T(8,128)(2,1)}) custom-call(s32[1]{0:T(128)} %bitcast.refs_0_.refs_2_, bf16[3,1280,256]{2,1,0:T(8,128)(2,1)} %refs_7_.9, bf16[1280,1024]{1,0:T(8,128)(2,1)} %refs_9_.1, bf16[1024,128]{1,0:T(8,128)(2,1)S(1)} %copy-done.96, ...), custom_call_target="tpu_custom_call" | custom-call | flops 7516192768 | bytes 19791876 | tf_op jit(solution)/shard_map/slow_enter/pallas_call | solution.py:50
  167.3 28.5 %all-to-all-done.3 = bf16[16,512,128]{2,1,0:T(8,128)(2,1)} async-done(((bf16[16,512,128]{2,1,0:T(8,128)(2,1)}), bf16[16,512,128]{2,1,0:T(8,128)(2,1)}, u32[]{:S(2)}, u32[]{:S(2)}) %all-to-all-start.3) | async-done | bytes 2097184 | tf_op jit(solution)/shard_map/all_to_all | solution.py:815
  195.7 4.5 lateral_enter.1
  200.2 9.4 %all-to-all-start.4 = ((f32[32,2,256]{2,1,0:T(2,128)}), f32[32,2,256]{2,1,0:T(2,128)S(1)}, u32[]{:S(2)}, u32[]{:S(2)}) async-start(f32[32,2,256]{2,1,0:T(2,128)} %get-tuple-element.187), calls=%async_computation.4 | async-start | bytes 131072 | tf_op jit(solution)/shard_map/all_to_all | solution.py:818
  209.6 6.0 pack.3
  226.0 5.5 narrow_enter.1
  232.5 25.0 %all_to_all.95.refs_3_.refs_0_.refs_9_.refs_4_ = f32[32,2,256]{2,1,0:T(2,128)S(1)} all-to-all(f32[32,2,256]{2,1,0:T(2,128)S(1)} %get-tuple-element.189), channel_id=1, replica_groups=mesh['dp'=2,'wa'=16] {'dp','wa'}, dimensions={0} | all-to-all | bytes 131072 | tf_op jit(solution)/shard_map/all_to_all | solution.py:818
  264.5 7.0 middle_enter.1
  271.6 4.9 all-to-all-start.6
  283.3 4.7 collective-permute-done.26.refs_14_
  290.0 9.1 %wide_enter.1 = (bf16[8,256,256]{2,1,0:T(8,128)(2,1)}, bf16[8,256,1024]{2,1,0:T(8,128)(2,1)}, f32[4,1024]{1,0:T(4,128)S(1)}) custom-call(f32[1,1]{1,0:T(1,128)} %bitcast.1.refs_0_, s32[1]{0:T(128)} %dynamic_slice.3.refs_0_.refs_1_, f32[8,256,256]{2,1,0:T(8,128)} %get-tuple-element.210.refs_2_.refs_8_.refs_3_, ...), custom_call_target="tpu_custom_call" | custom-call | bytes 17385480 | tf_op jit(solution)/shard_map/wide_enter/pallas_call | solution.py:50
  301.1 4.9 all-to-all-start.7
  315.1 4.2 collective-permute-start.32
  320.5 5.5 collective-permute-done.29.refs_16_
  326.0 9.6 %collective-permute-done.30.refs_22_ = bf16[1024,128]{1,0:T(8,128)(2,1)S(1)} collective-permute-done((bf16[1024,128]{1,0:T(8,128)(2,1)S(1)}, bf16[1024,128]{1,0:T(8,128)(2,1)S(1)}, u32[]{:S(2)}, u32[]{:S(2)}) %collective-permute-start.30) | collective-permute-done | bytes 262176 | tf_op jit(solution)/shard_map/ppermute | solution.py:879
  335.6 5.6 collective-permute-done.31.refs_23_
  342.0 4.8 collective-permute-done.32.refs_24_
  347.5 14.6 %wide_out.1 = (bf16[1024,128]{1,0:T(8,128)(2,1)S(1)}, bf16[1024,128]{1,0:T(8,128)(2,1)}, bf16[1024,128]{1,0:T(8,128)(2,1)}, bf16[1024,128]{1,0:T(8,128)(2,1)}, b...) custom-call(f32[1,1]{1,0:T(1,128)} %bitcast.1.refs_0_, ...), custom_call_target="tpu_custom_call" | custom-call | bytes 22839308 | tf_op jit(solution)/shard_map/wide_out/pallas_call | solution.py:50
  364.7 8.8 %all-to-all-start.8 = ((f32[16,4,1024]{2,1,0:T(4,128)}), f32[16,4,1024]{2,1,0:T(4,128)S(1)}, u32[]{:S(2)}, u32[]{:S(2)}) async-start(f32[16,4,1024]{2,1,0:T(4,128)} %broadcast_in_dim.10), calls=%async_computation.8 | async-start | bytes 524288 | tf_op jit(solution)/shard_map/all_to_all | solution.py:825
  379.8 15.8 %all-to-all-done.8.refs_5_ = f32[16,4,1024]{2,1,0:T(4,128)S(1)} async-done(((f32[16,4,1024]{2,1,0:T(4,128)}), f32[16,4,1024]{2,1,0:T(4,128)S(1)}, u32[]{:S(2)}, u32[]{:S(2)}) %all-to-all-start.8) | async-done | bytes 262176 | tf_op jit(solution)/shard_map/all_to_all | solution.py:825
  396.5 10.8 %middle_back.1 = (f32[8,256,256]{2,1,0:T(8,128)}, bf16[1024,256]{1,0:T(8,128)(2,1)S(1)}, f32[32,2,256]{2,1,0:T(2,128)}) custom-call(f32[1,1]{1,0:T(1,128)} %bitcast.1.refs_0_, s32[1]{0:T(128)} %dynamic_slice.3.refs_0_.refs_1_, f32[8,256,1024]{2,1,0:T(8,128)} %bitcast.119, bf16[8,256,256]{2,1,0:T(8,128)(2,1)} %get-tuple-element.227.refs_3_, ...), custom_call_target="tpu_custom_call" | custom-call | bytes 15345672 | tf_op jit(solution)/shard_map/middle_back/pallas_call | solution.py:50
  419.1 8.3 narrow_back.1
  439.6 22.0 %project_back.1 = (bf16[8,256,1280]{2,1,0:T(8,128)(2,1)}, bf16[5120,256]{1,0:T(8,128)(2,1)}) custom-call(f32[1,1]{1,0:T(1,128)} %bitcast.1.refs_0_, s32[1]{0:T(128)} %dynamic_slice.3.refs_0_.refs_1_, f32[8,256,1024]{2,1,0:T(8,128)} %bitcast.120, bf16[8,256,1024]{2,1,0:T(8,128)(2,1)} %get-tuple-element.228.refs_3_, f32[16,4,1024]{2,1,0:T(4,128)S(1)} %copy-done.7, ...), custom_call_target="tpu_custom_call" | custom-call | flops 10737418240 | bytes 28844040 | tf_op jit(solution)/shard_map/project_back/pallas_call | solution.py:50
  461.8 13.2 %join_back.1 = (bf16[10,256,256]{2,1,0:T(8,128)(2,1)}, bf16[16,1024,128]{2,1,0:T(8,128)(2,1)}, f32[2,4,256,256]{3,2,1,0:T(8,128)}, f32[32,2,256]{2,1,0:T(2,128)}) custom-call(f32[1,1]{1,0:T(1,128)} %bitcast.1.refs_0_, s32[1]{0:T(128)} %dynamic_slice.3.refs_0_.refs_1_, f32[8,256,256]{2,1,0:T(8,128)} %get-tuple-element.266.refs_2_, ...), custom_call_target="tpu_custom_call" | custom-call | bytes 22941704 | tf_op jit(solution)/shard_map/join_back/pallas_call | solution.py:50
  484.1 6.4 plane_weight.1
  494.3 6.6 weight_merge.1
  512.7 4.7 collective-permute-start.48
  520.0 5.0 collective-permute-done.40.refs_8_.refs_12_
  525.0 8.9 %collective-permute-done.46.refs_14_.refs_9_ = bf16[1024,128]{1,0:T(8,128)(2,1)S(1)} collective-permute-done((bf16[1024,128]{1,0:T(8,128)(2,1)}, bf16[1024,128]{1,0:T(8,128)(2,1)S(1)}, u32[]{:S(2)}, u32[]{:S(2)}) %collective-permute-start.46) | collective-permute-done | bytes 262176 | tf_op jit(solution)/shard_map/ppermute | solution.py:879
  534.0 6.0 collective-permute-done.47.refs_15_.refs_11_
  539.9 6.1 collective-permute-done.48.refs_16_.refs_13_
  546.1 5.6 all-to-all-done.12.refs_5_
  551.7 5.8 lateral_back.1
  557.6 4.6 all-to-all-start.13
  574.8 10.0 %collective-permute-done.56 = bf16[80,256]{1,0:T(8,128)(2,1)S(1)} collective-permute-done((bf16[80,256]{1,0:T(8,128)(2,1)S(1)}, bf16[80,256]{1,0:T(8,128)(2,1)S(1)}, u32[]{:S(2)}, u32[]{:S(2)}) %collective-permute-start.56) | collective-permute-done | bytes 40992 | tf_op jit(solution)/shard_map/ppermute | solution.py:1362
  586.9 28.5 %all-to-all-done.13 = bf16[16,512,128]{2,1,0:T(8,128)(2,1)} async-done(((bf16[16,512,128]{2,1,0:T(8,128)(2,1)}), bf16[16,512,128]{2,1,0:T(8,128)(2,1)}, u32[]{:S(2)}, u32[]{:S(2)}) %all-to-all-start.13) | async-done | bytes 2097184 | tf_op jit(solution)/shard_map/all_to_all | solution.py:815
  615.5 7.2 fast_back_sum.1
  622.6 23.9 %all_to_all.96.refs_5_ = f32[32,8,128]{2,1,0:T(8,128)S(1)} all-to-all(f32[32,8,128]{2,1,0:T(8,128)S(1)} %get-tuple-element.275), channel_id=1, replica_groups=mesh['dp'=2,'wa'=16] {'dp','wa'}, dimensions={0} | all-to-all | bytes 262144 | tf_op jit(solution)/shard_map/all_to_all | solution.py:818
  646.5 6.6 fast_back_widen.1
  653.1 10.3 %all_to_all.97.refs_4_ = f32[32,8,128]{2,1,0:T(8,128)S(1)} all-to-all(f32[32,8,128]{2,1,0:T(8,128)S(1)} %get-tuple-element.287), channel_id=1, replica_groups=mesh['dp'=2,'wa'=16] {'dp','wa'}, dimensions={0} | all-to-all | bytes 262144 | tf_op jit(solution)/shard_map/all_to_all | solution.py:818
  663.4 5.1 all-to-all-start.11
  682.9 7.9 unpack.2
  691.5 12.4 %collective-permute-done.58.refs_13_.refs_2_ = bf16[1616,256]{1,0:T(8,128)(2,1)S(1)} collective-permute-done((bf16[1616,256]{1,0:T(8,128)(2,1)S(1)}, bf16[1616,256]{1,0:T(8,128)(2,1)S(1)}, u32[]{:S(2)}, u32[]{:S(2)}) %collective-permute-start.58) | collective-permute-done | bytes 827424 | tf_op jit(solution)/shard_map/ppermute | solution.py:1418
  703.9 39.9 %collective-permute-done.59.refs_14_.refs_3_ = bf16[1616,256]{1,0:T(8,128)(2,1)} collective-permute-done((bf16[1616,256]{1,0:T(8,128)(2,1)S(1)}, bf16[1616,256]{1,0:T(8,128)(2,1)}, u32[]{:S(2)}, u32[]{:S(2)}) %collective-permute-start.59) | collective-permute-done | bytes 827424 | tf_op jit(solution)/shard_map/ppermute | solution.py:1418
  743.8 16.3 %collective-permute-done.60.refs_15_.refs_4_ = bf16[1616,256]{1,0:T(8,128)(2,1)} collective-permute-done((bf16[1616,256]{1,0:T(8,128)(2,1)S(1)}, bf16[1616,256]{1,0:T(8,128)(2,1)}, u32[]{:S(2)}, u32[]{:S(2)}) %collective-permute-start.60) | collective-permute-done | bytes 827424 | tf_op jit(solution)/shard_map/ppermute | solution.py:1418
  761.1 7.2 fast_back_plane.1
  772.8 7.8 unpack.3
  802.8 6.8 fast_back_out.1
  812.0 4.8 all-to-all-start.17
  816.8 7.9 all-to-all-done.17
  829.1 7.7 weight_split.1
  (472 shorter events, 227.4 us)
Async XLA Ops:
  13.7 22.8 %collective-permute-start.2 = (bf16[1024,128]{1,0:T(8,128)(2,1)}, bf16[1024,128]{1,0:T(8,128)(2,1)S(1)}, u32[]{:S(2)}, u32[]{:S(2)}) collective-permute-start(bf16[1024,128]{1,0:T(8,128)(2,1)} %get-tuple-element.163), channel_id=1, source_target_pairs={{0,8},{1,9},{2,10},{3,11},{4,12},{5,13},{6,14},{7,15},{8,0},{9,1},... | collective-permute-start | bytes 786440 | tf_op jit(solution)/shard_map/ppermute | solution.py:863
  17.8 20.5 %collective-permute-start.3 = (bf16[1024,128]{1,0:T(8,128)(2,1)S(1)}, bf16[1024,128]{1,0:T(8,128)(2,1)S(1)}, u32[]{:S(2)}, u32[]{:S(2)}) collective-permute-start(bf16[1024,128]{1,0:T(8,128)(2,1)S(1)} %get-tuple-element.164), channel_id=1, source_target_pairs={{0,1},{1,0},{2,3},{3,2},{4,5},{5,4},{6,7},{7,6},{8,9},{9,8},{10,11... | collective-permute-start | bytes 786440 | tf_op jit(solution)/shard_map/ppermute | solution.py:863
  19.3 29.6 %collective-permute-start.4 = (bf16[1024,128]{1,0:T(8,128)(2,1)}, bf16[1024,128]{1,0:T(8,128)(2,1)S(1)}, u32[]{:S(2)}, u32[]{:S(2)}) collective-permute-start(bf16[1024,128]{1,0:T(8,128)(2,1)} %get-tuple-element.165), channel_id=1, source_target_pairs={{0,9},{1,8},{2,11},{3,10},{4,13},{5,12},{6,15},{7,14},{8,1},{9,0},... | collective-permute-start | bytes 786440 | tf_op jit(solution)/shard_map/ppermute | solution.py:863
  25.0 27.0 %collective-permute-start = (bf16[4,256,128]{2,1,0:T(8,128)(2,1)S(1)}, bf16[4,256,128]{2,1,0:T(8,128)(2,1)S(1)}, u32[]{:S(2)}, u32[]{:S(2)}) collective-permute-start(bf16[4,256,128]{2,1,0:T(8,128)(2,1)S(1)} %get-tuple-element.161), channel_id=1, source_target_pairs={{0,1},{1,2},{2,3},{3,4},{4,5},{5,6},{6,7},{7,8},{8,9},{9,10},{10,1... | collective-permute-start | bytes 786440 | tf_op jit(solution)/shard_map/ppermute | solution.py:928
  28.7 23.3 %collective-permute-start.1 = (bf16[4,256,128]{2,1,0:T(8,128)(2,1)S(1)}, bf16[4,256,128]{2,1,0:T(8,128)(2,1)S(1)}, u32[]{:S(2)}, u32[]{:S(2)}) collective-permute-start(bf16[4,256,128]{2,1,0:T(8,128)(2,1)S(1)} %get-tuple-element.162), channel_id=1, source_target_pairs={{1,0},{2,1},{3,2},{4,3},{5,4},{6,5},{7,6},{8,7},{9,8},{10,9},{11,1... | collective-permute-start | bytes 786440 | tf_op jit(solution)/shard_map/ppermute | solution.py:929
  36.5 30.3 %collective-permute-start.5 = (bf16[1024,128]{1,0:T(8,128)(2,1)}, bf16[1024,128]{1,0:T(8,128)(2,1)S(1)}, u32[]{:S(2)}, u32[]{:S(2)}) collective-permute-start(bf16[1024,128]{1,0:T(8,128)(2,1)} %get-tuple-element.168), channel_id=1, source_target_pairs={{0,2},{1,3},{2,0},{3,1},{4,6},{5,7},{6,4},{7,5},{8,10},{9,11},{10,... | collective-permute-start | bytes 786440 | tf_op jit(solution)/shard_map/ppermute | solution.py:863
  38.2 31.2 %collective-permute-start.6 = (bf16[1024,128]{1,0:T(8,128)(2,1)}, bf16[1024,128]{1,0:T(8,128)(2,1)S(1)}, u32[]{:S(2)}, u32[]{:S(2)}) collective-permute-start(bf16[1024,128]{1,0:T(8,128)(2,1)} %get-tuple-element.169), channel_id=1, source_target_pairs={{0,10},{1,11},{2,8},{3,9},{4,14},{5,15},{6,12},{7,13},{8,2},{9,3},... | collective-permute-start | bytes 786440 | tf_op jit(solution)/shard_map/ppermute | solution.py:863
  48.9 29.0 %collective-permute-start.7 = (bf16[1024,128]{1,0:T(8,128)(2,1)S(1)}, bf16[1024,128]{1,0:T(8,128)(2,1)S(1)}, u32[]{:S(2)}, u32[]{:S(2)}) collective-permute-start(bf16[1024,128]{1,0:T(8,128)(2,1)S(1)} %get-tuple-element.170), channel_id=1, source_target_pairs={{0,3},{1,2},{2,1},{3,0},{4,7},{5,6},{6,5},{7,4},{8,11},{9,10},{10,... | collective-permute-start | bytes 786440 | tf_op jit(solution)/shard_map/ppermute | solution.py:863
  52.0 34.5 %collective-permute-start.8 = (bf16[1024,128]{1,0:T(8,128)(2,1)}, bf16[1024,128]{1,0:T(8,128)(2,1)S(1)}, u32[]{:S(2)}, u32[]{:S(2)}) collective-permute-start(bf16[1024,128]{1,0:T(8,128)(2,1)} %get-tuple-element.171), channel_id=1, source_target_pairs={{0,11},{1,10},{2,9},{3,8},{4,15},{5,14},{6,13},{7,12},{8,3},{9,2},... | collective-permute-start | bytes 786440 | tf_op jit(solution)/shard_map/ppermute | solution.py:863
  52.0 52.4 %collective-permute-start.10 = (bf16[1024,128]{1,0:T(8,128)(2,1)}, bf16[1024,128]{1,0:T(8,128)(2,1)S(1)}, u32[]{:S(2)}, u32[]{:S(2)}) collective-permute-start(bf16[1024,128]{1,0:T(8,128)(2,1)} %get-tuple-element.175), channel_id=1, source_target_pairs={{0,12},{1,13},{2,14},{3,15},{4,8},{5,9},{6,10},{7,11},{8,4},{9,5},... | collective-permute-start | bytes 786440 | tf_op jit(solution)/shard_map/ppermute | solution.py:863
  61.1 29.1 %all-to-all-start = ((f32[32,8,128]{2,1,0:T(8,128)}), f32[32,8,128]{2,1,0:T(8,128)S(1)}, u32[]{:S(2)}, u32[]{:S(2)}) async-start(f32[32,8,128]{2,1,0:T(8,128)} %get-tuple-element.167), calls=%async_computation | async-start | bytes 262144 | tf_op jit(solution)/shard_map/all_to_all | solution.py:818
  66.7 40.1 %collective-permute-start.11 = (bf16[1024,128]{1,0:T(8,128)(2,1)}, bf16[1024,128]{1,0:T(8,128)(2,1)S(1)}, u32[]{:S(2)}, u32[]{:S(2)}) collective-permute-start(bf16[1024,128]{1,0:T(8,128)(2,1)} %get-tuple-element.176), channel_id=1, source_target_pairs={{0,5},{1,4},{2,7},{3,6},{4,1},{5,0},{6,3},{7,2},{8,13},{9,12},{10,... | collective-permute-start | bytes 786440 | tf_op jit(solution)/shard_map/ppermute | solution.py:863
  69.5 40.5 %collective-permute-start.12 = (bf16[1024,128]{1,0:T(8,128)(2,1)}, bf16[1024,128]{1,0:T(8,128)(2,1)S(1)}, u32[]{:S(2)}, u32[]{:S(2)}) collective-permute-start(bf16[1024,128]{1,0:T(8,128)(2,1)} %get-tuple-element.177), channel_id=1, source_target_pairs={{0,13},{1,12},{2,15},{3,14},{4,9},{5,8},{6,11},{7,10},{8,5},{9,4},... | collective-permute-start | bytes 786440 | tf_op jit(solution)/shard_map/ppermute | solution.py:863
  77.9 33.9 %collective-permute-start.9 = (bf16[1024,128]{1,0:T(8,128)(2,1)}, bf16[1024,128]{1,0:T(8,128)(2,1)S(1)}, u32[]{:S(2)}, u32[]{:S(2)}) collective-permute-start(bf16[1024,128]{1,0:T(8,128)(2,1)} %copy-done.99), channel_id=1, source_target_pairs={{0,4},{1,5},{2,6},{3,7},{4,0},{5,1},{6,2},{7,3},{8,12},{9,13},{10,... | collective-permute-start | bytes 786440 | tf_op jit(solution)/shard_map/ppermute | solution.py:863
  95.5 17.0 %all-to-all-start.1 = ((f32[32,8,128]{2,1,0:T(8,128)}), f32[32,8,128]{2,1,0:T(8,128)S(1)}, u32[]{:S(2)}, u32[]{:S(2)}) async-start(f32[32,8,128]{2,1,0:T(8,128)} %get-tuple-element.173), calls=%async_computation.1 | async-start | bytes 262144 | tf_op jit(solution)/shard_map/all_to_all | solution.py:818
  101.7 22.6 %collective-permute-start.13 = (bf16[1024,128]{1,0:T(8,128)(2,1)S(1)}, bf16[1024,128]{1,0:T(8,128)(2,1)S(1)}, u32[]{:S(2)}, u32[]{:S(2)}) collective-permute-start(bf16[1024,128]{1,0:T(8,128)(2,1)S(1)} %copy-done.98), channel_id=1, source_target_pairs={{0,6},{1,7},{2,4},{3,5},{4,2},{5,3},{6,0},{7,1},{8,14},{9,15},{10,... | collective-permute-start | bytes 786440 | tf_op jit(solution)/shard_map/ppermute | solution.py:863
  104.4 21.2 %collective-permute-start.14 = (bf16[1024,128]{1,0:T(8,128)(2,1)}, bf16[1024,128]{1,0:T(8,128)(2,1)S(1)}, u32[]{:S(2)}, u32[]{:S(2)}) collective-permute-start(bf16[1024,128]{1,0:T(8,128)(2,1)} %get-tuple-element.181), channel_id=1, source_target_pairs={{0,14},{1,15},{2,12},{3,13},{4,10},{5,11},{6,8},{7,9},{8,6},{9,7},... | collective-permute-start | bytes 786440 | tf_op jit(solution)/shard_map/ppermute | solution.py:863
  107.5 20.2 %collective-permute-start.15 = (bf16[1024,128]{1,0:T(8,128)(2,1)}, bf16[1024,128]{1,0:T(8,128)(2,1)S(1)}, u32[]{:S(2)}, u32[]{:S(2)}) collective-permute-start(bf16[1024,128]{1,0:T(8,128)(2,1)} %get-tuple-element.182), channel_id=1, source_target_pairs={{0,7},{1,6},{2,5},{3,4},{4,3},{5,2},{6,1},{7,0},{8,15},{9,14},{10,... | collective-permute-start | bytes 786440 | tf_op jit(solution)/shard_map/ppermute | solution.py:863
  110.7 30.2 %collective-permute-start.16 = (bf16[1024,128]{1,0:T(8,128)(2,1)}, bf16[1024,128]{1,0:T(8,128)(2,1)S(1)}, u32[]{:S(2)}, u32[]{:S(2)}) collective-permute-start(bf16[1024,128]{1,0:T(8,128)(2,1)} %get-tuple-element.183), channel_id=1, source_target_pairs={{0,15},{1,14},{2,13},{3,12},{4,11},{5,10},{6,9},{7,8},{8,7},{9,6},... | collective-permute-start | bytes 786440 | tf_op jit(solution)/shard_map/ppermute | solution.py:863
  119.3 23.6 %all-to-all-start.2 = ((f32[32,8,128]{2,1,0:T(8,128)}), f32[32,8,128]{2,1,0:T(8,128)S(1)}, u32[]{:S(2)}, u32[]{:S(2)}) async-start(f32[32,8,128]{2,1,0:T(8,128)} %get-tuple-element.179), calls=%async_computation.2 | async-start | bytes 262144 | tf_op jit(solution)/shard_map/all_to_all | solution.py:818
  147.9 47.8 %all-to-all-start.3 = ((bf16[16,512,128]{2,1,0:T(8,128)(2,1)}), bf16[16,512,128]{2,1,0:T(8,128)(2,1)}, u32[]{:S(2)}, u32[]{:S(2)}) async-start(bf16[16,512,128]{2,1,0:T(8,128)(2,1)} %bitcast.123), calls=%async_computation.3 | async-start | bytes 4194304 | tf_op jit(solution)/shard_map/all_to_all | solution.py:815
  217.6 40.0 %collective-permute-start.17 = (bf16[1024,128]{1,0:T(8,128)(2,1)}, bf16[1024,128]{1,0:T(8,128)(2,1)S(1)}, u32[]{:S(2)}, u32[]{:S(2)}) collective-permute-start(bf16[1024,128]{1,0:T(8,128)(2,1)} %get-tuple-element.206), channel_id=1, source_target_pairs={{0,8},{1,9},{2,10},{3,11},{4,12},{5,13},{6,14},{7,15},{8,0},{9,1},... | collective-permute-start | bytes 786440 | tf_op jit(solution)/shard_map/ppermute | solution.py:879
  219.1 39.4 %collective-permute-start.18 = (bf16[1024,128]{1,0:T(8,128)(2,1)S(1)}, bf16[1024,128]{1,0:T(8,128)(2,1)S(1)}, u32[]{:S(2)}, u32[]{:S(2)}) collective-permute-start(bf16[1024,128]{1,0:T(8,128)(2,1)S(1)} %get-tuple-element.207), channel_id=1, source_target_pairs={{0,1},{1,0},{2,3},{3,2},{4,5},{5,4},{6,7},{7,6},{8,9},{9,8},{10,11... | collective-permute-start | bytes 786440 | tf_op jit(solution)/shard_map/ppermute | solution.py:879
  220.6 41.4 %collective-permute-start.19 = (bf16[1024,128]{1,0:T(8,128)(2,1)}, bf16[1024,128]{1,0:T(8,128)(2,1)S(1)}, u32[]{:S(2)}, u32[]{:S(2)}) collective-permute-start(bf16[1024,128]{1,0:T(8,128)(2,1)} %get-tuple-element.208), channel_id=1, source_target_pairs={{0,9},{1,8},{2,11},{3,10},{4,13},{5,12},{6,15},{7,14},{8,1},{9,0},... | collective-permute-start | bytes 786440 | tf_op jit(solution)/shard_map/ppermute | solution.py:879
  222.0 41.8 %collective-permute-start.20 = (bf16[1024,128]{1,0:T(8,128)(2,1)}, bf16[1024,128]{1,0:T(8,128)(2,1)S(1)}, u32[]{:S(2)}, u32[]{:S(2)}) collective-permute-start(bf16[1024,128]{1,0:T(8,128)(2,1)} %get-tuple-element.209), channel_id=1, source_target_pairs={{0,2},{1,3},{2,0},{3,1},{4,6},{5,7},{6,4},{7,5},{8,10},{9,11},{10,... | collective-permute-start | bytes 786440 | tf_op jit(solution)/shard_map/ppermute | solution.py:879
  222.8 41.7 %collective-permute-start.21 = (bf16[1024,128]{1,0:T(8,128)(2,1)}, bf16[1024,128]{1,0:T(8,128)(2,1)}, u32[]{:S(2)}, u32[]{:S(2)}) collective-permute-start(bf16[1024,128]{1,0:T(8,128)(2,1)} %get-tuple-element.214), channel_id=1, source_target_pairs={{0,10},{1,11},{2,8},{3,9},{4,14},{5,15},{6,12},{7,13},{8,2},{9,3},... | collective-permute-start | bytes 786440 | tf_op jit(solution)/shard_map/ppermute | solution.py:879
  257.6 18.9 %collective-permute-start.22 = (bf16[1024,128]{1,0:T(8,128)(2,1)}, bf16[1024,128]{1,0:T(8,128)(2,1)S(1)}, u32[]{:S(2)}, u32[]{:S(2)}) collective-permute-start(bf16[1024,128]{1,0:T(8,128)(2,1)} %get-tuple-element.215), channel_id=1, source_target_pairs={{0,3},{1,2},{2,1},{3,0},{4,7},{5,6},{6,5},{7,4},{8,11},{9,10},{10,... | collective-permute-start | bytes 786440 | tf_op jit(solution)/shard_map/ppermute | solution.py:879
  258.5 21.8 %collective-permute-start.23 = (bf16[1024,128]{1,0:T(8,128)(2,1)}, bf16[1024,128]{1,0:T(8,128)(2,1)S(1)}, u32[]{:S(2)}, u32[]{:S(2)}) collective-permute-start(bf16[1024,128]{1,0:T(8,128)(2,1)} %get-tuple-element.216), channel_id=1, source_target_pairs={{0,11},{1,10},{2,9},{3,8},{4,15},{5,14},{6,13},{7,12},{8,3},{9,2},... | collective-permute-start | bytes 786440 | tf_op jit(solution)/shard_map/ppermute | solution.py:879
  262.0 20.6 %collective-permute-start.24 = (bf16[1024,128]{1,0:T(8,128)(2,1)}, bf16[1024,128]{1,0:T(8,128)(2,1)S(1)}, u32[]{:S(2)}, u32[]{:S(2)}) collective-permute-start(bf16[1024,128]{1,0:T(8,128)(2,1)} %get-tuple-element.217), channel_id=1, source_target_pairs={{0,4},{1,5},{2,6},{3,7},{4,0},{5,1},{6,2},{7,3},{8,12},{9,13},{10,... | collective-permute-start | bytes 786440 | tf_op jit(solution)/shard_map/ppermute | solution.py:879
  263.8 19.5 %collective-permute-start.25 = (bf16[1024,128]{1,0:T(8,128)(2,1)}, bf16[1024,128]{1,0:T(8,128)(2,1)}, u32[]{:S(2)}, u32[]{:S(2)}) collective-permute-start(bf16[1024,128]{1,0:T(8,128)(2,1)} %get-tuple-element.225), channel_id=1, source_target_pairs={{0,12},{1,13},{2,14},{3,15},{4,8},{5,9},{6,10},{7,11},{8,4},{9,5},... | collective-permute-start | bytes 786440 | tf_op jit(solution)/shard_map/ppermute | solution.py:879
  264.5 23.5 %collective-permute-start.26 = (bf16[1024,128]{1,0:T(8,128)(2,1)S(1)}, bf16[1024,128]{1,0:T(8,128)(2,1)}, u32[]{:S(2)}, u32[]{:S(2)}) collective-permute-start(bf16[1024,128]{1,0:T(8,128)(2,1)S(1)} %get-tuple-element.226), channel_id=1, source_target_pairs={{0,5},{1,4},{2,7},{3,6},{4,1},{5,0},{6,3},{7,2},{8,13},{9,12},{10,... | collective-permute-start | bytes 786440 | tf_op jit(solution)/shard_map/ppermute | solution.py:879
  301.1 45.6 %all-to-all-start.7 = ((f32[16,4,1024]{2,1,0:T(4,128)}), f32[16,4,1024]{2,1,0:T(4,128)S(1)}, u32[]{:S(2)}, u32[]{:S(2)}) async-start(f32[16,4,1024]{2,1,0:T(4,128)} %broadcast_in_dim.9), calls=%async_computation.7 | async-start | bytes 524288 | tf_op jit(solution)/shard_map/all_to_all | solution.py:825
  308.9 17.1 %collective-permute-start.29 = (bf16[1024,128]{1,0:T(8,128)(2,1)S(1)}, bf16[1024,128]{1,0:T(8,128)(2,1)S(1)}, u32[]{:S(2)}, u32[]{:S(2)}) collective-permute-start(bf16[1024,128]{1,0:T(8,128)(2,1)S(1)} %copy-done.39), channel_id=1, source_target_pairs={{0,7},{1,6},{2,5},{3,4},{4,3},{5,2},{6,1},{7,0},{8,15},{9,14},{10,... | collective-permute-start | bytes 786440 | tf_op jit(solution)/shard_map/ppermute | solution.py:879
  310.4 25.2 %collective-permute-start.30 = (bf16[1024,128]{1,0:T(8,128)(2,1)S(1)}, bf16[1024,128]{1,0:T(8,128)(2,1)S(1)}, u32[]{:S(2)}, u32[]{:S(2)}) collective-permute-start(bf16[1024,128]{1,0:T(8,128)(2,1)S(1)} %copy-done.42), channel_id=1, source_target_pairs={{0,13},{1,12},{2,15},{3,14},{4,9},{5,8},{6,11},{7,10},{8,5},{9,4},... | collective-permute-start | bytes 786440 | tf_op jit(solution)/shard_map/ppermute | solution.py:879
  313.7 27.6 %collective-permute-start.31 = (bf16[1024,128]{1,0:T(8,128)(2,1)S(1)}, bf16[1024,128]{1,0:T(8,128)(2,1)S(1)}, u32[]{:S(2)}, u32[]{:S(2)}) collective-permute-start(bf16[1024,128]{1,0:T(8,128)(2,1)S(1)} %copy-done.45), channel_id=1, source_target_pairs={{0,14},{1,15},{2,12},{3,13},{4,10},{5,11},{6,8},{7,9},{8,6},{9,7},... | collective-permute-start | bytes 786440 | tf_op jit(solution)/shard_map/ppermute | solution.py:879
  315.1 31.6 %collective-permute-start.32 = (bf16[1024,128]{1,0:T(8,128)(2,1)S(1)}, bf16[1024,128]{1,0:T(8,128)(2,1)}, u32[]{:S(2)}, u32[]{:S(2)}) collective-permute-start(bf16[1024,128]{1,0:T(8,128)(2,1)S(1)} %copy-done.48), channel_id=1, source_target_pairs={{0,15},{1,14},{2,13},{3,12},{4,11},{5,10},{6,9},{7,8},{8,7},{9,6},... | collective-permute-start | bytes 786440 | tf_op jit(solution)/shard_map/ppermute | solution.py:879
  364.7 30.9 %all-to-all-start.8 = ((f32[16,4,1024]{2,1,0:T(4,128)}), f32[16,4,1024]{2,1,0:T(4,128)S(1)}, u32[]{:S(2)}, u32[]{:S(2)}) async-start(f32[16,4,1024]{2,1,0:T(4,128)} %broadcast_in_dim.10), calls=%async_computation.8 | async-start | bytes 524288 | tf_op jit(solution)/shard_map/all_to_all | solution.py:825
  373.5 45.6 %collective-permute-start.33 = (bf16[1024,128]{1,0:T(8,128)(2,1)}, bf16[1024,128]{1,0:T(8,128)(2,1)S(1)}, u32[]{:S(2)}, u32[]{:S(2)}) collective-permute-start(bf16[1024,128]{1,0:T(8,128)(2,1)} %get-tuple-element.237), channel_id=1, source_target_pairs={{0,1},{1,0},{2,3},{3,2},{4,5},{5,4},{6,7},{7,6},{8,9},{9,8},{10,11... | collective-permute-start | bytes 786440 | tf_op jit(solution)/shard_map/ppermute | solution.py:879
  375.4 43.7 %collective-permute-start.41 = (bf16[1024,128]{1,0:T(8,128)(2,1)}, bf16[1024,128]{1,0:T(8,128)(2,1)S(1)}, u32[]{:S(2)}, u32[]{:S(2)}) collective-permute-start(bf16[1024,128]{1,0:T(8,128)(2,1)} %get-tuple-element.257), channel_id=1, source_target_pairs={{0,8},{1,9},{2,10},{3,11},{4,12},{5,13},{6,14},{7,15},{8,0},{9,1},... | collective-permute-start | bytes 786440 | tf_op jit(solution)/shard_map/ppermute | solution.py:879
  377.8 41.3 %collective-permute-start.42 = (bf16[1024,128]{1,0:T(8,128)(2,1)}, bf16[1024,128]{1,0:T(8,128)(2,1)}, u32[]{:S(2)}, u32[]{:S(2)}) collective-permute-start(bf16[1024,128]{1,0:T(8,128)(2,1)} %get-tuple-element.258), channel_id=1, source_target_pairs={{0,9},{1,8},{2,11},{3,10},{4,13},{5,12},{6,15},{7,14},{8,1},{9,0},... | collective-permute-start | bytes 786440 | tf_op jit(solution)/shard_map/ppermute | solution.py:879
  378.0 61.5 %collective-permute-start.34 = (bf16[1024,128]{1,0:T(8,128)(2,1)}, bf16[1024,128]{1,0:T(8,128)(2,1)S(1)}, u32[]{:S(2)}, u32[]{:S(2)}) collective-permute-start(bf16[1024,128]{1,0:T(8,128)(2,1)} %get-tuple-element.238), channel_id=1, source_target_pairs={{0,2},{1,3},{2,0},{3,1},{4,6},{5,7},{6,4},{7,5},{8,10},{9,11},{10,... | collective-permute-start | bytes 786440 | tf_op jit(solution)/shard_map/ppermute | solution.py:879
  415.5 46.1 %collective-permute-start.43 = (bf16[1024,128]{1,0:T(8,128)(2,1)}, bf16[1024,128]{1,0:T(8,128)(2,1)S(1)}, u32[]{:S(2)}, u32[]{:S(2)}) collective-permute-start(bf16[1024,128]{1,0:T(8,128)(2,1)} %get-tuple-element.259), channel_id=1, source_target_pairs={{0,10},{1,11},{2,8},{3,9},{4,14},{5,15},{6,12},{7,13},{8,2},{9,3},... | collective-permute-start | bytes 786440 | tf_op jit(solution)/shard_map/ppermute | solution.py:879
  428.9 32.9 %all-to-all-start.10 = ((f32[32,2,256]{2,1,0:T(2,128)}), f32[32,2,256]{2,1,0:T(2,128)S(1)}, u32[]{:S(2)}, u32[]{:S(2)}) async-start(f32[32,2,256]{2,1,0:T(2,128)} %get-tuple-element.267), calls=%async_computation.10 | async-start | bytes 131072 | tf_op jit(solution)/shard_map/all_to_all | solution.py:818
  431.7 153.1 %reduce-scatter.2.cloned.1.call-start = ((), (), s32[]{:S(2)}) async-start(), calls=%async_computation.20 | async-start | bytes 3932160 | tf_op jit(solution)/shard_map/reduce_scatter | solution.py:1340
  432.9 28.9 %collective-permute-start.36 = (bf16[1024,128]{1,0:T(8,128)(2,1)}, bf16[1024,128]{1,0:T(8,128)(2,1)}, u32[]{:S(2)}, u32[]{:S(2)}) collective-permute-start(bf16[1024,128]{1,0:T(8,128)(2,1)} %get-tuple-element.252), channel_id=1, source_target_pairs={{0,3},{1,2},{2,1},{3,0},{4,7},{5,6},{6,5},{7,4},{8,11},{9,10},{10,... | collective-permute-start | bytes 786440 | tf_op jit(solution)/shard_map/ppermute | solution.py:879
  435.5 26.2 %collective-permute-start.37 = (bf16[1024,128]{1,0:T(8,128)(2,1)}, bf16[1024,128]{1,0:T(8,128)(2,1)}, u32[]{:S(2)}, u32[]{:S(2)}) collective-permute-start(bf16[1024,128]{1,0:T(8,128)(2,1)} %get-tuple-element.253), channel_id=1, source_target_pairs={{0,4},{1,5},{2,6},{3,7},{4,0},{5,1},{6,2},{7,3},{8,12},{9,13},{10,... | collective-permute-start | bytes 786440 | tf_op jit(solution)/shard_map/ppermute | solution.py:879
  437.0 24.8 %collective-permute-start.44 = (bf16[1024,128]{1,0:T(8,128)(2,1)}, bf16[1024,128]{1,0:T(8,128)(2,1)}, u32[]{:S(2)}, u32[]{:S(2)}) collective-permute-start(bf16[1024,128]{1,0:T(8,128)(2,1)} %get-tuple-element.260), channel_id=1, source_target_pairs={{0,11},{1,10},{2,9},{3,8},{4,15},{5,14},{6,13},{7,12},{8,3},{9,2},... | collective-permute-start | bytes 786440 | tf_op jit(solution)/shard_map/ppermute | solution.py:879
  439.4 22.4 %collective-permute-start.45 = (bf16[1024,128]{1,0:T(8,128)(2,1)}, bf16[1024,128]{1,0:T(8,128)(2,1)}, u32[]{:S(2)}, u32[]{:S(2)}) collective-permute-start(bf16[1024,128]{1,0:T(8,128)(2,1)} %get-tuple-element.261), channel_id=1, source_target_pairs={{0,12},{1,13},{2,14},{3,15},{4,8},{5,9},{6,10},{7,11},{8,4},{9,5},... | collective-permute-start | bytes 786440 | tf_op jit(solution)/shard_map/ppermute | solution.py:879
  461.6 32.6 %collective-permute-start.49 = (bf16[5120,256]{1,0:T(8,128)(2,1)}, bf16[5120,256]{1,0:T(8,128)(2,1)}, u32[]{:S(2)}, u32[]{:S(2)}) collective-permute-start(bf16[5120,256]{1,0:T(8,128)(2,1)} %get-tuple-element.276.refs_1_), channel_id=1, source_target_pairs={{0,16},{16,0},{1,17},{17,1},{2,18},{18,2},{3,19},{19,3},{4,20},{20... | collective-permute-start | bytes 7864328 | tf_op jit(solution)/shard_map/ppermute | solution.py:1328
  506.0 19.0 %collective-permute-start.40 = (bf16[1024,128]{1,0:T(8,128)(2,1)}, bf16[1024,128]{1,0:T(8,128)(2,1)S(1)}, u32[]{:S(2)}, u32[]{:S(2)}) collective-permute-start(bf16[1024,128]{1,0:T(8,128)(2,1)} %get-tuple-element.256), channel_id=1, source_target_pairs={{0,7},{1,6},{2,5},{3,4},{4,3},{5,2},{6,1},{7,0},{8,15},{9,14},{10,... | collective-permute-start | bytes 786440 | tf_op jit(solution)/shard_map/ppermute | solution.py:879
  507.1 26.9 %collective-permute-start.46 = (bf16[1024,128]{1,0:T(8,128)(2,1)}, bf16[1024,128]{1,0:T(8,128)(2,1)S(1)}, u32[]{:S(2)}, u32[]{:S(2)}) collective-permute-start(bf16[1024,128]{1,0:T(8,128)(2,1)} %get-tuple-element.262), channel_id=1, source_target_pairs={{0,13},{1,12},{2,15},{3,14},{4,9},{5,8},{6,11},{7,10},{8,5},{9,4},... | collective-permute-start | bytes 786440 | tf_op jit(solution)/shard_map/ppermute | solution.py:879
  510.3 29.6 %collective-permute-start.47 = (bf16[1024,128]{1,0:T(8,128)(2,1)}, bf16[1024,128]{1,0:T(8,128)(2,1)S(1)}, u32[]{:S(2)}, u32[]{:S(2)}) collective-permute-start(bf16[1024,128]{1,0:T(8,128)(2,1)} %get-tuple-element.263), channel_id=1, source_target_pairs={{0,14},{1,15},{2,12},{3,13},{4,10},{5,11},{6,8},{7,9},{8,6},{9,7},... | collective-permute-start | bytes 786440 | tf_op jit(solution)/shard_map/ppermute | solution.py:879
  512.7 33.4 %collective-permute-start.48 = (bf16[1024,128]{1,0:T(8,128)(2,1)}, bf16[1024,128]{1,0:T(8,128)(2,1)S(1)}, u32[]{:S(2)}, u32[]{:S(2)}) collective-permute-start(bf16[1024,128]{1,0:T(8,128)(2,1)} %get-tuple-element.264), channel_id=1, source_target_pairs={{0,15},{1,14},{2,13},{3,12},{4,11},{5,10},{6,9},{7,8},{8,7},{9,6},... | collective-permute-start | bytes 786440 | tf_op jit(solution)/shard_map/ppermute | solution.py:879
  517.4 34.3 %all-to-all-start.12 = ((f32[32,2,256]{2,1,0:T(2,128)}), f32[32,2,256]{2,1,0:T(2,128)S(1)}, u32[]{:S(2)}, u32[]{:S(2)}) async-start(f32[32,2,256]{2,1,0:T(2,128)} %get-tuple-element.272), calls=%async_computation.12 | async-start | bytes 131072 | tf_op jit(solution)/shard_map/all_to_all | solution.py:818
  557.6 57.9 %all-to-all-start.13 = ((bf16[16,512,128]{2,1,0:T(8,128)(2,1)}), bf16[16,512,128]{2,1,0:T(8,128)(2,1)}, u32[]{:S(2)}, u32[]{:S(2)}) async-start(bf16[16,512,128]{2,1,0:T(8,128)(2,1)} %bitcast.134), calls=%async_computation.13 | async-start | bytes 4194304 | tf_op jit(solution)/shard_map/all_to_all | solution.py:815
  562.2 84.3 %all-reduce.3.cloned.1.call-start = ((), (), s32[]{:S(2)}) async-start(), calls=%async_computation.21 | async-start | bytes 1654784 | tf_op jit(solution)/shard_map/psum | solution.py:1364
  663.4 105.7 %all-to-all-start.11 = ((bf16[16,1024,128]{2,1,0:T(8,128)(2,1)}), bf16[16,1024,128]{2,1,0:T(8,128)(2,1)}, u32[]{:S(2)}, u32[]{:S(2)}) async-start(bf16[16,1024,128]{2,1,0:T(8,128)(2,1)} %get-tuple-element.270), calls=%async_computation.11 | async-start | bytes 8388608 | tf_op jit(solution)/shard_map/all_to_all | solution.py:815
  674.2 29.6 %collective-permute-start.58 = (bf16[1616,256]{1,0:T(8,128)(2,1)S(1)}, bf16[1616,256]{1,0:T(8,128)(2,1)S(1)}, u32[]{:S(2)}, u32[]{:S(2)}) collective-permute-start(bf16[1616,256]{1,0:T(8,128)(2,1)S(1)} %copy-done.2), channel_id=1, source_target_pairs={{0,1},{1,0},{2,3},{3,2},{4,5},{5,4},{6,7},{7,6},{8,9},{9,8},{10,11... | collective-permute-start | bytes 2482184 | tf_op jit(solution)/shard_map/ppermute | solution.py:1418
  676.2 67.6 %collective-permute-start.59 = (bf16[1616,256]{1,0:T(8,128)(2,1)S(1)}, bf16[1616,256]{1,0:T(8,128)(2,1)}, u32[]{:S(2)}, u32[]{:S(2)}) collective-permute-start(bf16[1616,256]{1,0:T(8,128)(2,1)S(1)} %copy-done.2), channel_id=1, source_target_pairs={{0,2},{1,3},{2,0},{3,1},{4,6},{5,7},{6,4},{7,5},{8,10},{9,11},{10,... | collective-permute-start | bytes 2482184 | tf_op jit(solution)/shard_map/ppermute | solution.py:1418
  677.7 82.4 %collective-permute-start.60 = (bf16[1616,256]{1,0:T(8,128)(2,1)S(1)}, bf16[1616,256]{1,0:T(8,128)(2,1)}, u32[]{:S(2)}, u32[]{:S(2)}) collective-permute-start(bf16[1616,256]{1,0:T(8,128)(2,1)S(1)} %copy-done.2), channel_id=1, source_target_pairs={{0,3},{1,2},{2,1},{3,0},{4,7},{5,6},{6,5},{7,4},{8,11},{9,10},{10,... | collective-permute-start | bytes 2482184 | tf_op jit(solution)/shard_map/ppermute | solution.py:1418
  791.2 37.9 %collective-permute-start.63 = (bf16[1616,256]{1,0:T(8,128)(2,1)S(1)}, bf16[1616,256]{1,0:T(8,128)(2,1)}, u32[]{:S(2)}, u32[]{:S(2)}) collective-permute-start(bf16[1616,256]{1,0:T(8,128)(2,1)S(1)} %copy-done.3), channel_id=1, source_target_pairs={{0,16},{16,0},{1,17},{17,1},{2,18},{18,2},{3,19},{19,3},{4,20},{20... | collective-permute-start | bytes 2482184 | tf_op jit(solution)/shard_map/ppermute | solution.py:1453
  798.9 30.2 %collective-permute-start.64 = (bf16[1616,256]{1,0:T(8,128)(2,1)S(1)}, bf16[1616,256]{1,0:T(8,128)(2,1)}, u32[]{:S(2)}, u32[]{:S(2)}) collective-permute-start(bf16[1616,256]{1,0:T(8,128)(2,1)S(1)} %copy-done.9), channel_id=1, source_target_pairs={{0,16},{16,0},{1,17},{17,1},{2,18},{18,2},{3,19},{19,3},{4,20},{20... | collective-permute-start | bytes 2482184 | tf_op jit(solution)/shard_map/ppermute | solution.py:1453
  799.5 29.6 %collective-permute-start.65 = (bf16[1616,256]{1,0:T(8,128)(2,1)}, bf16[1616,256]{1,0:T(8,128)(2,1)}, u32[]{:S(2)}, u32[]{:S(2)}) collective-permute-start(bf16[1616,256]{1,0:T(8,128)(2,1)} %collective-permute-done.59.refs_14_.refs_3_), channel_id=1, source_target_pairs={{0,16},{16,0},{1,17},{17,1},{2,18},{18,2},{3,19},{19,3},{4,20},{20... | collective-permute-start | bytes 2482184 | tf_op jit(solution)/shard_map/ppermute | solution.py:1453
  800.9 28.2 %collective-permute-start.66 = (bf16[1616,256]{1,0:T(8,128)(2,1)}, bf16[1616,256]{1,0:T(8,128)(2,1)}, u32[]{:S(2)}, u32[]{:S(2)}) collective-permute-start(bf16[1616,256]{1,0:T(8,128)(2,1)} %collective-permute-done.60.refs_15_.refs_4_), channel_id=1, source_target_pairs={{0,16},{16,0},{1,17},{17,1},{2,18},{18,2},{3,19},{19,3},{4,20},{20... | collective-permute-start | bytes 2482184 | tf_op jit(solution)/shard_map/ppermute | solution.py:1453
  (135 other events, 1958.8 us)
Sparse Core Ops, SparseCore 0:
  501.1 83.4 reduce-scatter.1
  587.6 58.2 all-reduce.2

commit v4 on v3

--- a/solution.py
+++ b/solution.py
@@ -13,7 +13,7 @@
 LANES = 128
 GROUPS = 4
 VMEM_BYTES = 52 * 1024 * 1024
-CUT_SLOW = (3, 7, 11, 15)
+CUT_SLOW = (2, 6, 10, 15)
 CUT_COT = (0, 4, 10)
 CUT_RESULT = (0, 3, 9)
 GATE_COT = 8

time: 858 us -> 848 us (0.988)
  waiting for transfers between devices: 280 us -> 269 us
    ppermute x15, waiting for transfers between devices: 33.7 us -> 16.3 us  [exchange_pieces(): lax.ppermute(pieces[step], 'wa', [(i, i ^ step) for i in range(wa_count)])]
    unnamed x229 -> x255, local copies, waits for them, and re-layouts: 29.5 us -> 29.2 us
  transfers between devices with their start and end apart: 85 -> 85, of which waited for: 37 -> 37; matrix products, arithmetic and copies ran while one was open for 5% -> 5% of each run, Pallas kernels for 19% -> 20%
where the time goes in v4:
time: 848 us; the launch traced here: 836 us
  waiting for transfers between devices  269 us (32%)
  Pallas kernels  218 us (26%)
  starting transfers between devices  193 us (23%)
  blocking collectives  62 us (7%)
  local copies, waits for them, and re-layouts  54.5 us (6%)
  other arithmetic  18.2 us (2%)
  between operations  16.4 us (2%)
    pallas_call x34, Pallas kernels, launch(): pl.pallas_call(kernel, name=name, grid=grid, in_specs=[spec for _, spec i...  218 us
    ppermute x3, waiting for transfers between devices, per_device(): lax.ppermute(second_stage, 'wa', [(i, i ^ step) for i in range(wa_count)])  65.7 us
    ppermute x30, waiting for transfers between devices, send(): return lax.ppermute(piece, 'wa', [(i, i ^ step) for i in range(wa_count)])  64.3 us
    ppermute x30, starting transfers between devices, send(): return lax.ppermute(piece, 'wa', [(i, i ^ step) for i in range(wa_count)])  59.6 us
    all_to_all x3, blocking collectives, gather_stats(): return lax.all_to_all(copies, axes, 0, 0, tiled=True)  59.5 us
    all_to_all x3, waiting for transfers between devices, exchange(): return lax.all_to_all(array, 'wa', 0, 0, tiled=True)  56.4 us
    all_to_all x11, starting transfers between devices, gather_stats(): return lax.all_to_all(copies, axes, 0, 0, tiled=True)  52 us
    ppermute x15, starting transfers between devices, exchange_pieces(): lax.ppermute(pieces[step], 'wa', [(i, i ^ step) for i in range(wa_count)])  34.4 us
  transfers between devices with their start and end apart: 85, of which 37 were waited for; matrix products, arithmetic and copies ran while one was open for 5% of the time, Pallas kernels for 20%

profile of v4, /device:TPU:0, one launch (start us, length us, event | category | flops | bytes accessed | tf_op | source)
XLA Modules:
  0.0 836.3 jit_solution(483601430746827531)
XLA Ops:
  7.2 5.7 pack.2
  13.0 4.1 collective-permute-start.2
  41.6 4.6 collective-permute-done.1.refs_2_
  49.8 13.4 %all-to-all-start = ((f32[32,8,128]{2,1,0:T(8,128)}), f32[32,8,128]{2,1,0:T(8,128)S(1)}, u32[]{:S(2)}, u32[]{:S(2)}) async-start(f32[32,8,128]{2,1,0:T(8,128)} %get-tuple-element.166), calls=%async_computation | async-start | bytes 262144 | tf_op jit(solution)/shard_map/all_to_all | solution.py:818
  74.4 5.4 fast_plane.1
  83.3 4.6 collective-permute-start.12
  92.7 4.2 collective-permute-start.16
  108.6 6.1 collective-permute-done.15.refs_10_
  114.7 8.4 collective-permute-done.16.refs_11_.refs_18_
  123.1 8.4 %all-to-all-done.2.refs_4_.refs_6_ = f32[32,8,128]{2,1,0:T(8,128)S(1)} async-done(((f32[32,8,128]{2,1,0:T(8,128)}), f32[32,8,128]{2,1,0:T(8,128)S(1)}, u32[]{:S(2)}, u32[]{:S(2)}) %all-to-all-start.2) | async-done | bytes 131104 | tf_op jit(solution)/shard_map/all_to_all | solution.py:818
  131.5 5.0 fast_out.1
  136.6 4.6 all-to-all-start.3
  141.8 14.2 %slow_enter.1 = (bf16[2,4,256,1024]{3,2,1,0:T(8,128)(2,1)}, f32[10,256,256]{2,1,0:T(8,128)}, bf16[2,4,256,1024]{3,2,1,0:T(8,128)(2,1)}) custom-call(s32[1]{0:T(128)} %bitcast.refs_0_.refs_2_, bf16[3,1280,256]{2,1,0:T(8,128)(2,1)} %refs_7_.9, bf16[1280,1024]{1,0:T(8,128)(2,1)} %refs_9_.1, bf16[1024,128]{1,0:T(8,128)(2,1)S(1)} %copy-done.110, ...), custom_call_target="tpu_custom_call" | custom-call | flops 7516192768 | bytes 19791876 | tf_op jit(solution)/shard_map/slow_enter/pallas_call | solution.py:50
  155.9 28.5 %all-to-all-done.3 = bf16[16,512,128]{2,1,0:T(8,128)(2,1)} async-done(((bf16[16,512,128]{2,1,0:T(8,128)(2,1)}), bf16[16,512,128]{2,1,0:T(8,128)(2,1)}, u32[]{:S(2)}, u32[]{:S(2)}) %all-to-all-start.3) | async-done | bytes 2097184 | tf_op jit(solution)/shard_map/all_to_all | solution.py:815
  184.4 4.5 lateral_enter.1
  188.9 9.4 %all-to-all-start.4 = ((f32[32,2,256]{2,1,0:T(2,128)}), f32[32,2,256]{2,1,0:T(2,128)S(1)}, u32[]{:S(2)}, u32[]{:S(2)}) async-start(f32[32,2,256]{2,1,0:T(2,128)} %get-tuple-element.187), calls=%async_computation.4 | async-start | bytes 131072 | tf_op jit(solution)/shard_map/all_to_all | solution.py:818
  198.3 6.0 pack.3
  214.1 5.5 narrow_enter.1
  220.6 25.0 %all_to_all.95.refs_3_.refs_0_.refs_9_.refs_4_ = f32[32,2,256]{2,1,0:T(2,128)S(1)} all-to-all(f32[32,2,256]{2,1,0:T(2,128)S(1)} %get-tuple-element.189), channel_id=1, replica_groups=mesh['dp'=2,'wa'=16] {'dp','wa'}, dimensions={0} | all-to-all | bytes 131072 | tf_op jit(solution)/shard_map/all_to_all | solution.py:818
  252.6 7.0 middle_enter.1
  259.6 4.9 all-to-all-start.6
  270.7 5.3 collective-permute-done.26.refs_14_
  277.1 9.1 %wide_enter.1 = (bf16[8,256,256]{2,1,0:T(8,128)(2,1)}, bf16[8,256,1024]{2,1,0:T(8,128)(2,1)}, f32[4,1024]{1,0:T(4,128)S(1)}) custom-call(f32[1,1]{1,0:T(1,128)} %bitcast.1.refs_0_, s32[1]{0:T(128)} %dynamic_slice.3.refs_0_.refs_1_, f32[8,256,256]{2,1,0:T(8,128)} %get-tuple-element.210.refs_2_.refs_8_.refs_3_, ...), custom_call_target="tpu_custom_call" | custom-call | bytes 17385480 | tf_op jit(solution)/shard_map/wide_enter/pallas_call | solution.py:50
  288.2 4.9 all-to-all-start.7
  302.1 4.2 collective-permute-start.32
  307.6 5.5 collective-permute-done.29.refs_16_
  313.1 9.7 %collective-permute-done.30.refs_22_ = bf16[1024,128]{1,0:T(8,128)(2,1)S(1)} collective-permute-done((bf16[1024,128]{1,0:T(8,128)(2,1)S(1)}, bf16[1024,128]{1,0:T(8,128)(2,1)S(1)}, u32[]{:S(2)}, u32[]{:S(2)}) %collective-permute-start.30) | collective-permute-done | bytes 262176 | tf_op jit(solution)/shard_map/ppermute | solution.py:879
  322.7 5.6 collective-permute-done.31.refs_23_
  328.3 5.5 collective-permute-done.32.refs_24_
  334.5 14.3 %wide_out.1 = (bf16[1024,128]{1,0:T(8,128)(2,1)S(1)}, bf16[1024,128]{1,0:T(8,128)(2,1)S(1)}, bf16[1024,128]{1,0:T(8,128)(2,1)}, bf16[1024,128]{1,0:T(8,128)(2,1)...) custom-call(f32[1,1]{1,0:T(1,128)} %bitcast.1.refs_0_, ...), custom_call_target="tpu_custom_call" | custom-call | bytes 22839308 | tf_op jit(solution)/shard_map/wide_out/pallas_call | solution.py:50
  353.0 8.8 %all-to-all-start.8 = ((f32[16,4,1024]{2,1,0:T(4,128)}), f32[16,4,1024]{2,1,0:T(4,128)S(1)}, u32[]{:S(2)}, u32[]{:S(2)}) async-start(f32[16,4,1024]{2,1,0:T(4,128)} %broadcast_in_dim.10), calls=%async_computation.8 | async-start | bytes 524288 | tf_op jit(solution)/shard_map/all_to_all | solution.py:825
  368.1 15.8 %all-to-all-done.8.refs_5_ = f32[16,4,1024]{2,1,0:T(4,128)S(1)} async-done(((f32[16,4,1024]{2,1,0:T(4,128)}), f32[16,4,1024]{2,1,0:T(4,128)S(1)}, u32[]{:S(2)}, u32[]{:S(2)}) %all-to-all-start.8) | async-done | bytes 262176 | tf_op jit(solution)/shard_map/all_to_all | solution.py:825
  384.8 10.8 %middle_back.1 = (f32[8,256,256]{2,1,0:T(8,128)}, bf16[1024,256]{1,0:T(8,128)(2,1)S(1)}, f32[32,2,256]{2,1,0:T(2,128)}) custom-call(f32[1,1]{1,0:T(1,128)} %bitcast.1.refs_0_, s32[1]{0:T(128)} %dynamic_slice.3.refs_0_.refs_1_, f32[8,256,1024]{2,1,0:T(8,128)} %bitcast.119, bf16[8,256,256]{2,1,0:T(8,128)(2,1)} %get-tuple-element.227.refs_3_, ...), custom_call_target="tpu_custom_call" | custom-call | bytes 15345672 | tf_op jit(solution)/shard_map/middle_back/pallas_call | solution.py:50
  407.5 8.3 narrow_back.1
  428.8 22.0 %project_back.1 = (bf16[8,256,1280]{2,1,0:T(8,128)(2,1)}, bf16[5120,256]{1,0:T(8,128)(2,1)}) custom-call(f32[1,1]{1,0:T(1,128)} %bitcast.1.refs_0_, s32[1]{0:T(128)} %dynamic_slice.3.refs_0_.refs_1_, f32[8,256,1024]{2,1,0:T(8,128)} %bitcast.120, bf16[8,256,1024]{2,1,0:T(8,128)(2,1)} %get-tuple-element.228.refs_3_, f32[16,4,1024]{2,1,0:T(4,128)S(1)} %copy-done.9, ...), custom_call_target="tpu_custom_call" | custom-call | flops 10737418240 | bytes 28844040 | tf_op jit(solution)/shard_map/project_back/pallas_call | solution.py:50
  451.0 13.3 %join_back.1 = (bf16[10,256,256]{2,1,0:T(8,128)(2,1)}, bf16[16,1024,128]{2,1,0:T(8,128)(2,1)}, f32[2,4,256,256]{3,2,1,0:T(8,128)}, f32[32,2,256]{2,1,0:T(2,128)S(1)}) custom-call(f32[1,1]{1,0:T(1,128)} %bitcast.1.refs_0_, s32[1]{0:T(128)} %dynamic_slice.3.refs_0_.refs_1_, f32[8,256,256]{2,1,0:T(8,128)} %get-tuple-element.266.refs_2_, ...), custom_call_target="tpu_custom_call" | custom-call | bytes 22941704 | tf_op jit(solution)/shard_map/join_back/pallas_call | solution.py:50
  473.4 6.4 plane_weight.1
  483.6 6.6 weight_merge.1
  502.0 4.7 collective-permute-start.48
  509.3 4.9 collective-permute-done.40.refs_8_.refs_12_
  514.3 9.0 %collective-permute-done.46.refs_14_.refs_9_ = bf16[1024,128]{1,0:T(8,128)(2,1)S(1)} collective-permute-done((bf16[1024,128]{1,0:T(8,128)(2,1)}, bf16[1024,128]{1,0:T(8,128)(2,1)S(1)}, u32[]{:S(2)}, u32[]{:S(2)}) %collective-permute-start.46) | collective-permute-done | bytes 262176 | tf_op jit(solution)/shard_map/ppermute | solution.py:879
  523.3 6.0 collective-permute-done.47.refs_15_.refs_11_
  529.2 6.1 collective-permute-done.48.refs_16_.refs_13_
  535.4 5.6 all-to-all-done.12.refs_5_
  541.0 5.8 lateral_back.1
  546.9 4.6 all-to-all-start.13
  564.1 10.1 %collective-permute-done.56 = bf16[80,256]{1,0:T(8,128)(2,1)S(1)} collective-permute-done((bf16[80,256]{1,0:T(8,128)(2,1)S(1)}, bf16[80,256]{1,0:T(8,128)(2,1)S(1)}, u32[]{:S(2)}, u32[]{:S(2)}) %collective-permute-start.56) | collective-permute-done | bytes 40992 | tf_op jit(solution)/shard_map/ppermute | solution.py:1362
  576.5 27.9 %all-to-all-done.13 = bf16[16,512,128]{2,1,0:T(8,128)(2,1)} async-done(((bf16[16,512,128]{2,1,0:T(8,128)(2,1)}), bf16[16,512,128]{2,1,0:T(8,128)(2,1)}, u32[]{:S(2)}, u32[]{:S(2)}) %all-to-all-start.13) | async-done | bytes 2097184 | tf_op jit(solution)/shard_map/all_to_all | solution.py:815
  604.4 7.2 fast_back_sum.1
  611.6 24.3 %all_to_all.96.refs_5_ = f32[32,8,128]{2,1,0:T(8,128)S(1)} all-to-all(f32[32,8,128]{2,1,0:T(8,128)S(1)} %get-tuple-element.275), channel_id=1, replica_groups=mesh['dp'=2,'wa'=16] {'dp','wa'}, dimensions={0} | all-to-all | bytes 262144 | tf_op jit(solution)/shard_map/all_to_all | solution.py:818
  635.9 6.6 fast_back_widen.1
  643.1 10.3 %all_to_all.97.refs_4_ = f32[32,8,128]{2,1,0:T(8,128)S(1)} all-to-all(f32[32,8,128]{2,1,0:T(8,128)S(1)} %get-tuple-element.287), channel_id=1, replica_groups=mesh['dp'=2,'wa'=16] {'dp','wa'}, dimensions={0} | all-to-all | bytes 262144 | tf_op jit(solution)/shard_map/all_to_all | solution.py:818
  653.3 5.1 all-to-all-start.11
  675.8 7.8 unpack.2
  684.3 9.5 %collective-permute-done.58.refs_13_.refs_2_ = bf16[1616,256]{1,0:T(8,128)(2,1)S(1)} collective-permute-done((bf16[1616,256]{1,0:T(8,128)(2,1)S(1)}, bf16[1616,256]{1,0:T(8,128)(2,1)S(1)}, u32[]{:S(2)}, u32[]{:S(2)}) %collective-permute-start.58) | collective-permute-done | bytes 827424 | tf_op jit(solution)/shard_map/ppermute | solution.py:1418
  693.8 39.9 %collective-permute-done.59.refs_14_.refs_3_ = bf16[1616,256]{1,0:T(8,128)(2,1)} collective-permute-done((bf16[1616,256]{1,0:T(8,128)(2,1)S(1)}, bf16[1616,256]{1,0:T(8,128)(2,1)}, u32[]{:S(2)}, u32[]{:S(2)}) %collective-permute-start.59) | collective-permute-done | bytes 827424 | tf_op jit(solution)/shard_map/ppermute | solution.py:1418
  733.7 16.3 %collective-permute-done.60.refs_15_.refs_4_ = bf16[1616,256]{1,0:T(8,128)(2,1)} collective-permute-done((bf16[1616,256]{1,0:T(8,128)(2,1)S(1)}, bf16[1616,256]{1,0:T(8,128)(2,1)}, u32[]{:S(2)}, u32[]{:S(2)}) %collective-permute-start.60) | collective-permute-done | bytes 827424 | tf_op jit(solution)/shard_map/ppermute | solution.py:1418
  751.1 7.2 fast_back_plane.1
  762.8 7.8 unpack.3
  775.4 4.5 collective-permute-start.61
  792.9 7.0 fast_back_out.1
  802.3 4.6 all-to-all-start.17
  807.7 7.1 all-to-all-done.17
  819.3 7.7 weight_split.1
  (498 shorter events, 226.7 us)
Async XLA Ops:
  13.0 17.5 %collective-permute-start.2 = (bf16[1024,128]{1,0:T(8,128)(2,1)}, bf16[1024,128]{1,0:T(8,128)(2,1)S(1)}, u32[]{:S(2)}, u32[]{:S(2)}) collective-permute-start(bf16[1024,128]{1,0:T(8,128)(2,1)} %get-tuple-element.163), channel_id=1, source_target_pairs={{0,8},{1,9},{2,10},{3,11},{4,12},{5,13},{6,14},{7,15},{8,0},{9,1},... | collective-permute-start | bytes 786440 | tf_op jit(solution)/shard_map/ppermute | solution.py:863
  26.2 20.0 %collective-permute-start.1 = (bf16[4,256,128]{2,1,0:T(8,128)(2,1)S(1)}, bf16[4,256,128]{2,1,0:T(8,128)(2,1)S(1)}, u32[]{:S(2)}, u32[]{:S(2)}) collective-permute-start(bf16[4,256,128]{2,1,0:T(8,128)(2,1)S(1)} %get-tuple-element.162), channel_id=1, source_target_pairs={{1,0},{2,1},{3,2},{4,3},{5,4},{6,5},{7,6},{8,7},{9,8},{10,9},{11,1... | collective-permute-start | bytes 786440 | tf_op jit(solution)/shard_map/ppermute | solution.py:929
  27.5 35.7 %collective-permute-start.4 = (bf16[1024,128]{1,0:T(8,128)(2,1)}, bf16[1024,128]{1,0:T(8,128)(2,1)S(1)}, u32[]{:S(2)}, u32[]{:S(2)}) collective-permute-start(bf16[1024,128]{1,0:T(8,128)(2,1)} %get-tuple-element.167), channel_id=1, source_target_pairs={{0,9},{1,8},{2,11},{3,10},{4,13},{5,12},{6,15},{7,14},{8,1},{9,0},... | collective-permute-start | bytes 786440 | tf_op jit(solution)/shard_map/ppermute | solution.py:863
  30.4 35.6 %collective-permute-start.5 = (bf16[1024,128]{1,0:T(8,128)(2,1)S(1)}, bf16[1024,128]{1,0:T(8,128)(2,1)S(1)}, u32[]{:S(2)}, u32[]{:S(2)}) collective-permute-start(bf16[1024,128]{1,0:T(8,128)(2,1)S(1)} %get-tuple-element.168), channel_id=1, source_target_pairs={{0,2},{1,3},{2,0},{3,1},{4,6},{5,7},{6,4},{7,5},{8,10},{9,11},{10,... | collective-permute-start | bytes 786440 | tf_op jit(solution)/shard_map/ppermute | solution.py:863
  32.2 37.2 %collective-permute-start.6 = (bf16[1024,128]{1,0:T(8,128)(2,1)}, bf16[1024,128]{1,0:T(8,128)(2,1)S(1)}, u32[]{:S(2)}, u32[]{:S(2)}) collective-permute-start(bf16[1024,128]{1,0:T(8,128)(2,1)} %get-tuple-element.169), channel_id=1, source_target_pairs={{0,10},{1,11},{2,8},{3,9},{4,14},{5,15},{6,12},{7,13},{8,2},{9,3},... | collective-permute-start | bytes 786440 | tf_op jit(solution)/shard_map/ppermute | solution.py:863
  38.6 35.8 %collective-permute-start.7 = (bf16[1024,128]{1,0:T(8,128)(2,1)}, bf16[1024,128]{1,0:T(8,128)(2,1)S(1)}, u32[]{:S(2)}, u32[]{:S(2)}) collective-permute-start(bf16[1024,128]{1,0:T(8,128)(2,1)} %get-tuple-element.170), channel_id=1, source_target_pairs={{0,3},{1,2},{2,1},{3,0},{4,7},{5,6},{6,5},{7,4},{8,11},{9,10},{10,... | collective-permute-start | bytes 786440 | tf_op jit(solution)/shard_map/ppermute | solution.py:863
  46.2 41.7 %collective-permute-start.10 = (bf16[1024,128]{1,0:T(8,128)(2,1)}, bf16[1024,128]{1,0:T(8,128)(2,1)S(1)}, u32[]{:S(2)}, u32[]{:S(2)}) collective-permute-start(bf16[1024,128]{1,0:T(8,128)(2,1)} %get-tuple-element.175), channel_id=1, source_target_pairs={{0,12},{1,13},{2,14},{3,15},{4,8},{5,9},{6,10},{7,11},{8,4},{9,5},... | collective-permute-start | bytes 786440 | tf_op jit(solution)/shard_map/ppermute | solution.py:863
  49.8 24.6 %all-to-all-start = ((f32[32,8,128]{2,1,0:T(8,128)}), f32[32,8,128]{2,1,0:T(8,128)S(1)}, u32[]{:S(2)}, u32[]{:S(2)}) async-start(f32[32,8,128]{2,1,0:T(8,128)} %get-tuple-element.166), calls=%async_computation | async-start | bytes 262144 | tf_op jit(solution)/shard_map/all_to_all | solution.py:818
  63.3 25.2 %collective-permute-start.11 = (bf16[1024,128]{1,0:T(8,128)(2,1)}, bf16[1024,128]{1,0:T(8,128)(2,1)S(1)}, u32[]{:S(2)}, u32[]{:S(2)}) collective-permute-start(bf16[1024,128]{1,0:T(8,128)(2,1)} %get-tuple-element.176), channel_id=1, source_target_pairs={{0,5},{1,4},{2,7},{3,6},{4,1},{5,0},{6,3},{7,2},{8,13},{9,12},{10,... | collective-permute-start | bytes 786440 | tf_op jit(solution)/shard_map/ppermute | solution.py:863
  66.0 23.9 %collective-permute-start.8 = (bf16[1024,128]{1,0:T(8,128)(2,1)}, bf16[1024,128]{1,0:T(8,128)(2,1)S(1)}, u32[]{:S(2)}, u32[]{:S(2)}) collective-permute-start(bf16[1024,128]{1,0:T(8,128)(2,1)} %get-tuple-element.173), channel_id=1, source_target_pairs={{0,11},{1,10},{2,9},{3,8},{4,15},{5,14},{6,13},{7,12},{8,3},{9,2},... | collective-permute-start | bytes 786440 | tf_op jit(solution)/shard_map/ppermute | solution.py:863
  69.4 22.7 %collective-permute-start.9 = (bf16[1024,128]{1,0:T(8,128)(2,1)}, bf16[1024,128]{1,0:T(8,128)(2,1)S(1)}, u32[]{:S(2)}, u32[]{:S(2)}) collective-permute-start(bf16[1024,128]{1,0:T(8,128)(2,1)} %copy-done.112), channel_id=1, source_target_pairs={{0,4},{1,5},{2,6},{3,7},{4,0},{5,1},{6,2},{7,3},{8,12},{9,13},{10,... | collective-permute-start | bytes 786440 | tf_op jit(solution)/shard_map/ppermute | solution.py:863
  79.8 17.8 %all-to-all-start.1 = ((f32[32,8,128]{2,1,0:T(8,128)}), f32[32,8,128]{2,1,0:T(8,128)S(1)}, u32[]{:S(2)}, u32[]{:S(2)}) async-start(f32[32,8,128]{2,1,0:T(8,128)} %get-tuple-element.172), calls=%async_computation.1 | async-start | bytes 262144 | tf_op jit(solution)/shard_map/all_to_all | solution.py:818
  83.3 23.4 %collective-permute-start.12 = (bf16[1024,128]{1,0:T(8,128)(2,1)}, bf16[1024,128]{1,0:T(8,128)(2,1)S(1)}, u32[]{:S(2)}, u32[]{:S(2)}) collective-permute-start(bf16[1024,128]{1,0:T(8,128)(2,1)} %get-tuple-element.179), channel_id=1, source_target_pairs={{0,13},{1,12},{2,15},{3,14},{4,9},{5,8},{6,11},{7,10},{8,5},{9,4},... | collective-permute-start | bytes 786440 | tf_op jit(solution)/shard_map/ppermute | solution.py:863
  87.9 18.9 %collective-permute-start.13 = (bf16[1024,128]{1,0:T(8,128)(2,1)}, bf16[1024,128]{1,0:T(8,128)(2,1)S(1)}, u32[]{:S(2)}, u32[]{:S(2)}) collective-permute-start(bf16[1024,128]{1,0:T(8,128)(2,1)} %copy-done.111), channel_id=1, source_target_pairs={{0,6},{1,7},{2,4},{3,5},{4,2},{5,3},{6,0},{7,1},{8,14},{9,15},{10,... | collective-permute-start | bytes 786440 | tf_op jit(solution)/shard_map/ppermute | solution.py:863
  88.4 20.1 %collective-permute-start.14 = (bf16[1024,128]{1,0:T(8,128)(2,1)}, bf16[1024,128]{1,0:T(8,128)(2,1)S(1)}, u32[]{:S(2)}, u32[]{:S(2)}) collective-permute-start(bf16[1024,128]{1,0:T(8,128)(2,1)} %get-tuple-element.181), channel_id=1, source_target_pairs={{0,14},{1,15},{2,12},{3,13},{4,10},{5,11},{6,8},{7,9},{8,6},{9,7},... | collective-permute-start | bytes 786440 | tf_op jit(solution)/shard_map/ppermute | solution.py:863
  90.6 24.1 %collective-permute-start.15 = (bf16[1024,128]{1,0:T(8,128)(2,1)}, bf16[1024,128]{1,0:T(8,128)(2,1)S(1)}, u32[]{:S(2)}, u32[]{:S(2)}) collective-permute-start(bf16[1024,128]{1,0:T(8,128)(2,1)} %get-tuple-element.182), channel_id=1, source_target_pairs={{0,7},{1,6},{2,5},{3,4},{4,3},{5,2},{6,1},{7,0},{8,15},{9,14},{10,... | collective-permute-start | bytes 786440 | tf_op jit(solution)/shard_map/ppermute | solution.py:863
  92.7 30.3 %collective-permute-start.16 = (bf16[1024,128]{1,0:T(8,128)(2,1)}, bf16[1024,128]{1,0:T(8,128)(2,1)S(1)}, u32[]{:S(2)}, u32[]{:S(2)}) collective-permute-start(bf16[1024,128]{1,0:T(8,128)(2,1)} %get-tuple-element.183), channel_id=1, source_target_pairs={{0,15},{1,14},{2,13},{3,12},{4,11},{5,10},{6,9},{7,8},{8,7},{9,6},... | collective-permute-start | bytes 786440 | tf_op jit(solution)/shard_map/ppermute | solution.py:863
  104.2 27.3 %all-to-all-start.2 = ((f32[32,8,128]{2,1,0:T(8,128)}), f32[32,8,128]{2,1,0:T(8,128)S(1)}, u32[]{:S(2)}, u32[]{:S(2)}) async-start(f32[32,8,128]{2,1,0:T(8,128)} %get-tuple-element.178), calls=%async_computation.2 | async-start | bytes 262144 | tf_op jit(solution)/shard_map/all_to_all | solution.py:818
  136.6 47.8 %all-to-all-start.3 = ((bf16[16,512,128]{2,1,0:T(8,128)(2,1)}), bf16[16,512,128]{2,1,0:T(8,128)(2,1)}, u32[]{:S(2)}, u32[]{:S(2)}) async-start(bf16[16,512,128]{2,1,0:T(8,128)(2,1)} %bitcast.123), calls=%async_computation.3 | async-start | bytes 4194304 | tf_op jit(solution)/shard_map/all_to_all | solution.py:815
  188.9 16.7 %all-to-all-start.4 = ((f32[32,2,256]{2,1,0:T(2,128)}), f32[32,2,256]{2,1,0:T(2,128)S(1)}, u32[]{:S(2)}, u32[]{:S(2)}) async-start(f32[32,2,256]{2,1,0:T(2,128)} %get-tuple-element.187), calls=%async_computation.4 | async-start | bytes 131072 | tf_op jit(solution)/shard_map/all_to_all | solution.py:818
  205.6 40.1 %collective-permute-start.17 = (bf16[1024,128]{1,0:T(8,128)(2,1)}, bf16[1024,128]{1,0:T(8,128)(2,1)S(1)}, u32[]{:S(2)}, u32[]{:S(2)}) collective-permute-start(bf16[1024,128]{1,0:T(8,128)(2,1)} %get-tuple-element.206), channel_id=1, source_target_pairs={{0,8},{1,9},{2,10},{3,11},{4,12},{5,13},{6,14},{7,15},{8,0},{9,1},... | collective-permute-start | bytes 786440 | tf_op jit(solution)/shard_map/ppermute | solution.py:879
  207.2 39.3 %collective-permute-start.18 = (bf16[1024,128]{1,0:T(8,128)(2,1)}, bf16[1024,128]{1,0:T(8,128)(2,1)S(1)}, u32[]{:S(2)}, u32[]{:S(2)}) collective-permute-start(bf16[1024,128]{1,0:T(8,128)(2,1)} %get-tuple-element.207), channel_id=1, source_target_pairs={{0,1},{1,0},{2,3},{3,2},{4,5},{5,4},{6,7},{7,6},{8,9},{9,8},{10,11... | collective-permute-start | bytes 786440 | tf_op jit(solution)/shard_map/ppermute | solution.py:879
  208.6 41.4 %collective-permute-start.19 = (bf16[1024,128]{1,0:T(8,128)(2,1)}, bf16[1024,128]{1,0:T(8,128)(2,1)S(1)}, u32[]{:S(2)}, u32[]{:S(2)}) collective-permute-start(bf16[1024,128]{1,0:T(8,128)(2,1)} %get-tuple-element.208), channel_id=1, source_target_pairs={{0,9},{1,8},{2,11},{3,10},{4,13},{5,12},{6,15},{7,14},{8,1},{9,0},... | collective-permute-start | bytes 786440 | tf_op jit(solution)/shard_map/ppermute | solution.py:879
  210.0 41.9 %collective-permute-start.20 = (bf16[1024,128]{1,0:T(8,128)(2,1)}, bf16[1024,128]{1,0:T(8,128)(2,1)S(1)}, u32[]{:S(2)}, u32[]{:S(2)}) collective-permute-start(bf16[1024,128]{1,0:T(8,128)(2,1)} %get-tuple-element.209), channel_id=1, source_target_pairs={{0,2},{1,3},{2,0},{3,1},{4,6},{5,7},{6,4},{7,5},{8,10},{9,11},{10,... | collective-permute-start | bytes 786440 | tf_op jit(solution)/shard_map/ppermute | solution.py:879
  210.8 41.7 %collective-permute-start.21 = (bf16[1024,128]{1,0:T(8,128)(2,1)}, bf16[1024,128]{1,0:T(8,128)(2,1)}, u32[]{:S(2)}, u32[]{:S(2)}) collective-permute-start(bf16[1024,128]{1,0:T(8,128)(2,1)} %get-tuple-element.214), channel_id=1, source_target_pairs={{0,10},{1,11},{2,8},{3,9},{4,14},{5,15},{6,12},{7,13},{8,2},{9,3},... | collective-permute-start | bytes 786440 | tf_op jit(solution)/shard_map/ppermute | solution.py:879
  245.7 18.9 %collective-permute-start.22 = (bf16[1024,128]{1,0:T(8,128)(2,1)}, bf16[1024,128]{1,0:T(8,128)(2,1)S(1)}, u32[]{:S(2)}, u32[]{:S(2)}) collective-permute-start(bf16[1024,128]{1,0:T(8,128)(2,1)} %get-tuple-element.215), channel_id=1, source_target_pairs={{0,3},{1,2},{2,1},{3,0},{4,7},{5,6},{6,5},{7,4},{8,11},{9,10},{10,... | collective-permute-start | bytes 786440 | tf_op jit(solution)/shard_map/ppermute | solution.py:879
  246.4 21.9 %collective-permute-start.23 = (bf16[1024,128]{1,0:T(8,128)(2,1)}, bf16[1024,128]{1,0:T(8,128)(2,1)S(1)}, u32[]{:S(2)}, u32[]{:S(2)}) collective-permute-start(bf16[1024,128]{1,0:T(8,128)(2,1)} %get-tuple-element.216), channel_id=1, source_target_pairs={{0,11},{1,10},{2,9},{3,8},{4,15},{5,14},{6,13},{7,12},{8,3},{9,2},... | collective-permute-start | bytes 786440 | tf_op jit(solution)/shard_map/ppermute | solution.py:879
  250.0 20.7 %collective-permute-start.24 = (bf16[1024,128]{1,0:T(8,128)(2,1)}, bf16[1024,128]{1,0:T(8,128)(2,1)}, u32[]{:S(2)}, u32[]{:S(2)}) collective-permute-start(bf16[1024,128]{1,0:T(8,128)(2,1)} %get-tuple-element.217), channel_id=1, source_target_pairs={{0,4},{1,5},{2,6},{3,7},{4,0},{5,1},{6,2},{7,3},{8,12},{9,13},{10,... | collective-permute-start | bytes 786440 | tf_op jit(solution)/shard_map/ppermute | solution.py:879
  251.8 18.9 %collective-permute-start.25 = (bf16[1024,128]{1,0:T(8,128)(2,1)S(1)}, bf16[1024,128]{1,0:T(8,128)(2,1)}, u32[]{:S(2)}, u32[]{:S(2)}) collective-permute-start(bf16[1024,128]{1,0:T(8,128)(2,1)S(1)} %get-tuple-element.225), channel_id=1, source_target_pairs={{0,12},{1,13},{2,14},{3,15},{4,8},{5,9},{6,10},{7,11},{8,4},{9,5},... | collective-permute-start | bytes 786440 | tf_op jit(solution)/shard_map/ppermute | solution.py:879
  252.5 23.5 %collective-permute-start.26 = (bf16[1024,128]{1,0:T(8,128)(2,1)S(1)}, bf16[1024,128]{1,0:T(8,128)(2,1)}, u32[]{:S(2)}, u32[]{:S(2)}) collective-permute-start(bf16[1024,128]{1,0:T(8,128)(2,1)S(1)} %get-tuple-element.226), channel_id=1, source_target_pairs={{0,5},{1,4},{2,7},{3,6},{4,1},{5,0},{6,3},{7,2},{8,13},{9,12},{10,... | collective-permute-start | bytes 786440 | tf_op jit(solution)/shard_map/ppermute | solution.py:879
  259.6 16.5 %all-to-all-start.6 = ((f32[32,2,256]{2,1,0:T(2,128)}), f32[32,2,256]{2,1,0:T(2,128)S(1)}, u32[]{:S(2)}, u32[]{:S(2)}) async-start(f32[32,2,256]{2,1,0:T(2,128)} %get-tuple-element.211), calls=%async_computation.6 | async-start | bytes 131072 | tf_op jit(solution)/shard_map/all_to_all | solution.py:818
  288.2 45.6 %all-to-all-start.7 = ((f32[16,4,1024]{2,1,0:T(4,128)}), f32[16,4,1024]{2,1,0:T(4,128)S(1)}, u32[]{:S(2)}, u32[]{:S(2)}) async-start(f32[16,4,1024]{2,1,0:T(4,128)} %broadcast_in_dim.9), calls=%async_computation.7 | async-start | bytes 524288 | tf_op jit(solution)/shard_map/all_to_all | solution.py:825
  295.9 17.1 %collective-permute-start.29 = (bf16[1024,128]{1,0:T(8,128)(2,1)S(1)}, bf16[1024,128]{1,0:T(8,128)(2,1)S(1)}, u32[]{:S(2)}, u32[]{:S(2)}) collective-permute-start(bf16[1024,128]{1,0:T(8,128)(2,1)S(1)} %get-tuple-element.232), channel_id=1, source_target_pairs={{0,7},{1,6},{2,5},{3,4},{4,3},{5,2},{6,1},{7,0},{8,15},{9,14},{10,... | collective-permute-start | bytes 786440 | tf_op jit(solution)/shard_map/ppermute | solution.py:879
  297.4 25.3 %collective-permute-start.30 = (bf16[1024,128]{1,0:T(8,128)(2,1)S(1)}, bf16[1024,128]{1,0:T(8,128)(2,1)S(1)}, u32[]{:S(2)}, u32[]{:S(2)}) collective-permute-start(bf16[1024,128]{1,0:T(8,128)(2,1)S(1)} %copy-done.42), channel_id=1, source_target_pairs={{0,13},{1,12},{2,15},{3,14},{4,9},{5,8},{6,11},{7,10},{8,5},{9,4},... | collective-permute-start | bytes 786440 | tf_op jit(solution)/shard_map/ppermute | solution.py:879
  300.7 27.7 %collective-permute-start.31 = (bf16[1024,128]{1,0:T(8,128)(2,1)S(1)}, bf16[1024,128]{1,0:T(8,128)(2,1)S(1)}, u32[]{:S(2)}, u32[]{:S(2)}) collective-permute-start(bf16[1024,128]{1,0:T(8,128)(2,1)S(1)} %copy-done.45), channel_id=1, source_target_pairs={{0,14},{1,15},{2,12},{3,13},{4,10},{5,11},{6,8},{7,9},{8,6},{9,7},... | collective-permute-start | bytes 786440 | tf_op jit(solution)/shard_map/ppermute | solution.py:879
  302.1 31.7 %collective-permute-start.32 = (bf16[1024,128]{1,0:T(8,128)(2,1)S(1)}, bf16[1024,128]{1,0:T(8,128)(2,1)}, u32[]{:S(2)}, u32[]{:S(2)}) collective-permute-start(bf16[1024,128]{1,0:T(8,128)(2,1)S(1)} %copy-done.48), channel_id=1, source_target_pairs={{0,15},{1,14},{2,13},{3,12},{4,11},{5,10},{6,9},{7,8},{8,7},{9,6},... | collective-permute-start | bytes 786440 | tf_op jit(solution)/shard_map/ppermute | solution.py:879
  353.0 30.9 %all-to-all-start.8 = ((f32[16,4,1024]{2,1,0:T(4,128)}), f32[16,4,1024]{2,1,0:T(4,128)S(1)}, u32[]{:S(2)}, u32[]{:S(2)}) async-start(f32[16,4,1024]{2,1,0:T(4,128)} %broadcast_in_dim.10), calls=%async_computation.8 | async-start | bytes 524288 | tf_op jit(solution)/shard_map/all_to_all | solution.py:825
  361.8 45.6 %collective-permute-start.33 = (bf16[1024,128]{1,0:T(8,128)(2,1)S(1)}, bf16[1024,128]{1,0:T(8,128)(2,1)S(1)}, u32[]{:S(2)}, u32[]{:S(2)}) collective-permute-start(bf16[1024,128]{1,0:T(8,128)(2,1)S(1)} %get-tuple-element.237), channel_id=1, source_target_pairs={{0,1},{1,0},{2,3},{3,2},{4,5},{5,4},{6,7},{7,6},{8,9},{9,8},{10,11... | collective-permute-start | bytes 786440 | tf_op jit(solution)/shard_map/ppermute | solution.py:879
  363.7 43.7 %collective-permute-start.41 = (bf16[1024,128]{1,0:T(8,128)(2,1)}, bf16[1024,128]{1,0:T(8,128)(2,1)S(1)}, u32[]{:S(2)}, u32[]{:S(2)}) collective-permute-start(bf16[1024,128]{1,0:T(8,128)(2,1)} %get-tuple-element.257), channel_id=1, source_target_pairs={{0,8},{1,9},{2,10},{3,11},{4,12},{5,13},{6,14},{7,15},{8,0},{9,1},... | collective-permute-start | bytes 786440 | tf_op jit(solution)/shard_map/ppermute | solution.py:879
  366.1 41.4 %collective-permute-start.42 = (bf16[1024,128]{1,0:T(8,128)(2,1)}, bf16[1024,128]{1,0:T(8,128)(2,1)S(1)}, u32[]{:S(2)}, u32[]{:S(2)}) collective-permute-start(bf16[1024,128]{1,0:T(8,128)(2,1)} %get-tuple-element.258), channel_id=1, source_target_pairs={{0,9},{1,8},{2,11},{3,10},{4,13},{5,12},{6,15},{7,14},{8,1},{9,0},... | collective-permute-start | bytes 786440 | tf_op jit(solution)/shard_map/ppermute | solution.py:879
  366.3 62.4 %collective-permute-start.34 = (bf16[1024,128]{1,0:T(8,128)(2,1)}, bf16[1024,128]{1,0:T(8,128)(2,1)S(1)}, u32[]{:S(2)}, u32[]{:S(2)}) collective-permute-start(bf16[1024,128]{1,0:T(8,128)(2,1)} %get-tuple-element.238), channel_id=1, source_target_pairs={{0,2},{1,3},{2,0},{3,1},{4,6},{5,7},{6,4},{7,5},{8,10},{9,11},{10,... | collective-permute-start | bytes 786440 | tf_op jit(solution)/shard_map/ppermute | solution.py:879
  403.8 47.0 %collective-permute-start.43 = (bf16[1024,128]{1,0:T(8,128)(2,1)}, bf16[1024,128]{1,0:T(8,128)(2,1)S(1)}, u32[]{:S(2)}, u32[]{:S(2)}) collective-permute-start(bf16[1024,128]{1,0:T(8,128)(2,1)} %get-tuple-element.259), channel_id=1, source_target_pairs={{0,10},{1,11},{2,8},{3,9},{4,14},{5,15},{6,12},{7,13},{8,2},{9,3},... | collective-permute-start | bytes 786440 | tf_op jit(solution)/shard_map/ppermute | solution.py:879
  417.1 33.8 %all-to-all-start.10 = ((f32[32,2,256]{2,1,0:T(2,128)}), f32[32,2,256]{2,1,0:T(2,128)S(1)}, u32[]{:S(2)}, u32[]{:S(2)}) async-start(f32[32,2,256]{2,1,0:T(2,128)} %copy-done.90), calls=%async_computation.10 | async-start | bytes 131072 | tf_op jit(solution)/shard_map/all_to_all | solution.py:818
  419.9 154.4 %reduce-scatter.2.cloned.1.call-start = ((), (), s32[]{:S(2)}) async-start(), calls=%async_computation.20 | async-start | bytes 3932160 | tf_op jit(solution)/shard_map/reduce_scatter | solution.py:1340
  422.1 28.9 %collective-permute-start.36 = (bf16[1024,128]{1,0:T(8,128)(2,1)}, bf16[1024,128]{1,0:T(8,128)(2,1)S(1)}, u32[]{:S(2)}, u32[]{:S(2)}) collective-permute-start(bf16[1024,128]{1,0:T(8,128)(2,1)} %get-tuple-element.252), channel_id=1, source_target_pairs={{0,3},{1,2},{2,1},{3,0},{4,7},{5,6},{6,5},{7,4},{8,11},{9,10},{10,... | collective-permute-start | bytes 786440 | tf_op jit(solution)/shard_map/ppermute | solution.py:879
  424.7 26.2 %collective-permute-start.37 = (bf16[1024,128]{1,0:T(8,128)(2,1)}, bf16[1024,128]{1,0:T(8,128)(2,1)S(1)}, u32[]{:S(2)}, u32[]{:S(2)}) collective-permute-start(bf16[1024,128]{1,0:T(8,128)(2,1)} %get-tuple-element.253), channel_id=1, source_target_pairs={{0,4},{1,5},{2,6},{3,7},{4,0},{5,1},{6,2},{7,3},{8,12},{9,13},{10,... | collective-permute-start | bytes 786440 | tf_op jit(solution)/shard_map/ppermute | solution.py:879
  426.2 24.8 %collective-permute-start.44 = (bf16[1024,128]{1,0:T(8,128)(2,1)}, bf16[1024,128]{1,0:T(8,128)(2,1)}, u32[]{:S(2)}, u32[]{:S(2)}) collective-permute-start(bf16[1024,128]{1,0:T(8,128)(2,1)} %get-tuple-element.260), channel_id=1, source_target_pairs={{0,11},{1,10},{2,9},{3,8},{4,15},{5,14},{6,13},{7,12},{8,3},{9,2},... | collective-permute-start | bytes 786440 | tf_op jit(solution)/shard_map/ppermute | solution.py:879
  428.6 22.4 %collective-permute-start.45 = (bf16[1024,128]{1,0:T(8,128)(2,1)}, bf16[1024,128]{1,0:T(8,128)(2,1)}, u32[]{:S(2)}, u32[]{:S(2)}) collective-permute-start(bf16[1024,128]{1,0:T(8,128)(2,1)} %get-tuple-element.261), channel_id=1, source_target_pairs={{0,12},{1,13},{2,14},{3,15},{4,8},{5,9},{6,10},{7,11},{8,4},{9,5},... | collective-permute-start | bytes 786440 | tf_op jit(solution)/shard_map/ppermute | solution.py:879
  450.8 32.8 %collective-permute-start.49 = (bf16[5120,256]{1,0:T(8,128)(2,1)}, bf16[5120,256]{1,0:T(8,128)(2,1)}, u32[]{:S(2)}, u32[]{:S(2)}) collective-permute-start(bf16[5120,256]{1,0:T(8,128)(2,1)} %get-tuple-element.276.refs_1_), channel_id=1, source_target_pairs={{0,16},{16,0},{1,17},{17,1},{2,18},{18,2},{3,19},{19,3},{4,20},{20... | collective-permute-start | bytes 7864328 | tf_op jit(solution)/shard_map/ppermute | solution.py:1328
  495.3 18.9 %collective-permute-start.40 = (bf16[1024,128]{1,0:T(8,128)(2,1)}, bf16[1024,128]{1,0:T(8,128)(2,1)S(1)}, u32[]{:S(2)}, u32[]{:S(2)}) collective-permute-start(bf16[1024,128]{1,0:T(8,128)(2,1)} %get-tuple-element.256), channel_id=1, source_target_pairs={{0,7},{1,6},{2,5},{3,4},{4,3},{5,2},{6,1},{7,0},{8,15},{9,14},{10,... | collective-permute-start | bytes 786440 | tf_op jit(solution)/shard_map/ppermute | solution.py:879
  496.3 26.9 %collective-permute-start.46 = (bf16[1024,128]{1,0:T(8,128)(2,1)}, bf16[1024,128]{1,0:T(8,128)(2,1)S(1)}, u32[]{:S(2)}, u32[]{:S(2)}) collective-permute-start(bf16[1024,128]{1,0:T(8,128)(2,1)} %get-tuple-element.262), channel_id=1, source_target_pairs={{0,13},{1,12},{2,15},{3,14},{4,9},{5,8},{6,11},{7,10},{8,5},{9,4},... | collective-permute-start | bytes 786440 | tf_op jit(solution)/shard_map/ppermute | solution.py:879
  499.6 29.6 %collective-permute-start.47 = (bf16[1024,128]{1,0:T(8,128)(2,1)}, bf16[1024,128]{1,0:T(8,128)(2,1)S(1)}, u32[]{:S(2)}, u32[]{:S(2)}) collective-permute-start(bf16[1024,128]{1,0:T(8,128)(2,1)} %get-tuple-element.263), channel_id=1, source_target_pairs={{0,14},{1,15},{2,12},{3,13},{4,10},{5,11},{6,8},{7,9},{8,6},{9,7},... | collective-permute-start | bytes 786440 | tf_op jit(solution)/shard_map/ppermute | solution.py:879
  502.0 33.4 %collective-permute-start.48 = (bf16[1024,128]{1,0:T(8,128)(2,1)}, bf16[1024,128]{1,0:T(8,128)(2,1)S(1)}, u32[]{:S(2)}, u32[]{:S(2)}) collective-permute-start(bf16[1024,128]{1,0:T(8,128)(2,1)} %get-tuple-element.264), channel_id=1, source_target_pairs={{0,15},{1,14},{2,13},{3,12},{4,11},{5,10},{6,9},{7,8},{8,7},{9,6},... | collective-permute-start | bytes 786440 | tf_op jit(solution)/shard_map/ppermute | solution.py:879
  506.7 34.3 %all-to-all-start.12 = ((f32[32,2,256]{2,1,0:T(2,128)}), f32[32,2,256]{2,1,0:T(2,128)S(1)}, u32[]{:S(2)}, u32[]{:S(2)}) async-start(f32[32,2,256]{2,1,0:T(2,128)} %copy-done.89), calls=%async_computation.12 | async-start | bytes 131072 | tf_op jit(solution)/shard_map/all_to_all | solution.py:818
  546.9 57.6 %all-to-all-start.13 = ((bf16[16,512,128]{2,1,0:T(8,128)(2,1)}), bf16[16,512,128]{2,1,0:T(8,128)(2,1)}, u32[]{:S(2)}, u32[]{:S(2)}) async-start(bf16[16,512,128]{2,1,0:T(8,128)(2,1)} %bitcast.134), calls=%async_computation.13 | async-start | bytes 4194304 | tf_op jit(solution)/shard_map/all_to_all | solution.py:815
  551.4 84.5 %all-reduce.3.cloned.1.call-start = ((), (), s32[]{:S(2)}) async-start(), calls=%async_computation.21 | async-start | bytes 1654784 | tf_op jit(solution)/shard_map/psum | solution.py:1364
  653.3 105.8 %all-to-all-start.11 = ((bf16[16,1024,128]{2,1,0:T(8,128)(2,1)}), bf16[16,1024,128]{2,1,0:T(8,128)(2,1)}, u32[]{:S(2)}, u32[]{:S(2)}) async-start(bf16[16,1024,128]{2,1,0:T(8,128)(2,1)} %get-tuple-element.270), calls=%async_computation.11 | async-start | bytes 8388608 | tf_op jit(solution)/shard_map/all_to_all | solution.py:815
  665.3 28.5 %collective-permute-start.58 = (bf16[1616,256]{1,0:T(8,128)(2,1)S(1)}, bf16[1616,256]{1,0:T(8,128)(2,1)S(1)}, u32[]{:S(2)}, u32[]{:S(2)}) collective-permute-start(bf16[1616,256]{1,0:T(8,128)(2,1)S(1)} %copy-done.2), channel_id=1, source_target_pairs={{0,1},{1,0},{2,3},{3,2},{4,5},{5,4},{6,7},{7,6},{8,9},{9,8},{10,11... | collective-permute-start | bytes 2482184 | tf_op jit(solution)/shard_map/ppermute | solution.py:1418
  667.3 66.5 %collective-permute-start.59 = (bf16[1616,256]{1,0:T(8,128)(2,1)S(1)}, bf16[1616,256]{1,0:T(8,128)(2,1)}, u32[]{:S(2)}, u32[]{:S(2)}) collective-permute-start(bf16[1616,256]{1,0:T(8,128)(2,1)S(1)} %copy-done.2), channel_id=1, source_target_pairs={{0,2},{1,3},{2,0},{3,1},{4,6},{5,7},{6,4},{7,5},{8,10},{9,11},{10,... | collective-permute-start | bytes 2482184 | tf_op jit(solution)/shard_map/ppermute | solution.py:1418
  668.7 81.3 %collective-permute-start.60 = (bf16[1616,256]{1,0:T(8,128)(2,1)S(1)}, bf16[1616,256]{1,0:T(8,128)(2,1)}, u32[]{:S(2)}, u32[]{:S(2)}) collective-permute-start(bf16[1616,256]{1,0:T(8,128)(2,1)S(1)} %copy-done.2), channel_id=1, source_target_pairs={{0,3},{1,2},{2,1},{3,0},{4,7},{5,6},{6,5},{7,4},{8,11},{9,10},{10,... | collective-permute-start | bytes 2482184 | tf_op jit(solution)/shard_map/ppermute | solution.py:1418
  782.6 36.7 %collective-permute-start.63 = (bf16[1616,256]{1,0:T(8,128)(2,1)S(1)}, bf16[1616,256]{1,0:T(8,128)(2,1)}, u32[]{:S(2)}, u32[]{:S(2)}) collective-permute-start(bf16[1616,256]{1,0:T(8,128)(2,1)S(1)} %copy-done.3), channel_id=1, source_target_pairs={{0,16},{16,0},{1,17},{17,1},{2,18},{18,2},{3,19},{19,3},{4,20},{20... | collective-permute-start | bytes 2482184 | tf_op jit(solution)/shard_map/ppermute | solution.py:1453
  788.2 31.0 %collective-permute-start.64 = (bf16[1616,256]{1,0:T(8,128)(2,1)S(1)}, bf16[1616,256]{1,0:T(8,128)(2,1)}, u32[]{:S(2)}, u32[]{:S(2)}) collective-permute-start(bf16[1616,256]{1,0:T(8,128)(2,1)S(1)} %copy-done.11), channel_id=1, source_target_pairs={{0,16},{16,0},{1,17},{17,1},{2,18},{18,2},{3,19},{19,3},{4,20},{20... | collective-permute-start | bytes 2482184 | tf_op jit(solution)/shard_map/ppermute | solution.py:1453
  788.8 30.5 %collective-permute-start.65 = (bf16[1616,256]{1,0:T(8,128)(2,1)}, bf16[1616,256]{1,0:T(8,128)(2,1)}, u32[]{:S(2)}, u32[]{:S(2)}) collective-permute-start(bf16[1616,256]{1,0:T(8,128)(2,1)} %collective-permute-done.59.refs_14_.refs_3_), channel_id=1, source_target_pairs={{0,16},{16,0},{1,17},{17,1},{2,18},{18,2},{3,19},{19,3},{4,20},{20... | collective-permute-start | bytes 2482184 | tf_op jit(solution)/shard_map/ppermute | solution.py:1453
  791.0 28.2 %collective-permute-start.66 = (bf16[1616,256]{1,0:T(8,128)(2,1)}, bf16[1616,256]{1,0:T(8,128)(2,1)}, u32[]{:S(2)}, u32[]{:S(2)}) collective-permute-start(bf16[1616,256]{1,0:T(8,128)(2,1)} %collective-permute-done.60.refs_15_.refs_4_), channel_id=1, source_target_pairs={{0,16},{16,0},{1,17},{17,1},{2,18},{18,2},{3,19},{19,3},{4,20},{20... | collective-permute-start | bytes 2482184 | tf_op jit(solution)/shard_map/ppermute | solution.py:1453
  (148 other events, 2381.2 us)
Sparse Core Ops, SparseCore 0:
  490.4 83.9 reduce-scatter.1
  577.3 57.8 all-reduce.2
